TPU v7x, 512 devices: a whole 4x8x8 slice. The times are simulated.
512 devices in a mesh: seq: 32 (over x, y), head: 16 (over z, core).
Axes of the slice: x: 4, y: 8, z: 8, core: 2. Of those that a mesh axis runs over, the one named last changes fastest.
Arguments:
- queries: bfloat16 [114688, 2048], P(('seq', 'head')), may hold values from -110 to 110
- key_rows: bfloat16 [114688, 2048], P(('seq', 'head')), may hold values from -6 to 6
- value_rows: bfloat16 [114688, 2048], P(('seq', 'head')), may hold values from -6 to 6
- token_rank: int32 [32, 3584], P('seq'), may hold values from 0 to 3583, each once within a row
- masked_index: int32 [32, 224], P('seq'), may hold values from 0 to 3583, as said below
- masked_counts: int32 [32], replicated, may hold values from 1 to 224, 2368 in all
- clean_latents: bfloat16 [114688, 16], P('seq'), may hold values from -6 to 6
- noise_draws: bfloat16 [114688, 64], P('seq'), may hold values from -6 to 6
- noise_times: bfloat16 [114688, 4], P('seq'), may hold values from 0.049804688 to 0.94921875
- w_cond: bfloat16 [2048, 1536], P('head'), may hold values from -0.5 to 0.5
- w_in: float32 [16, 1536], replicated, may hold values from -1.5 to 1.5
- time_vec: float32 [1536], replicated, may hold values from -5 to 5
- norm_gain: float32 [1536], replicated, may hold values from 0.25 to 1.75
- w_out: float32 [1536, 16], replicated, may hold values from -0.15625 to 0.15625
Outputs:
- attended: bfloat16 [114688, 2048], P(('seq', 'head'))
- grad_cond: float32 [2048, 1536], P('head')
- grad_in: float32 [16, 1536], replicated
- grad_time: float32 [1536], replicated
- grad_gain: float32 [1536], replicated
- grad_out: float32 [1536, 16], replicated
Inputs may be any that keep to these rules, and one draw needn't show every extreme that they name: `token_rank`: each clip's row holds each rank once. `masked_index`: row s holds 224 distinct positions within clip s; only its first masked_counts[s] entries are used. `masked_counts`: they sum to 2368; the largest is 224.
All inputs are finite; a program needn't handle non-finite values.
Results may differ from a plain program's by a relative error of at most 0.009.
Values may be sent and summed in bfloat16 or wider, within the bound.
No kernel may reach another device: no remote copies, remote signals or barrier semaphores. Data moves between devices by JAX's collectives and lax.ppermute only.
A program may use at most 64 MiB of HBM per device.

v0:
```python
import math

import jax
import jax.numpy as jnp
from jax import lax
from jax.sharding import PartitionSpec as P

HD = 128
LAT = 16
DRAWS = 4


NORM_EPS = 1e-06
FLOOR_SCORE = -1e30


def head_loss(condition, w_in, time_vec, norm_gain, w_out, payload, row_weight, loss_scale):
    row_count = condition.shape[0]
    load_float = payload.astype(jnp.float32)
    clean_part = load_float[:, :LAT]
    noise_part = load_float[:, LAT : LAT + DRAWS * LAT].reshape(row_count, DRAWS, LAT)
    time_part = load_float[:, LAT + DRAWS * LAT :]
    angles = 0.5 * math.pi * time_part
    noisy_input = (
        jnp.cos(angles)[:, :, None] * clean_part[:, None, :]
        + jnp.sin(angles)[:, :, None] * noise_part
    )
    hidden = jnp.einsum("rdc,cw->rdw", noisy_input, w_in, precision=lax.Precision.HIGHEST)
    hidden = hidden + condition[:, None, :] + time_part[:, :, None] * time_vec
    normed = (
        hidden * lax.rsqrt(jnp.mean(hidden * hidden, axis=-1, keepdims=True) + NORM_EPS) * norm_gain
    )
    activated = jax.nn.silu(normed)
    predicted = jnp.einsum("rdw,wc->rdc", activated, w_out, precision=lax.Precision.HIGHEST)
    residual = predicted - noise_part
    return jnp.sum(row_weight[:, None, None] * residual * residual) * loss_scale


def attention_fold(local_query, query_rank, key_rank):
    factor = 1.0 / math.sqrt(local_query.shape[2])

    def update(state_in, key_block, value_block, rank_block):
        running_max, running_sum, running_out = state_in
        scores = (
            jnp.einsum("qhd,khd->hqk", local_query, key_block, preferred_element_type=jnp.float32)
            * factor
        )
        visible = rank_block[None, None, :] <= query_rank[None, :, None]
        block_max = jnp.max(jnp.where(visible, scores, FLOOR_SCORE), axis=-1)
        new_max = jnp.maximum(running_max, block_max)
        weights = jnp.where(visible, jnp.exp(scores - new_max[:, :, None]), 0.0)
        shrink = jnp.exp(running_max - new_max)
        running_sum = running_sum * shrink + jnp.sum(weights, axis=-1)
        mixed_block = jnp.einsum(
            "hqk,khd->qhd",
            weights.astype(jnp.bfloat16),
            value_block,
            preferred_element_type=jnp.float32,
        )
        running_out = running_out * jnp.transpose(shrink)[:, :, None] + mixed_block
        return (new_max, running_sum, running_out)

    def fold_keys(state_in, arrived, first_row):
        key_piece, value_piece = arrived
        piece_rows = key_piece.shape[0]
        block_rows = math.gcd(piece_rows, 512)
        block_count = piece_rows // block_rows

        def one_block(block_index, state_now):
            begin_row = block_index * block_rows
            key_block = lax.dynamic_slice_in_dim(key_piece, begin_row, block_rows, 0)
            value_block = lax.dynamic_slice_in_dim(value_piece, begin_row, block_rows, 0)
            rank_block = lax.dynamic_slice_in_dim(key_rank, first_row + begin_row, block_rows, 0)
            return update(state_now, key_block, value_block, rank_block)

        return lax.fori_loop(0, block_count, one_block, state_in)

    return fold_keys


def head_section(
    picked_rows, payload, row_weight, w_cond, w_in, time_vec, norm_gain, w_out, loss_scale
):
    total_rows = picked_rows.shape[0]
    share_rows = total_rows // lax.axis_size("head")
    offset = lax.axis_index("head") * share_rows
    segment = picked_rows
    condition = lax.psum_scatter(
        jnp.dot(segment, w_cond, preferred_element_type=jnp.float32),
        "head",
        scatter_dimension=0,
        tiled=True,
    )
    local_load = lax.dynamic_slice_in_dim(payload, offset, share_rows, 0)
    local_weight = lax.dynamic_slice_in_dim(row_weight.astype(jnp.float32), offset, share_rows, 0)

    def local_loss(cond_in, in_weight, time_weight, gain_weight, out_weight):
        return head_loss(
            cond_in,
            in_weight,
            time_weight,
            gain_weight,
            out_weight,
            local_load,
            local_weight,
            loss_scale,
        )

    loss_value, pull_back = jax.vjp(local_loss, condition, w_in, time_vec, norm_gain, w_out)
    cond_grad, in_grad, time_grad, gain_grad, out_grad = pull_back(jnp.ones_like(loss_value))
    segment = picked_rows
    cond_part = lax.dot_general(
        segment,
        lax.all_gather(cond_grad.astype(jnp.bfloat16), "head", axis=0, tiled=True),
        (((0,), (0,)), ((), ())),
        preferred_element_type=jnp.float32,
    )
    return (cond_part, in_grad, time_grad, gain_grad, out_grad)


def local(
    queries,
    key_rows,
    value_rows,
    token_rank,
    masked_index,
    masked_counts,
    clean_latents,
    noise_draws,
    noise_times,
    w_cond,
    w_in,
    time_vec,
    norm_gain,
    w_out,
):
    tok_rows = queries.shape[0]
    heads_all = lax.axis_size("head")
    seq_count = lax.axis_size("seq")
    seq_rows = tok_rows * heads_all
    seq_index = lax.axis_index("seq")
    clip_rank = token_rank[0]
    split_query = queries.reshape(tok_rows, heads_all, -1, HD)
    split_key = key_rows.reshape(tok_rows, heads_all, -1, HD)
    split_value = value_rows.reshape(tok_rows, heads_all, -1, HD)
    local_query = lax.all_to_all(split_query, "head", split_axis=1, concat_axis=0, tiled=True)
    local_key = lax.all_to_all(split_key, "head", split_axis=1, concat_axis=0, tiled=True)
    local_value = lax.all_to_all(split_value, "head", split_axis=1, concat_axis=0, tiled=True)
    query_count = local_query.shape[0]
    head_count = local_query.shape[2]
    local_query = local_query.reshape(query_count, head_count, HD)
    local_key = local_key.reshape(local_key.shape[0], head_count, HD)
    local_value = local_value.reshape(local_value.shape[0], head_count, HD)
    start_state = (
        jnp.full((head_count, query_count), FLOOR_SCORE, jnp.float32),
        jnp.zeros((head_count, query_count), jnp.float32),
        jnp.zeros((query_count, head_count, HD), jnp.float32),
    )
    fold_keys = attention_fold(local_query, clip_rank, clip_rank)
    running_max, running_sum, running_out = fold_keys(start_state, (local_key, local_value), 0)
    mixed_heads = (running_out / jnp.transpose(running_sum)[:, :, None]).astype(jnp.bfloat16)
    returned = lax.all_to_all(mixed_heads, "head", split_axis=0, concat_axis=1, tiled=True)
    attended = returned.reshape(tok_rows, -1)
    head_rows = mixed_heads.reshape(seq_rows, -1)
    chosen = masked_index[0]
    most_rows = chosen.shape[0]
    live_count = lax.dynamic_index_in_dim(masked_counts, seq_index, 0, keepdims=False)
    alive_mask = jnp.arange(most_rows, dtype=jnp.int32) < live_count
    picked_rows = jnp.where(
        alive_mask[:, None], jnp.take(head_rows, chosen, axis=0), jnp.zeros((), jnp.bfloat16)
    )
    payload = jnp.concatenate(
        [
            jnp.take(clean_latents, chosen, axis=0),
            jnp.take(noise_draws, chosen, axis=0),
            jnp.take(noise_times, chosen, axis=0),
        ],
        axis=1,
    )
    loss_scale = 1.0 / math.sqrt(most_rows // 3 * seq_count * DRAWS)
    cond_part, in_grad, time_grad, gain_grad, out_grad = head_section(
        picked_rows, payload, alive_mask, w_cond, w_in, time_vec, norm_gain, w_out, loss_scale
    )
    cond_whole = lax.psum(cond_part, "seq")
    in_grad, time_grad, gain_grad, out_grad = lax.psum(
        (in_grad, time_grad, gain_grad, out_grad), ("seq", "head")
    )
    return (attended, cond_whole, in_grad, time_grad, gain_grad, out_grad)


def solution(mesh):
    return jax.shard_map(
        local,
        mesh=mesh,
        in_specs=(
            P(("seq", "head"), None),
            P(("seq", "head"), None),
            P(("seq", "head"), None),
            P("seq", None),
            P("seq", None),
            P(),
            P("seq", None),
            P("seq", None),
            P("seq", None),
            P("head", None),
            P(),
            P(),
            P(),
            P(),
        ),
        out_specs=(P(("seq", "head"), None), P("head", None), P(), P(), P(), P()),
        check_vma=False,
    )
```

profile of v0, /device:TPU:6, one launch (start us, length us, event | category | flops | bytes accessed | tf_op | source)
XLA Modules:
  0.0 689.5 jit_solution(2858217623305970465)
XLA Ops:
  9.8 10.6 %all-to-all-start = ((bf16[224,16,1,128]{3,0,2,1:T(8,128)(2,1)}), bf16[224,16,1,128]{3,0,2,1:T(8,128)(2,1)S(1)}, u32[]{:S(2)}, u32[]{:S(2)}) async-start(bf16[224,16,1,128]{3,0,2,1:T(8,128)(2,1)} %copy.83), calls=%async_computation | async-start | bytes 1835008 | tf_op jit(solution)/shard_map/all_to_all | solution.py:147
  21.8 22.3 %all-to-all-done = bf16[224,16,1,128]{3,0,2,1:T(8,128)(2,1)S(1)} async-done(((bf16[224,16,1,128]{3,0,2,1:T(8,128)(2,1)}), bf16[224,16,1,128]{3,0,2,1:T(8,128)(2,1)S(1)}, u32[]{:S(2)}, u32[]{:S(2)}) %all-to-all-start) | async-done | bytes 917536 | tf_op jit(solution)/shard_map/all_to_all | solution.py:147
  44.0 5.0 all-to-all-start.1
  50.5 22.1 %all-to-all-done.1 = bf16[224,16,1,128]{3,0,2,1:T(8,128)(2,1)} async-done(((bf16[224,16,1,128]{3,0,2,1:T(8,128)(2,1)}), bf16[224,16,1,128]{3,0,2,1:T(8,128)(2,1)}, u32[]{:S(2)}, u32[]{:S(2)}) %all-to-all-start.1) | async-done | bytes 917536 | tf_op jit(solution)/shard_map/all_to_all | solution.py:146
  72.6 5.2 all-to-all-start.2
  87.7 13.7 %all-to-all-done.2 = bf16[224,16,1,128]{3,0,2,1:T(8,128)(2,1)} async-done(((bf16[224,16,1,128]{3,0,2,1:T(8,128)(2,1)}), bf16[224,16,1,128]{3,0,2,1:T(8,128)(2,1)}, u32[]{:S(2)}, u32[]{:S(2)}) %all-to-all-start.2) | async-done | bytes 917536 | tf_op jit(solution)/shard_map/all_to_all | solution.py:148
  101.3 61.6 %while.18 = (s32[]{:T(128)}, f32[1,3584]{1,0:T(1,128)S(1)}, f32[1,3584]{1,0:T(1,128)S(1)}, f32[3584,1,128]{0,2,1:T(8,128)}, s32[3584]{0:T(1024)S(1)}, /*index=5*...) while((s32[]{:T(128)}, f32[1,3584]{1,0:T(1,128)S(1)}, ...), condition=%wide.region_3.4_spmd.clone, body=%wide.region_0.3_spmd.clone.sunk | while | flops 966611968 | bytes 41877764 | solution.py:76
  101.4 2.4 fusion.63
  105.9 2.9 fusion.67
  110.2 2.4 fusion.63
  114.7 2.9 fusion.67
  119.0 2.4 fusion.63
  123.5 2.9 fusion.67
  127.8 2.4 fusion.63
  132.3 2.9 fusion.67
  141.1 2.9 fusion.67
  149.9 2.9 fusion.67
  158.7 2.9 fusion.67
  167.6 33.2 %fusion = f32[16,1536]{1,0:T(8,128)S(1)} fusion(f32[224,1536]{1,0:T(8,128)} %fusion.45), kind=kCustom, calls=%all-reduce-scatter | all-reduce-scatter fusion | flops 393217 | bytes 1476608
  208.2 6.2 all-to-all-start.3
  219.0 32.4 %all-gather = bf16[16,14,1536]{2,1,0:T(8,128)(2,1)S(1)} all-gather(bf16[1,14,1536]{2,1,0:T(8,128)(2,1)S(1)} %bitcast.132), channel_id=1, replica_groups=mesh['seq'=32,'head'=16] {'head'}, dimensions={0}, use_global_device_ids=true | all-gather | bytes 731136 | tf_op jit(solution)/shard_map/all_gather | solution.py:114
  256.3 97.4 %all-reduce.2 = (f32[1536]{0:T(1024)}, f32[1536]{0:T(1024)}) all-reduce(f32[1536]{0:T(1024)S(1)} %get-tuple-element.197, f32[1536]{0:T(1024)S(1)} %get-tuple-element.195), channel_id=1, replica_groups=mesh['seq'=32,'head'=16] {'seq','head'}, use_global_device_ids=true, to_apply=%region_11.12 | all-reduce | flops 3072 | bytes 24576 | tf_op jit(solution)/shard_map/psum | solution.py:185
  356.3 163.5 %all-reduce.9.cloned.1.call-done = (f32[16,1536]{1,0:T(8,128)}, f32[1536,16]{0,1:T(8,128)}) async-done(((f32[16,1536]{1,0:T(8,128)}, f32[1536,16]{0,1:T(8,128)}), (f32[16,1536]{1,0:T(8,128)}, f32[1536,16]{0,1:T(8,128)})) %all-reduce.9.cloned.1.call-update) | async-done | bytes 196624 | tf_op jit(solution)/shard_map/psum | solution.py:185
  519.8 157.7 %all-reduce.7.cloned.1.call-done = f32[128,1536]{1,0:T(8,128)} async-done(((f32[128,1536]{1,0:T(8,128)}), f32[128,1536]{1,0:T(8,128)}) %all-reduce.7.cloned.1.call-update) | async-done | bytes 786448 | tf_op jit(solution)/shard_map/psum | solution.py:184
  (168 shorter events, 74.7 us)
Async XLA Ops:
  7.2 159.0 %copy-start = (bf16[128,1536]{1,0:T(8,128)(2,1)S(1)}, bf16[128,1536]{1,0:T(8,128)(2,1)}, u32[]{:S(2)}) copy-start(bf16[128,1536]{1,0:T(8,128)(2,1)} %param.25) | copy-start | bytes 1179652
  7.2 13.2 %copy-start.3 = (bf16[224,2048]{1,0:T(8,128)(2,1)S(1)}, bf16[224,2048]{1,0:T(8,128)(2,1)}, u32[]{:S(2)}) copy-start(bf16[224,2048]{1,0:T(8,128)(2,1)} %param.16) | copy-start | bytes 2752516
  9.8 39.3 %copy-start.4 = (bf16[224,2048]{1,0:T(8,128)(2,1)S(1)}, bf16[224,2048]{1,0:T(8,128)(2,1)}, u32[]{:S(2)}) copy-start(bf16[224,2048]{1,0:T(8,128)(2,1)} %param.18) | copy-start | bytes 2752516
  9.8 34.2 %all-to-all-start = ((bf16[224,16,1,128]{3,0,2,1:T(8,128)(2,1)}), bf16[224,16,1,128]{3,0,2,1:T(8,128)(2,1)S(1)}, u32[]{:S(2)}, u32[]{:S(2)}) async-start(bf16[224,16,1,128]{3,0,2,1:T(8,128)(2,1)} %copy.83), calls=%async_computation | async-start | bytes 1835008 | tf_op jit(solution)/shard_map/all_to_all | solution.py:147
  20.6 29.9 %copy-start.11 = (s32[1,224]{1,0:T(1,128)S(1)}, s32[1,224]{1,0:T(1,128)}, u32[]{:S(2)}) copy-start(s32[1,224]{1,0:T(1,128)} %param.20) | copy-start | bytes 2692
  21.8 56.1 %copy-start.5 = (s32[1,3584]{1,0:T(1,128)S(1)}, s32[1,3584]{1,0:T(1,128)}, u32[]{:S(2)}) copy-start(s32[1,3584]{1,0:T(1,128)} %param.19) | copy-start | bytes 43012
  21.8 56.2 %copy-start.8 = (bf16[3584,4]{0,1:T(4,128)(2,1)S(1)}, bf16[3584,4]{0,1:T(4,128)(2,1)}, u32[]{:S(2)}) copy-start(bf16[3584,4]{0,1:T(4,128)(2,1)} %param.24) | copy-start | bytes 86020
  44.0 28.6 %all-to-all-start.1 = ((bf16[224,16,1,128]{3,0,2,1:T(8,128)(2,1)}), bf16[224,16,1,128]{3,0,2,1:T(8,128)(2,1)}, u32[]{:S(2)}, u32[]{:S(2)}) async-start(bf16[224,16,1,128]{3,0,2,1:T(8,128)(2,1)} %copy.84), calls=%async_computation.1 | async-start | bytes 1835008 | tf_op jit(solution)/shard_map/all_to_all | solution.py:146
  49.3 32.2 %copy-start.6 = (bf16[3584,16]{0,1:T(8,128)(2,1)S(1)}, bf16[3584,16]{0,1:T(8,128)(2,1)}, u32[]{:S(2)}) copy-start(bf16[3584,16]{0,1:T(8,128)(2,1)} %param.22) | copy-start | bytes 344068
  50.4 32.3 %copy-start.13 = (s32[32]{0:T(128)S(1)}, s32[32]{0:T(128)}, u32[]{:S(2)}) copy-start(s32[32]{0:T(128)} %param.21) | copy-start | bytes 388
  72.6 28.7 %all-to-all-start.2 = ((bf16[224,16,1,128]{3,0,2,1:T(8,128)(2,1)}), bf16[224,16,1,128]{3,0,2,1:T(8,128)(2,1)}, u32[]{:S(2)}, u32[]{:S(2)}) async-start(bf16[224,16,1,128]{3,0,2,1:T(8,128)(2,1)} %copy.85), calls=%async_computation.2 | async-start | bytes 1835008 | tf_op jit(solution)/shard_map/all_to_all | solution.py:148
  103.9 2.0 copy-start.1
  112.7 2.0 copy-start.1
  121.5 2.0 copy-start.1
  130.3 2.0 copy-start.1
  201.4 13.3 %collective-permute-start = (f32[16,1536]{1,0:T(8,128)S(1)}, f32[16,1536]{1,0:T(8,128)S(1)}, u32[]{:S(2)}, u32[]{:S(2)}) collective-permute-start(f32[16,1536]{1,0:T(8,128)S(1)} %fusion), channel_id=1, source_target_pairs={{0,1},{1,2},{2,3},{3,4},{4,5},{5,6},{6,7},{7,8},{8,9},{9,10},{10,1... | collective-permute-start | bytes 294920
  202.7 12.0 %collective-permute-start.1 = (f32[14,1536]{1,0:T(8,128)}, f32[14,1536]{1,0:T(8,128)}, u32[]{:S(2)}, u32[]{:S(2)}) collective-permute-start(f32[14,1536]{1,0:T(8,128)} %slice.23), channel_id=1, source_target_pairs={{0,2},{1,3},{2,4},{3,5},{4,6},{5,7},{6,8},{7,9},{8,10},{9,11},{10,... | collective-permute-start | bytes 258056
  205.2 10.8 %copy-start.7 = (f32[16,1536]{1,0:T(8,128)S(1)}, f32[16,1536]{1,0:T(8,128)}, u32[]{:S(2)}) copy-start(f32[16,1536]{1,0:T(8,128)} %param.26) | copy-start | bytes 294916
  205.2 10.8 %copy-start.9 = (f32[1536]{0:T(1024)S(1)}, f32[1536]{0:T(1024)}, u32[]{:S(2)}) copy-start(f32[1536]{0:T(1024)} %param.27) | copy-start | bytes 18436
  205.2 11.4 %copy-start.10 = (f32[1536]{0:T(1024)S(1)}, f32[1536]{0:T(1024)}, u32[]{:S(2)}) copy-start(f32[1536]{0:T(1024)} %param.28) | copy-start | bytes 18436
  205.2 11.4 %copy-start.12 = (f32[1536,16]{0,1:T(8,128)S(1)}, f32[1536,16]{0,1:T(8,128)}, u32[]{:S(2)}) copy-start(f32[1536,16]{0,1:T(8,128)} %param.29) | copy-start | bytes 294916
  208.2 145.5 %all-to-all-start.3 = ((bf16[16,2,14336]{2,1,0:T(2,128)(2,1)}), bf16[16,2,14336]{2,1,0:T(2,128)(2,1)S(1)}, u32[]{:S(2)}, u32[]{:S(2)}) async-start(bf16[16,2,14336]{2,1,0:T(2,128)(2,1)} %reshape.225), calls=%async_computation.3 | async-start | bytes 1835008 | tf_op jit(solution)/shard_map/all_to_all | solution.py:162
  214.5 305.3 %all-reduce.9.cloned.1.call-start = ((), (), s32[]{:S(2)}) async-start(), calls=%async_computation.5 | async-start | bytes 393216 | tf_op jit(solution)/shard_map/psum | solution.py:185
  254.9 422.6 %all-reduce.7.cloned.1.call-start = ((), (), s32[]{:S(2)}) async-start(), calls=%async_computation.4 | async-start | bytes 1572864 | tf_op jit(solution)/shard_map/psum | solution.py:184
  (10 other events, 14.9 us)
Sparse Core Ops, SparseCore 0:
  255.0 264.6 all-reduce.8
  524.1 153.4 all-reduce.6
where the time goes:
time: 692 us; the launch traced here: 690 us
  waiting for transfers between devices  379 us (55%)
  blocking collectives  163 us (24%)
  matrix products  45 us (7%)
  local copies, waits for them, and re-layouts  35.7 us (5%)
  starting transfers between devices  30.6 us (4%)
  other arithmetic  20.3 us (3%)
  between operations  15.1 us (2%)
    psum x1, waiting for transfers between devices, local(): lax.psum((in_grad, time_grad, gain_grad, out_grad), ('seq', 'head'))  163 us
    psum x1, waiting for transfers between devices, local(): cond_whole = lax.psum(cond_part, 'seq')  158 us
    psum x1, blocking collectives, local(): lax.psum((in_grad, time_grad, gain_grad, out_grad), ('seq', 'head'))  97.4 us
    unnamed x1, blocking collectives  33.2 us
    all_gather x1, blocking collectives, head_section(): lax.all_gather(cond_grad.astype(jnp.bfloat16), 'head', axis=0, tiled=True)  32.4 us
    all_to_all x1, waiting for transfers between devices, local(): lax.all_to_all(split_key, 'head', split_axis=1, concat_axis=0, tiled=True)  22.3 us
    all_to_all x1, waiting for transfers between devices, local(): lax.all_to_all(split_query, 'head', split_axis=1, concat_axis=0, tiled=True)  22.1 us
    dot_general x7, matrix products, update(): jnp.einsum('hqk,khd->qhd', weights.astype(jnp.bfloat16), value_block, pre...  20.4 us
  transfers between devices with their start and end apart: 8, of which 5 were waited for; matrix products, arithmetic and copies ran while one was open for 4% of the time, Pallas kernels for 0%

commit v1 on v0

v1 whole, which is shorter than its diff:
```python
import functools
import math

import jax
import jax.numpy as jnp
from jax import lax
from jax.experimental import pallas as pl
from jax.experimental.pallas import tpu as pltpu
from jax.sharding import PartitionSpec as P

HD = 128
LAT = 16
DRAWS = 4
NORM_EPS = 1e-06
HIDDEN_SCORE = -1e30
SLOT = 16
EXTRA = 128
PACK = 256
GROUP_ROWS = 16
LOG2E = 1.4426950408889634
F32 = jnp.float32
BF16 = jnp.bfloat16
VMEM_LIMIT = 56 * 1024 * 1024


def params():
    return pltpu.CompilerParams(vmem_limit_bytes=VMEM_LIMIT)


def vmem():
    return pl.BlockSpec(memory_space=pltpu.VMEM)


def anywhere():
    return pl.BlockSpec(memory_space=pl.ANY)


def dot(a, b):
    return jnp.dot(a, b, preferred_element_type=F32)


def two_parts(value):
    high = value.astype(BF16)
    return high, (value - high.astype(F32)).astype(BF16)


def load_keys(k_ref, v_ref, key_scr, val_scr):
    rows = key_scr.shape[0]
    key_scr[...] = k_ref[:, 0].reshape(rows, HD)
    val_scr[:, :HD] = v_ref[:, 0].reshape(rows, HD)
    val_scr[:, HD:] = jnp.ones((rows, HD), BF16)


def attend(query, query_rank, rank_ref, key_scr, val_scr, score_scr):
    total = key_scr.shape[0]
    chunk = math.gcd(total, 512)
    scale = LOG2E / math.sqrt(HD)
    top = None
    for start in range(0, total, chunk):
        scores = lax.dot_general(
            query,
            key_scr[start : start + chunk, :],
            (((1,), (1,)), ((), ())),
            preferred_element_type=F32,
        )
        visible = rank_ref[:, start : start + chunk] <= query_rank
        scores = jnp.where(visible, scores, HIDDEN_SCORE)
        score_scr[:, start : start + chunk] = scores
        for lane in range(0, chunk, 128):
            part = scores[:, lane : lane + 128]
            top = part if top is None else jnp.maximum(top, part)
    top = jnp.max(top, axis=1, keepdims=True)
    total_out = None
    for start in range(0, total, chunk):
        weights = jnp.exp2((score_scr[:, start : start + chunk] - top) * scale)
        mixed = dot(weights.astype(BF16), val_scr[start : start + chunk, :])
        total_out = mixed if total_out is None else total_out + mixed
    return total_out[:, :HD] / total_out[:, HD:]


def masked_kernel(
    q_ref, k_ref, v_ref, where_ref, qrank_ref, rank_ref, w_ref, part_ref, picked_ref,
    key_scr, val_scr, score_scr,
):
    load_keys(k_ref, v_ref, key_scr, val_scr)
    slots = where_ref.shape[0]
    total = key_scr.shape[0]
    chunk = math.gcd(total, 512)
    sources, _, each, _ = q_ref.shape
    query = jnp.zeros((slots, HD), F32)
    step = math.gcd(each * sources, each * 4)
    for start in range(0, total, step):
        lanes = lax.broadcasted_iota(jnp.int32, (slots, step), 1) + start
        hit = jnp.where(lanes == where_ref[...], 1.0, 0.0).astype(BF16)
        rows = q_ref[start // each : (start + step) // each, 0].reshape(step, HD)
        query = query + dot(hit, rows)
    out = attend(query.astype(BF16), qrank_ref[...], rank_ref, key_scr, val_scr, score_scr)
    picked = jnp.where(qrank_ref[...] >= 0, out, 0.0).astype(BF16)
    picked_ref[...] = picked
    part = dot(picked, w_ref[...]).astype(BF16)
    part_ref[...] = part.reshape(part_ref.shape)


def attend_masked(arrived, where, where_rank, rank_row, w_cond):
    heads, _, each, _ = arrived.shape
    total = heads * each
    slots = where.shape[0]
    width = w_cond.shape[1]
    return pl.pallas_call(
        masked_kernel,
        grid=(1,),
        in_specs=[
            pl.BlockSpec((heads, 1, each, HD), lambda i: (0, 0, 0, 0)),
            pl.BlockSpec((heads, 1, each, HD), lambda i: (0, 1, 0, 0)),
            pl.BlockSpec((heads, 1, each, HD), lambda i: (0, 2, 0, 0)),
            vmem(),
            vmem(),
            vmem(),
            vmem(),
        ],
        out_specs=[vmem(), vmem()],
        out_shape=[
            jax.ShapeDtypeStruct((heads, slots // heads, width), BF16),
            jax.ShapeDtypeStruct((slots, HD), BF16),
        ],
        scratch_shapes=[
            pltpu.VMEM((total, HD), BF16),
            pltpu.VMEM((total, 2 * HD), BF16),
            pltpu.VMEM((slots, total), F32),
        ],
        compiler_params=params(),
        name="masked_rows",
    )(arrived, arrived, arrived, where, where_rank, rank_row, w_cond)


def attend_kernel(q_ref, k_ref, v_ref, qrank_ref, rank_ref, *rest):
    out_ref, key_scr, val_scr, score_scr = rest[-4:]

    @pl.when(pl.program_id(0) == 0)
    def _():
        load_keys(k_ref, v_ref, key_scr, val_scr)

    out = attend(q_ref[0, 0], qrank_ref[0], rank_ref, key_scr, val_scr, score_scr)
    out_ref[0] = out.astype(BF16)


def attend_some(arrived, rank_column, rank_row, first, count, after, earlier=None):
    heads, _, each, _ = arrived.shape
    total = heads * each
    specs = [
        pl.BlockSpec((1, 1, each, HD), lambda i: (i + first, 0, 0, 0)),
        pl.BlockSpec((heads, 1, each, HD), lambda i: (0, 1, 0, 0)),
        pl.BlockSpec((heads, 1, each, HD), lambda i: (0, 2, 0, 0)),
        pl.BlockSpec((1, each, 1), lambda i: (i + first, 0, 0)),
        vmem(),
        anywhere(),
    ]
    operands = [arrived, arrived, arrived, rank_column, rank_row, after]
    aliases = {}
    if earlier is not None:
        specs.append(anywhere())
        operands.append(earlier)
        aliases = {len(operands) - 1: 0}
    return pl.pallas_call(
        attend_kernel,
        grid=(count,),
        in_specs=specs,
        out_specs=pl.BlockSpec((1, each, HD), lambda i: (i + first, 0, 0)),
        out_shape=jax.ShapeDtypeStruct((heads, each, HD), BF16),
        scratch_shapes=[
            pltpu.VMEM((total, HD), BF16),
            pltpu.VMEM((total, 2 * HD), BF16),
            pltpu.VMEM((each, total), F32),
        ],
        input_output_aliases=aliases,
        compiler_params=params(),
        name="attention",
    )(*operands)


def head_kernel(
    cond_ref, base_ref, gain_ref, outhi_ref, outlo_ref, outhi_t_ref, outlo_t_ref, noise_ref,
    weight_ref, feat_ref, after_ref, send_ref, block_scr,
):
    heads, rows, width = cond_ref.shape
    count = base_ref.shape[0]
    condition = cond_ref[0].astype(F32)
    for source in range(1, heads):
        condition = condition + cond_ref[source].astype(F32)
    hidden = base_ref[...] + jnp.concatenate([condition] * (count // rows), axis=0)
    inverse = lax.rsqrt(jnp.mean(hidden * hidden, axis=1, keepdims=True) + NORM_EPS)
    unit = hidden * inverse
    gain = gain_ref[...]
    scaled = unit * gain
    gate = 1.0 / (1.0 + jnp.exp(-scaled))
    active = scaled * gate
    act_hi, act_lo = two_parts(active)
    both = dot(jnp.concatenate([act_hi, act_lo], axis=0), outhi_ref[...])
    predicted = both[:count] + both[count:] + dot(act_hi, outlo_ref[...])
    pred_grad = (predicted - noise_ref[...]) * weight_ref[...]
    pg_hi, pg_lo = two_parts(pred_grad)
    both = dot(jnp.concatenate([pg_hi, pg_lo], axis=0), outhi_t_ref[...])
    act_grad = both[:count] + both[count:] + dot(pg_hi, outlo_t_ref[...])
    scaled_grad = act_grad * gate * (1.0 + scaled * (1.0 - gate))
    gain_grad = jnp.sum(scaled_grad * unit, axis=0, keepdims=True)
    unit_grad = scaled_grad * gain
    along = jnp.mean(unit_grad * unit, axis=1, keepdims=True)
    hidden_grad = inverse * (unit_grad - unit * along)
    hg_hi, hg_lo = two_parts(hidden_grad)
    feats = feat_ref[...]
    half = feats.shape[0] // 2
    both = dot(feats, hg_hi)
    feat_grad = both[:half] + both[half:] + dot(feats[:half], hg_lo)
    turned = jnp.transpose(pred_grad)[:LAT]
    tg_hi, tg_lo = two_parts(turned)
    both = dot(jnp.concatenate([tg_hi, tg_lo], axis=0), act_hi)
    out_grad = both[:LAT] + both[LAT:] + dot(tg_hi, act_lo)
    cond_grad = hidden_grad[:rows]
    for draw in range(1, count // rows):
        cond_grad = cond_grad + hidden_grad[draw * rows : (draw + 1) * rows]
    block_scr[:, :width] = cond_grad
    block_scr[:, width:] = jnp.zeros((rows, EXTRA), F32)
    pieces = width // EXTRA
    for target in range(heads):
        source_rows = feat_grad if 2 * target < LAT else out_grad
        begin = 2 * target % LAT
        block_scr[rows - 2 : rows, :width] = source_rows[begin : begin + 2]
        if target < pieces:
            cols = slice(target * EXTRA, (target + 1) * EXTRA)
            block_scr[0:1, width:] = feat_grad[LAT : LAT + 1, cols]
            block_scr[1:2, width:] = gain_grad[:, cols]
        elif target == pieces:
            block_scr[:, width:] = jnp.zeros((rows, EXTRA), F32)
        send_ref[target] = block_scr[...].astype(BF16)


def grad_kernel(got_ref, picked_ref, after_ref, send_ref, pack_scr):
    heads, rows, wide = got_ref.shape
    width = wide - EXTRA
    groups = send_ref.shape[0]
    cond_grad = got_ref[:, :, :width].reshape(heads * rows, width)
    part = lax.dot_general(
        picked_ref[...], cond_grad, (((0,), (0,)), ((), ())), preferred_element_type=F32
    ).astype(BF16)
    summed = got_ref[0].astype(F32)
    for source in range(1, heads):
        summed = summed + got_ref[source].astype(F32)
    pack_scr[...] = jnp.zeros(pack_scr.shape, F32)
    pieces = width // 128
    for piece in range(pieces):
        row, lane = 2 * (piece % 8), 128 * (piece // 8)
        pack_scr[row : row + 2, lane : lane + 128] = summed[
            rows - 2 : rows, piece * 128 : (piece + 1) * 128
        ]
    row, lane = 2 * (pieces % 8), 128 * (pieces // 8)
    pack_scr[row : row + 2, lane : lane + 128] = summed[0:2, width:]
    packed = pack_scr[...].astype(BF16)
    row_groups = HD // GROUP_ROWS
    col_groups = groups // row_groups
    cols = width // col_groups
    for group in range(groups):
        top = group // col_groups * GROUP_ROWS
        left = group % col_groups * cols
        send_ref[group, :, :cols] = part[top : top + GROUP_ROWS, left : left + cols]
        send_ref[group, :, cols:] = packed


def total_kernel(got_ref, big_ref, small_ref):
    groups, rows, wide = got_ref.shape
    cols = wide - PACK
    total = got_ref[0].astype(F32)
    for source in range(1, groups):
        total = total + got_ref[source].astype(F32)
    rounded = total.astype(BF16)
    for group in range(groups):
        big_ref[group] = rounded[:, :cols]
    for head in range(small_ref.shape[0]):
        small_ref[head] = rounded[:, cols:]


def spread_kernel(big_ref, small_ref, cond_ref, in_ref, time_ref, gain_ref, out_ref):
    groups, rows, cols = big_ref.shape
    heads = small_ref.shape[0]
    width = cond_ref.shape[1]
    col_groups = width // cols
    for group in range(groups):
        top = group // col_groups * GROUP_ROWS
        left = group % col_groups * cols
        cond_ref[top : top + GROUP_ROWS, left : left + cols] = big_ref[group].astype(F32)
    pieces = width // 128
    for head in range(heads):
        packed = small_ref[head].astype(F32)
        target = in_ref if 2 * head < LAT else out_ref
        begin = 2 * head % LAT
        for piece in range(pieces):
            row, lane = 2 * (piece % 8), 128 * (piece // 8)
            target[begin : begin + 2, piece * 128 : (piece + 1) * 128] = packed[
                row : row + 2, lane : lane + 128
            ]
        if head < pieces:
            row, lane = 2 * (pieces % 8), 128 * (pieces // 8)
            cut = slice(head * 128, (head + 1) * 128)
            time_ref[:, cut] = packed[row : row + 1, lane : lane + 128]
            gain_ref[:, cut] = packed[row + 1 : row + 2, lane : lane + 128]


def call(kernel, out_shape, scratch, name, *operands, unread=0):
    specs = [vmem()] * (len(operands) - unread) + [anywhere()] * unread
    many = isinstance(out_shape, list)
    return pl.pallas_call(
        kernel,
        in_specs=specs,
        out_specs=[vmem()] * len(out_shape) if many else vmem(),
        out_shape=out_shape,
        scratch_shapes=scratch,
        compiler_params=params(),
        name=name,
    )(*operands)


def exchange(value, axis):
    return lax.all_to_all(value, axis, split_axis=0, concat_axis=0, tiled=True)


def local(
    queries, key_rows, value_rows, token_rank, masked_index, masked_counts, clean_latents,
    noise_draws, noise_times, w_cond, w_in, time_vec, norm_gain, w_out,
):
    each = queries.shape[0]
    heads = lax.axis_size("head")
    groups = lax.axis_size("seq")
    total = each * heads
    width = w_cond.shape[1]
    share = masked_index.shape[1] // heads
    count = DRAWS * SLOT

    stacked = jnp.stack([queries, key_rows, value_rows])
    stacked = jnp.transpose(stacked.reshape(3, each, heads, HD), (2, 0, 1, 3))
    arrived = exchange(stacked, "head")

    chosen = masked_index[0]
    live = lax.dynamic_index_in_dim(masked_counts, lax.axis_index("seq"), 0, keepdims=False)
    alive = jnp.arange(heads * share, dtype=jnp.int32) < live
    ranks = token_rank[0]

    def in_slots(value, fill):
        value = value.reshape(heads, share)
        return jnp.pad(value, ((0, 0), (0, SLOT - share)), constant_values=fill)

    where = in_slots(jnp.where(alive, chosen, -1), -1).reshape(heads * SLOT, 1)
    where_rank = in_slots(jnp.where(alive, jnp.take(ranks, chosen), -1), -1)
    where_rank = where_rank.reshape(heads * SLOT, 1)
    rank_row = ranks.reshape(1, total)
    rank_column = ranks.reshape(heads, each, 1)

    mine = lax.dynamic_index_in_dim(
        in_slots(chosen, 0), lax.axis_index("head"), 0, keepdims=False
    )
    my_alive = lax.dynamic_index_in_dim(
        in_slots(alive.astype(F32), 0.0), lax.axis_index("head"), 0, keepdims=False
    )
    clean = jnp.take(clean_latents, mine, axis=0).astype(F32)
    noise = jnp.take(noise_draws, mine, axis=0).astype(F32)
    times = jnp.take(noise_times, mine, axis=0).astype(F32)
    noise = jnp.transpose(noise.reshape(SLOT, DRAWS, LAT), (1, 0, 2))
    times = jnp.transpose(times)[:, :, None]
    angles = 0.5 * math.pi * times
    noisy = (jnp.cos(angles) * clean[None] + jnp.sin(angles) * noise).reshape(count, LAT)
    times = times.reshape(count, 1)
    noise = noise.reshape(count, LAT)
    base = jnp.dot(noisy, w_in, precision=lax.Precision.HIGHEST) + times * time_vec
    loss_scale = 1.0 / math.sqrt(masked_index.shape[1] // 3 * groups * DRAWS)
    row_weight = jnp.tile(my_alive * (2.0 * loss_scale), DRAWS).reshape(count, 1)
    feats = jnp.pad(jnp.concatenate([noisy, times], axis=1), ((0, 0), (0, 15))).T
    feats = jnp.concatenate(two_parts(feats), axis=0)
    out_wide = jnp.pad(w_out, ((0, 0), (0, 128 - LAT)))
    out_hi, out_lo = two_parts(out_wide)
    noise = jnp.pad(noise, ((0, 0), (0, 128 - LAT)))

    part, picked = attend_masked(arrived, where, where_rank, rank_row, w_cond)
    half = heads // 2
    got_cond = exchange(part, "head")
    first_half = attend_some(arrived, rank_column, rank_row, 0, half, part)

    send = call(
        head_kernel,
        jax.ShapeDtypeStruct((heads, SLOT, width + EXTRA), BF16),
        [pltpu.VMEM((SLOT, width + EXTRA), F32)],
        "diffusion_head",
        got_cond, base, norm_gain.reshape(1, width), out_hi, out_lo, out_hi.T, out_lo.T,
        noise, row_weight, feats, first_half,
        unread=1,
    )
    got_grad = exchange(send, "head")
    attended = attend_some(arrived, rank_column, rank_row, half, half, send, first_half)

    col_groups = groups // (HD // GROUP_ROWS)
    cols = width // col_groups
    parts = call(
        grad_kernel,
        jax.ShapeDtypeStruct((groups, GROUP_ROWS, cols + PACK), BF16),
        [pltpu.VMEM((GROUP_ROWS, PACK), F32)],
        "cond_weight_grad",
        got_grad, picked, attended,
        unread=1,
    )
    got_parts = exchange(parts, "seq")
    returned = exchange(attended, "head")
    big, small = call(
        total_kernel,
        [
            jax.ShapeDtypeStruct((groups, GROUP_ROWS, cols), BF16),
            jax.ShapeDtypeStruct((heads, GROUP_ROWS, PACK), BF16),
        ],
        [],
        "sum_over_clips",
        got_parts,
    )
    all_big = exchange(big, "seq")
    all_small = exchange(small, "head")
    cond_whole, in_grad, time_grad, gain_grad, out_grad = call(
        spread_kernel,
        [
            jax.ShapeDtypeStruct((HD, width), F32),
            jax.ShapeDtypeStruct((LAT, width), F32),
            jax.ShapeDtypeStruct((1, width), F32),
            jax.ShapeDtypeStruct((1, width), F32),
            jax.ShapeDtypeStruct((LAT, width), F32),
        ],
        [],
        "write_gradients",
        all_big, all_small,
    )
    attended_rows = jnp.transpose(returned, (1, 0, 2)).reshape(each, heads * HD)
    return (
        attended_rows, cond_whole, in_grad, time_grad.reshape(width),
        gain_grad.reshape(width), out_grad.T,
    )


def solution(mesh):
    return jax.shard_map(
        local,
        mesh=mesh,
        in_specs=(
            P(("seq", "head"), None),
            P(("seq", "head"), None),
            P(("seq", "head"), None),
            P("seq", None),
            P("seq", None),
            P(),
            P("seq", None),
            P("seq", None),
            P("seq", None),
            P("head", None),
            P(),
            P(),
            P(),
            P(),
        ),
        out_specs=(P(("seq", "head"), None), P("head", None), P(), P(), P(), P()),
        check_vma=False,
    )
```

time: 692 us -> 260 us (0.38)
  waiting for transfers between devices: 379 us -> 84 us
  blocking collectives: 163 us -> 40.8 us
  Pallas kernels: 0 us -> 56.8 us
  matrix products: 45 us -> 1.3 us
  between operations: 15.1 us -> 0.94 us
  other arithmetic: 20.3 us -> 8.12 us
  local copies, waits for them, and re-layouts: 35.7 us -> 27.2 us
    psum x2 -> x0, waiting for transfers between devices: 321 us -> none  [the longest x1 163 us: local(): lax.psum((in_grad, time_grad, gain_grad, out_grad), ('seq', 'head'))]
    psum x1 -> x0, blocking collectives: 97.4 us -> none  [local(): lax.psum((in_grad, time_grad, gain_grad, out_grad), ('seq', 'head'))]
    pallas_call x0 -> x7, Pallas kernels: none -> 56.8 us  [the longest x2 40.3 us: attend_some(): pl.pallas_call(attend_kernel, grid=(count,), in_specs=specs, out_specs=pl...]
    dot_general x21 -> x1, matrix products: 45 us -> 1.3 us  [local(): jnp.dot(noisy, w_in, precision=lax.Precision.HIGHEST) + times * time_vec]
    all_to_all x0 -> x2, blocking collectives: none -> 40.8 us  [exchange(): return lax.all_to_all(value, axis, split_axis=0, concat_axis=0, tiled=True)]
    unnamed x1 -> x0, blocking collectives: 33.2 us -> none
    all_gather x1 -> x0, blocking collectives: 32.4 us -> none  [head_section(): lax.all_gather(cond_grad.astype(jnp.bfloat16), 'head', axis=0, tiled=True)]
    all_to_all x4 -> x5, waiting for transfers between devices: 58 us -> 84 us  [exchange(): return lax.all_to_all(value, axis, split_axis=0, concat_axis=0, tiled=True)]
  transfers between devices with their start and end apart: 8 -> 5, of which waited for: 5 -> 4; matrix products, arithmetic and copies ran while one was open for 4% -> 10% of each run, Pallas kernels for 0% -> 16%
where the time goes in v1:
time: 260 us; the launch traced here: 256 us
  waiting for transfers between devices  84 us (32%)
  Pallas kernels  56.8 us (22%)
  blocking collectives  40.8 us (16%)
  starting transfers between devices  37.1 us (14%)
  local copies, waits for them, and re-layouts  27.2 us (10%)
  other arithmetic  8.12 us (3%)
    all_to_all x5, waiting for transfers between devices, exchange(): return lax.all_to_all(value, axis, split_axis=0, concat_axis=0, tiled=True)  84 us
    all_to_all x2, blocking collectives, exchange(): return lax.all_to_all(value, axis, split_axis=0, concat_axis=0, tiled=True)  40.8 us
    pallas_call x2, Pallas kernels, attend_some(): pl.pallas_call(attend_kernel, grid=(count,), in_specs=specs, out_specs=pl...  40.3 us
    all_to_all x5, starting transfers between devices, exchange(): return lax.all_to_all(value, axis, split_axis=0, concat_axis=0, tiled=True)  37.1 us
    pallas_call x4, Pallas kernels, call(): pl.pallas_call(kernel, in_specs=specs, out_specs=[vmem()] * len(out_shape...  10.3 us
    unnamed x39, local copies, waits for them, and re-layouts  9.1 us
    pallas_call x1, Pallas kernels, attend_masked(): pl.pallas_call(masked_kernel, grid=(1,), in_specs=[pl.BlockSpec((heads, 1...  6.2 us
  transfers between devices with their start and end apart: 5, of which 4 were waited for; matrix products, arithmetic and copies ran while one was open for 10% of the time, Pallas kernels for 16%

profile of v1, /device:TPU:6, one launch (start us, length us, event | category | flops | bytes accessed | tf_op | source)
XLA Modules:
  0.0 256.2 jit_solution(15279531243222670641)
XLA Ops:
  3.7 1.8 maximum_bitcast_fusion
  5.6 10.6 %all-to-all-start = ((bf16[16,3,224,128]{3,2,1,0:T(8,128)(2,1)}), bf16[16,3,224,128]{3,2,1,0:T(8,128)(2,1)S(1)}, u32[]{:S(2)}, u32[]{:S(2)}) async-start(bf16[16,3,224,128]{3,2,1,0:T(8,128)(2,1)} %maximum_bitcast_fusion), calls=%async_computation | async-start | bytes 5505024 | tf_op jit(solution)/shard_map/all_to_all | solution.py:322
  18.8 1.9 gather_fusion.1
  21.0 2.9 %reshape_squeeze.5.qrank_ref = s32[16,224,1]{2,1,0:T(8,128)} reshape(s32[3584]{0:T(1024)S(1)} %reduce) | data formatting | bytes 28672 | tf_op jit(solution)/shard_map/reshape;squeeze | solution.py:354
  23.9 1.7 gather_fusion
  30.9 48.5 %all-to-all-done.q_ref.k_ref.v_ref = bf16[16,3,224,128]{3,2,1,0:T(8,128)(2,1)S(1)} async-done(((bf16[16,3,224,128]{3,2,1,0:T(8,128)(2,1)}), bf16[16,3,224,128]{3,2,1,0:T(8,128)(2,1)S(1)}, u32[]{:S(2)}, u32[]{:S(2)}) %all-to-all-start) | async-done | bytes 2752544 | tf_op jit(solution)/shard_map/all_to_all | solution.py:322
  79.5 1.6 copy-done.1
  81.0 6.2 %masked_rows.1 = (bf16[16,16,1536]{2,1,0:T(8,128)(2,1)}, bf16[256,128]{1,0:T(8,128)(2,1)}) custom-call(bf16[16,3,224,128]{3,2,1,0:T(8,128)(2,1)} %copy-done.1, bf16[16,3,224,128]{3,2,1,0:T(8,128)(2,1)} %copy-done.1, bf16[16,3,224,128]{3,2,1,0:T(8,128)(2,1)} %copy-done.1, s32[256,1]{1,0:T(8,128)} %reshape.186.where_ref, s32[256,1]{1,0:T(8,128)} %reshape.187.qrank_ref, ...), custom_call_target="tpu_custom_call" | custom-call | tf_op jit(solution)/shard_map/masked_rows/pallas_call | solution.py:109
  87.2 4.8 %all-to-all-start.1 = ((bf16[16,16,1536]{2,1,0:T(8,128)(2,1)}), bf16[16,16,1536]{2,1,0:T(8,128)(2,1)S(1)}, u32[]{:S(2)}, u32[]{:S(2)}) async-start(bf16[16,16,1536]{2,1,0:T(8,128)(2,1)} %get-tuple-element.15.rest_0_), calls=%async_computation.1 | async-start | bytes 1572864 | tf_op jit(solution)/shard_map/all_to_all | solution.py:322
  94.3 1.9 copy.68.outhi_ref
  101.4 20.1 %attention.2.after_ref.rest_1_ = bf16[16,224,128]{2,1,0:T(8,128)(2,1)} custom-call(bf16[16,3,224,128]{3,2,1,0:T(8,128)(2,1)} %copy-done.1, bf16[16,3,224,128]{3,2,1,0:T(8,128)(2,1)} %copy-done.1, bf16[16,3,224,128]{3,2,1,0:T(8,128)(2,1)} %copy-done.1, s32[16,224,1]{2,1,0:T(8,128)} %reshape_squeeze.5.qrank_ref, s32[1,3584]{1,0:T(1,128)} %rank_ref.5, ...), custom_call_target="tpu_custom_call" | custom-call | tf_op jit(solution)/shard_map/attention/pallas_call | solution.py:164
  122.4 4.0 %diffusion_head.1.rest_0_ = bf16[16,16,1664]{2,1,0:T(8,128)(2,1)} custom-call(bf16[16,16,1536]{2,1,0:T(8,128)(2,1)} %copy-done.3, f32[64,1536]{1,0:T(8,128)} %convolution_add_fusion.base_ref, f32[1,1536]{1,0:T(1,128)} %reshape.149.gain_ref, bf16[1536,128]{1,0:T(8,128)(2,1)} %copy.68.outhi_ref, bf16[1536,128]{1,0:T(8,128)(2,1)} %copy.69.outlo_ref, ...), custom_call_target="tpu_custom_call" | custom-call | tf_op jit(solution)/shard_map/diffusion_head/pallas_call | solution.py:310
  126.4 7.2 %all-to-all-start.3 = ((bf16[16,16,1664]{2,1,0:T(8,128)(2,1)}), bf16[16,16,1664]{2,1,0:T(8,128)(2,1)S(1)}, u32[]{:S(2)}, u32[]{:S(2)}) async-start(bf16[16,16,1664]{2,1,0:T(8,128)(2,1)} %diffusion_head.1.rest_0_), calls=%async_computation.3 | async-start | bytes 1703936 | tf_op jit(solution)/shard_map/all_to_all | solution.py:322
  133.6 20.2 %attention.3.after_ref = bf16[16,224,128]{2,1,0:T(8,128)(2,1)} custom-call(bf16[16,3,224,128]{3,2,1,0:T(8,128)(2,1)} %copy-done.1, bf16[16,3,224,128]{3,2,1,0:T(8,128)(2,1)} %copy-done.1, bf16[16,3,224,128]{3,2,1,0:T(8,128)(2,1)} %copy-done.1, s32[16,224,1]{2,1,0:T(8,128)} %reshape_squeeze.5.qrank_ref, ...), custom_call_target="tpu_custom_call", output_to_operand_aliasing={{}: (6, {})} | custom-call | tf_op jit(solution)/shard_map/attention/pallas_call | solution.py:164
  153.8 1.7 all-to-all-done.3.got_ref
  156.4 2.3 cond_weight_grad.1
  158.7 26.9 %all_to_all.35.got_ref = bf16[32,16,640]{2,1,0:T(8,128)(2,1)} all-to-all(bf16[32,16,640]{2,1,0:T(8,128)(2,1)} %cond_weight_grad.1), channel_id=1, replica_groups=mesh['seq'=32,'head'=16] {'seq'}, dimensions={0} | all-to-all | bytes 1310720 | tf_op jit(solution)/shard_map/all_to_all | solution.py:322
  185.6 7.0 %all-to-all-start.2 = ((bf16[16,224,128]{2,1,0:T(8,128)(2,1)}), bf16[16,224,128]{2,1,0:T(8,128)(2,1)S(1)}, u32[]{:S(2)}, u32[]{:S(2)}) async-start(bf16[16,224,128]{2,1,0:T(8,128)(2,1)} %attention.3.after_ref), calls=%async_computation.2 | async-start | bytes 1835008 | tf_op jit(solution)/shard_map/all_to_all | solution.py:322
  192.6 2.0 sum_over_clips.1
  194.6 21.7 %all-to-all-done.2 = bf16[16,224,128]{2,1,0:T(8,128)(2,1)S(1)} async-done(((bf16[16,224,128]{2,1,0:T(8,128)(2,1)}), bf16[16,224,128]{2,1,0:T(8,128)(2,1)S(1)}, u32[]{:S(2)}, u32[]{:S(2)}) %all-to-all-start.2) | async-done | bytes 917536 | tf_op jit(solution)/shard_map/all_to_all | solution.py:322
  216.3 13.9 %all_to_all.36.small_ref = bf16[16,16,256]{2,1,0:T(8,128)(2,1)} all-to-all(bf16[16,16,256]{2,1,0:T(8,128)(2,1)} %get-tuple-element.18), channel_id=1, replica_groups=mesh['seq'=32,'head'=16] {'head'}, dimensions={0} | all-to-all | bytes 262144 | tf_op jit(solution)/shard_map/all_to_all | solution.py:322
  230.2 7.5 %all-to-all-start.5 = ((bf16[32,16,384]{2,1,0:T(8,128)(2,1)}), bf16[32,16,384]{2,1,0:T(8,128)(2,1)S(1)}, u32[]{:S(2)}, u32[]{:S(2)}) async-start(bf16[32,16,384]{2,1,0:T(8,128)(2,1)} %get-tuple-element.17), calls=%async_computation.5 | async-start | bytes 786432 | tf_op jit(solution)/shard_map/all_to_all | solution.py:322
  238.7 12.1 %all-to-all-done.5.big_ref = bf16[32,16,384]{2,1,0:T(8,128)(2,1)S(1)} async-done(((bf16[32,16,384]{2,1,0:T(8,128)(2,1)}), bf16[32,16,384]{2,1,0:T(8,128)(2,1)S(1)}, u32[]{:S(2)}, u32[]{:S(2)}) %all-to-all-start.5) | async-done | bytes 393248 | tf_op jit(solution)/shard_map/all_to_all | solution.py:322
  251.5 2.0 write_gradients.1
  (88 shorter events, 24.7 us)
Async XLA Ops:
  0.6 99.5 %copy-start = (f32[16,1536]{1,0:T(8,128)S(1)}, f32[16,1536]{1,0:T(8,128)}, u32[]{:S(2)}) copy-start(f32[16,1536]{1,0:T(8,128)} %param.24) | copy-start | bytes 294916
  0.6 1.7 copy-start.5
  2.1 1.2 copy-start.6
  5.6 11.1 %copy-start.14 = (s32[1,224]{1,0:T(1,128)S(1)}, s32[1,224]{1,0:T(1,128)}, u32[]{:S(2)}) copy-start(s32[1,224]{1,0:T(1,128)} %param.18) | copy-start | bytes 2692
  5.6 11.9 %copy-start.11 = (bf16[3584,4]{0,1:T(4,128)(2,1)S(1)}, bf16[3584,4]{0,1:T(4,128)(2,1)}, u32[]{:S(2)}) copy-start(bf16[3584,4]{0,1:T(4,128)(2,1)} %param.22) | copy-start | bytes 86020
  5.6 15.3 %copy-start.9 = (s32[1,3584]{1,0:T(1,128)S(1)}, s32[1,3584]{1,0:T(1,128)}, u32[]{:S(2)}) copy-start(s32[1,3584]{1,0:T(1,128)} %rank_ref.5) | copy-start | bytes 43012
  5.6 73.9 %all-to-all-start = ((bf16[16,3,224,128]{3,2,1,0:T(8,128)(2,1)}), bf16[16,3,224,128]{3,2,1,0:T(8,128)(2,1)S(1)}, u32[]{:S(2)}, u32[]{:S(2)}) async-start(bf16[16,3,224,128]{3,2,1,0:T(8,128)(2,1)} %maximum_bitcast_fusion), calls=%async_computation | async-start | bytes 5505024 | tf_op jit(solution)/shard_map/all_to_all | solution.py:322
  16.1 9.6 %copy-start.15 = (s32[32]{0:T(128)S(1)}, s32[32]{0:T(128)}, u32[]{:S(2)}) copy-start(s32[32]{0:T(128)} %param.19) | copy-start | bytes 388
  16.2 13.0 %copy-start.8 = (f32[1536,16]{0,1:T(8,128)S(1)}, f32[1536,16]{0,1:T(8,128)}, u32[]{:S(2)}) copy-start(f32[1536,16]{0,1:T(8,128)} %param.27) | copy-start | bytes 294916
  30.9 61.1 %copy-start.13 = (f32[1536]{0:T(1024)S(1)}, f32[1536]{0:T(1024)}, u32[]{:S(2)}) copy-start(f32[1536]{0:T(1024)} %param.26) | copy-start | bytes 18436
  79.5 1.6 copy-start.1
  87.2 9.0 %copy-start.10 = (bf16[3584,16]{0,1:T(8,128)(2,1)S(1)}, bf16[3584,16]{0,1:T(8,128)(2,1)}, u32[]{:S(2)}) copy-start(bf16[3584,16]{0,1:T(8,128)(2,1)} %param.20) | copy-start | bytes 344068
  87.2 10.1 %copy-start.7 = (bf16[3584,64]{0,1:T(8,128)(2,1)S(1)}, bf16[3584,64]{0,1:T(8,128)(2,1)}, u32[]{:S(2)}) copy-start(bf16[3584,64]{0,1:T(8,128)(2,1)} %param.21) | copy-start | bytes 1376260
  87.2 12.9 %copy-start.12 = (f32[1536]{0:T(1024)S(1)}, f32[1536]{0:T(1024)}, u32[]{:S(2)}) copy-start(f32[1536]{0:T(1024)} %param.25) | copy-start | bytes 18436
  87.2 34.3 %all-to-all-start.1 = ((bf16[16,16,1536]{2,1,0:T(8,128)(2,1)}), bf16[16,16,1536]{2,1,0:T(8,128)(2,1)S(1)}, u32[]{:S(2)}, u32[]{:S(2)}) async-start(bf16[16,16,1536]{2,1,0:T(8,128)(2,1)} %get-tuple-element.15.rest_0_), calls=%async_computation.1 | async-start | bytes 1572864 | tf_op jit(solution)/shard_map/all_to_all | solution.py:322
  121.5 0.9 copy-start.3
  126.4 29.1 %all-to-all-start.3 = ((bf16[16,16,1664]{2,1,0:T(8,128)(2,1)}), bf16[16,16,1664]{2,1,0:T(8,128)(2,1)S(1)}, u32[]{:S(2)}, u32[]{:S(2)}) async-start(bf16[16,16,1664]{2,1,0:T(8,128)(2,1)} %diffusion_head.1.rest_0_), calls=%async_computation.3 | async-start | bytes 1703936 | tf_op jit(solution)/shard_map/all_to_all | solution.py:322
  155.5 0.9 copy-start.2
  185.6 30.7 %all-to-all-start.2 = ((bf16[16,224,128]{2,1,0:T(8,128)(2,1)}), bf16[16,224,128]{2,1,0:T(8,128)(2,1)S(1)}, u32[]{:S(2)}, u32[]{:S(2)}) async-start(bf16[16,224,128]{2,1,0:T(8,128)(2,1)} %attention.3.after_ref), calls=%async_computation.2 | async-start | bytes 1835008 | tf_op jit(solution)/shard_map/all_to_all | solution.py:322
  230.2 20.6 %all-to-all-start.5 = ((bf16[32,16,384]{2,1,0:T(8,128)(2,1)}), bf16[32,16,384]{2,1,0:T(8,128)(2,1)S(1)}, u32[]{:S(2)}, u32[]{:S(2)}) async-start(bf16[32,16,384]{2,1,0:T(8,128)(2,1)} %get-tuple-element.17), calls=%async_computation.5 | async-start | bytes 786432 | tf_op jit(solution)/shard_map/all_to_all | solution.py:322
  250.8 0.8 copy-start.4

commit v2 on v1

--- a/solution.py
+++ b/solution.py
@@ -16,11 +16,13 @@
 SLOT = 16
 EXTRA = 128
 PACK = 256
+TAIL = 32
 GROUP_ROWS = 16
+CHIPS_Y = 8
 LOG2E = 1.4426950408889634
 F32 = jnp.float32
 BF16 = jnp.bfloat16
-VMEM_LIMIT = 56 * 1024 * 1024
+VMEM_LIMIT = 32 * 1024 * 1024
 
 
 def params():
@@ -44,10 +46,37 @@
     return high, (value - high.astype(F32)).astype(BF16)
 
 
-def load_keys(k_ref, v_ref, key_scr, val_scr):
+def in_vmem(value):
+    return pltpu.with_memory_space_constraint(value, pltpu.VMEM)
+
+
+def stack_kernel(q_ref, k_ref, v_ref, out_ref):
+    for head in range(out_ref.shape[0]):
+        cols = slice(head * HD, (head + 1) * HD)
+        out_ref[head, 0] = q_ref[:, cols]
+        out_ref[head, 1] = k_ref[:, cols]
+        out_ref[head, 2] = v_ref[:, cols]
+
+
+def stack_by_head(queries, key_rows, value_rows, heads):
+    each = queries.shape[0]
+    block = heads // 4
+    spec = pl.BlockSpec((each, block * HD), lambda i: (0, i))
+    return pl.pallas_call(
+        stack_kernel,
+        grid=(4,),
+        in_specs=[spec, spec, spec],
+        out_specs=pl.BlockSpec((block, 3, each, HD), lambda i: (i, 0, 0, 0)),
+        out_shape=jax.ShapeDtypeStruct((heads, 3, each, HD), BF16),
+        compiler_params=params(),
+        name="stack_by_head",
+    )(queries, key_rows, value_rows)
+
+
+def load_keys(got_ref, key_scr, val_scr):
     rows = key_scr.shape[0]
-    key_scr[...] = k_ref[:, 0].reshape(rows, HD)
-    val_scr[:, :HD] = v_ref[:, 0].reshape(rows, HD)
+    key_scr[...] = got_ref[:, 1].reshape(rows, HD)
+    val_scr[:, :HD] = got_ref[:, 2].reshape(rows, HD)
     val_scr[:, HD:] = jnp.ones((rows, HD), BF16)
 
 
@@ -78,21 +107,18 @@
     return total_out[:, :HD] / total_out[:, HD:]
 
 
-def masked_kernel(
-    q_ref, k_ref, v_ref, where_ref, qrank_ref, rank_ref, w_ref, part_ref, picked_ref,
-    key_scr, val_scr, score_scr,
-):
-    load_keys(k_ref, v_ref, key_scr, val_scr)
+def masked_kernel(got_ref, where_ref, qrank_ref, rank_ref, w_ref, *rest):
+    part_ref, picked_ref, key_scr, val_scr, score_scr = rest[-5:]
+    load_keys(got_ref, key_scr, val_scr)
     slots = where_ref.shape[0]
     total = key_scr.shape[0]
-    chunk = math.gcd(total, 512)
-    sources, _, each, _ = q_ref.shape
+    sources, _, each, _ = got_ref.shape
     query = jnp.zeros((slots, HD), F32)
     step = math.gcd(each * sources, each * 4)
     for start in range(0, total, step):
         lanes = lax.broadcasted_iota(jnp.int32, (slots, step), 1) + start
         hit = jnp.where(lanes == where_ref[...], 1.0, 0.0).astype(BF16)
-        rows = q_ref[start // each : (start + step) // each, 0].reshape(step, HD)
+        rows = got_ref[start // each : (start + step) // each, 0].reshape(step, HD)
         query = query + dot(hit, rows)
     out = attend(query.astype(BF16), qrank_ref[...], rank_ref, key_scr, val_scr, score_scr)
     picked = jnp.where(qrank_ref[...] >= 0, out, 0.0).astype(BF16)
@@ -101,23 +127,14 @@
     part_ref[...] = part.reshape(part_ref.shape)
 
 
-def attend_masked(arrived, where, where_rank, rank_row, w_cond):
+def attend_masked(arrived, where, where_rank, rank_row, w_cond, after):
     heads, _, each, _ = arrived.shape
     total = heads * each
     slots = where.shape[0]
     width = w_cond.shape[1]
     return pl.pallas_call(
         masked_kernel,
-        grid=(1,),
-        in_specs=[
-            pl.BlockSpec((heads, 1, each, HD), lambda i: (0, 0, 0, 0)),
-            pl.BlockSpec((heads, 1, each, HD), lambda i: (0, 1, 0, 0)),
-            pl.BlockSpec((heads, 1, each, HD), lambda i: (0, 2, 0, 0)),
-            vmem(),
-            vmem(),
-            vmem(),
-            vmem(),
-        ],
+        in_specs=[vmem()] * 5 + [anywhere()] * len(after),
         out_specs=[vmem(), vmem()],
         out_shape=[
             jax.ShapeDtypeStruct((heads, slots // heads, width), BF16),
@@ -130,17 +147,18 @@
         ],
         compiler_params=params(),
         name="masked_rows",
-    )(arrived, arrived, arrived, where, where_rank, rank_row, w_cond)
-
-
-def attend_kernel(q_ref, k_ref, v_ref, qrank_ref, rank_ref, *rest):
+    )(arrived, where, where_rank, rank_row, w_cond, *after)
+
+
+def attend_kernel(first, got_ref, qrank_ref, rank_ref, *rest):
     out_ref, key_scr, val_scr, score_scr = rest[-4:]
 
     @pl.when(pl.program_id(0) == 0)
     def _():
-        load_keys(k_ref, v_ref, key_scr, val_scr)
-
-    out = attend(q_ref[0, 0], qrank_ref[0], rank_ref, key_scr, val_scr, score_scr)
+        load_keys(got_ref, key_scr, val_scr)
+
+    query = got_ref[pl.program_id(0) + first, 0]
+    out = attend(query, qrank_ref[0], rank_ref, key_scr, val_scr, score_scr)
     out_ref[0] = out.astype(BF16)
 
 
@@ -148,25 +166,23 @@
     heads, _, each, _ = arrived.shape
     total = heads * each
     specs = [
-        pl.BlockSpec((1, 1, each, HD), lambda i: (i + first, 0, 0, 0)),
-        pl.BlockSpec((heads, 1, each, HD), lambda i: (0, 1, 0, 0)),
-        pl.BlockSpec((heads, 1, each, HD), lambda i: (0, 2, 0, 0)),
+        vmem(),
         pl.BlockSpec((1, each, 1), lambda i: (i + first, 0, 0)),
         vmem(),
         anywhere(),
     ]
-    operands = [arrived, arrived, arrived, rank_column, rank_row, after]
+    operands = [arrived, rank_column, rank_row, after]
     aliases = {}
     if earlier is not None:
         specs.append(anywhere())
         operands.append(earlier)
         aliases = {len(operands) - 1: 0}
     return pl.pallas_call(
-        attend_kernel,
+        functools.partial(attend_kernel, first),
         grid=(count,),
         in_specs=specs,
         out_specs=pl.BlockSpec((1, each, HD), lambda i: (i + first, 0, 0)),
-        out_shape=jax.ShapeDtypeStruct((heads, each, HD), BF16),
+        out_shape=jax.ShapeDtypeStruct((heads, each + TAIL, HD), BF16),
         scratch_shapes=[
             pltpu.VMEM((total, HD), BF16),
             pltpu.VMEM((total, 2 * HD), BF16),
@@ -265,43 +281,91 @@
         send_ref[group, :, cols:] = packed
 
 
-def total_kernel(got_ref, big_ref, small_ref):
+def total_kernel(got_ref, attended_ref, big_ref, tail_ref):
     groups, rows, wide = got_ref.shape
     cols = wide - PACK
     total = got_ref[0].astype(F32)
     for source in range(1, groups):
         total = total + got_ref[source].astype(F32)
     rounded = total.astype(BF16)
-    for group in range(groups):
-        big_ref[group] = rounded[:, :cols]
-    for head in range(small_ref.shape[0]):
-        small_ref[head] = rounded[:, cols:]
-
-
-def spread_kernel(big_ref, small_ref, cond_ref, in_ref, time_ref, gain_ref, out_ref):
-    groups, rows, cols = big_ref.shape
-    heads = small_ref.shape[0]
+    big_ref[...] = rounded[:, :cols]
+    for head in range(tail_ref.shape[0]):
+        tail_ref[head, :rows] = rounded[:, cols : cols + HD]
+        tail_ref[head, rows:] = rounded[:, cols + HD :]
+
+
+def total_over_clips(got, attended, each):
+    groups, rows, wide = got.shape
+    heads = attended.shape[0]
+    return pl.pallas_call(
+        total_kernel,
+        grid=(1,),
+        in_specs=[vmem(), anywhere()],
+        out_specs=[vmem(), pl.BlockSpec((heads, TAIL, HD), lambda i: (0, each // TAIL, 0))],
+        out_shape=[
+            jax.ShapeDtypeStruct((rows, wide - PACK), BF16),
+            jax.ShapeDtypeStruct(attended.shape, BF16),
+        ],
+        input_output_aliases={1: 1},
+        compiler_params=params(),
+        name="sum_over_clips",
+    )(got, attended)
+
+
+def spread_kernel(seq_ref, *refs):
+    big_refs = refs[:-6]
+    tail_ref, cond_ref, in_ref, time_ref, gain_ref, out_ref = refs[-6:]
+    far, rows, cols = big_refs[0].shape
+    near = len(big_refs)
+    heads = tail_ref.shape[0]
     width = cond_ref.shape[1]
     col_groups = width // cols
-    for group in range(groups):
-        top = group // col_groups * GROUP_ROWS
-        left = group % col_groups * cols
-        cond_ref[top : top + GROUP_ROWS, left : left + cols] = big_ref[group].astype(F32)
+    seq = seq_ref[0]
+    for back_y in range(near):
+        for back_x in range(far):
+            place_x = lax.rem(seq // near - back_x + far, far)
+            place_y = lax.rem(lax.rem(seq, near) - back_y + near, near)
+            group = place_x * near + place_y
+            top = pl.multiple_of(group // col_groups * GROUP_ROWS, GROUP_ROWS)
+            left = pl.multiple_of(lax.rem(group, col_groups) * cols, 128)
+            piece = big_refs[back_y][back_x].astype(F32)
+            cond_ref[pl.ds(top, GROUP_ROWS), pl.ds(left, cols)] = piece
     pieces = width // 128
     for head in range(heads):
-        packed = small_ref[head].astype(F32)
+        packed = tail_ref[head].astype(F32)
         target = in_ref if 2 * head < LAT else out_ref
         begin = 2 * head % LAT
         for piece in range(pieces):
-            row, lane = 2 * (piece % 8), 128 * (piece // 8)
-            target[begin : begin + 2, piece * 128 : (piece + 1) * 128] = packed[
-                row : row + 2, lane : lane + 128
-            ]
+            row = 2 * (piece % 8) + GROUP_ROWS * (piece // 8)
+            target[begin : begin + 2, piece * 128 : (piece + 1) * 128] = packed[row : row + 2]
         if head < pieces:
-            row, lane = 2 * (pieces % 8), 128 * (pieces // 8)
+            row = 2 * (pieces % 8) + GROUP_ROWS * (pieces // 8)
             cut = slice(head * 128, (head + 1) * 128)
-            time_ref[:, cut] = packed[row : row + 1, lane : lane + 128]
-            gain_ref[:, cut] = packed[row + 1 : row + 2, lane : lane + 128]
+            time_ref[cut] = packed[row]
+            gain_ref[cut] = packed[row + 1]
+
+
+def write_gradients(seq, big, returned, each, width):
+    heads = returned.shape[0]
+    return pl.pallas_call(
+        spread_kernel,
+        grid=(1,),
+        in_specs=[
+            pl.BlockSpec(memory_space=pltpu.SMEM),
+            *[vmem()] * len(big),
+            pl.BlockSpec((heads, TAIL, HD), lambda i: (0, each // TAIL, 0)),
+        ],
+        out_specs=[vmem()] * 5,
+        out_shape=[
+            jax.ShapeDtypeStruct((HD, width), F32),
+            jax.ShapeDtypeStruct((LAT, width), F32),
+            jax.ShapeDtypeStruct((width,), F32),
+            jax.ShapeDtypeStruct((width,), F32),
+            jax.ShapeDtypeStruct((LAT, width), F32),
+        ],
+        compiler_params=params(),
+        name="write_gradients",
+    )(seq, *big, returned)
 
 
 def call(kernel, out_shape, scratch, name, *operands, unread=0):
@@ -318,6 +382,21 @@
     )(*operands)
 
 
+def shifted(value, groups, stride, radix, step):
+    pairs = []
+    for source in range(groups):
+        digit = source // stride % radix
+        pairs.append((source, source + ((digit + step) % radix - digit) * stride))
+    return lax.ppermute(value, "seq", pairs)
+
+
+def gather_over_clips(piece, groups):
+    far = groups // CHIPS_Y
+    over_x = [piece] + [shifted(piece, groups, CHIPS_Y, far, k) for k in range(1, far)]
+    column = jnp.stack(over_x)
+    return [column] + [shifted(column, groups, 1, CHIPS_Y, k) for k in range(1, CHIPS_Y)]
+
+
 def exchange(value, axis):
     return lax.all_to_all(value, axis, split_axis=0, concat_axis=0, tiled=True)
 
@@ -334,9 +413,8 @@
     share = masked_index.shape[1] // heads
     count = DRAWS * SLOT
 
-    stacked = jnp.stack([queries, key_rows, value_rows])
-    stacked = jnp.transpose(stacked.reshape(3, each, heads, HD), (2, 0, 1, 3))
-    arrived = exchange(stacked, "head")
+    stacked = stack_by_head(queries, key_rows, value_rows, heads)
+    arrived = in_vmem(exchange(stacked, "head"))
 
     chosen = masked_index[0]
     live = lax.dynamic_index_in_dim(masked_counts, lax.axis_index("seq"), 0, keepdims=False)
@@ -377,7 +455,13 @@
     out_hi, out_lo = two_parts(out_wide)
     noise = jnp.pad(noise, ((0, 0), (0, 128 - LAT)))
 
-    part, picked = attend_masked(arrived, where, where_rank, rank_row, w_cond)
+    prepared = (
+        base, norm_gain.reshape(1, width), out_hi, out_lo, out_hi.T, out_lo.T, noise,
+        row_weight, feats,
+    )
+    part, picked = attend_masked(
+        arrived, where, where_rank, rank_row, w_cond, (*prepared, rank_column)
+    )
     half = heads // 2
     got_cond = exchange(part, "head")
     first_half = attend_some(arrived, rank_column, rank_row, 0, half, part)
@@ -387,8 +471,7 @@
         jax.ShapeDtypeStruct((heads, SLOT, width + EXTRA), BF16),
         [pltpu.VMEM((SLOT, width + EXTRA), F32)],
         "diffusion_head",
-        got_cond, base, norm_gain.reshape(1, width), out_hi, out_lo, out_hi.T, out_lo.T,
-        noise, row_weight, feats, first_half,
+        in_vmem(got_cond), *prepared, first_half,
         unread=1,
     )
     got_grad = exchange(send, "head")
@@ -401,41 +484,18 @@
         jax.ShapeDtypeStruct((groups, GROUP_ROWS, cols + PACK), BF16),
         [pltpu.VMEM((GROUP_ROWS, PACK), F32)],
         "cond_weight_grad",
-        got_grad, picked, attended,
+        in_vmem(got_grad), picked, attended,
         unread=1,
     )
     got_parts = exchange(parts, "seq")
-    returned = exchange(attended, "head")
-    big, small = call(
-        total_kernel,
-        [
-            jax.ShapeDtypeStruct((groups, GROUP_ROWS, cols), BF16),
-            jax.ShapeDtypeStruct((heads, GROUP_ROWS, PACK), BF16),
-        ],
-        [],
-        "sum_over_clips",
-        got_parts,
-    )
-    all_big = exchange(big, "seq")
-    all_small = exchange(small, "head")
-    cond_whole, in_grad, time_grad, gain_grad, out_grad = call(
-        spread_kernel,
-        [
-            jax.ShapeDtypeStruct((HD, width), F32),
-            jax.ShapeDtypeStruct((LAT, width), F32),
-            jax.ShapeDtypeStruct((1, width), F32),
-            jax.ShapeDtypeStruct((1, width), F32),
-            jax.ShapeDtypeStruct((LAT, width), F32),
-        ],
-        [],
-        "write_gradients",
-        all_big, all_small,
-    )
-    attended_rows = jnp.transpose(returned, (1, 0, 2)).reshape(each, heads * HD)
-    return (
-        attended_rows, cond_whole, in_grad, time_grad.reshape(width),
-        gain_grad.reshape(width), out_grad.T,
-    )
+    big, message = total_over_clips(in_vmem(got_parts), attended, each)
+    returned = exchange(message, "head")
+    all_big = gather_over_clips(big, groups)
+    cond_whole, in_grad, time_grad, gain_grad, out_grad = write_gradients(
+        lax.axis_index("seq").reshape(1), all_big, returned, each, width
+    )
+    rows = jnp.transpose(returned[:, :each], (1, 0, 2)).reshape(each, heads * HD)
+    return (rows, cond_whole, in_grad, time_grad, gain_grad, out_grad.T)
 
 
 def solution(mesh):

time: 260 us -> 240 us (0.923)
  waiting for transfers between devices: 84 us -> 35.7 us
  starting transfers between devices: 37.1 us -> 66.7 us
  local copies, waits for them, and re-layouts: 27.2 us -> 53.3 us
  blocking collectives: 40.8 us -> 26.5 us
  Pallas kernels: 56.8 us -> 46.7 us
    all_to_all x5 -> x4, waiting for transfers between devices: 84 us -> 29.2 us  [exchange(): return lax.all_to_all(value, axis, split_axis=0, concat_axis=0, tiled=True)]
    ppermute x0 -> x10, starting transfers between devices: none -> 36.8 us  [shifted(): return lax.ppermute(value, 'seq', pairs)]
    unnamed x39 -> x74, local copies, waits for them, and re-layouts: 9.1 us -> 29.7 us
    all_to_all x2 -> x1, blocking collectives: 40.8 us -> 26.5 us  [exchange(): return lax.all_to_all(value, axis, split_axis=0, concat_axis=0, tiled=True)]
    all_to_all x5 -> x4, starting transfers between devices: 37.1 us -> 29.9 us  [exchange(): return lax.all_to_all(value, axis, split_axis=0, concat_axis=0, tiled=True)]
    ppermute x0 -> x10, waiting for transfers between devices: none -> 6.52 us  [shifted(): return lax.ppermute(value, 'seq', pairs)]
    pallas_call x4 -> x2, Pallas kernels: 10.3 us -> 3.93 us  [call(): pl.pallas_call(kernel, in_specs=specs, out_specs=[vmem()] * len(out_shape...]
    pallas_call x3 -> x6, Pallas kernels: 46.5 us -> 42.7 us  [the longest x2 36.7 us: attend_some(): pl.pallas_call(functools.partial(attend_kernel, first), grid=(count,), in...]
  transfers between devices with their start and end apart: 5 -> 14, of which waited for: 4 -> 5; matrix products, arithmetic and copies ran while one was open for 10% -> 15% of each run, Pallas kernels for 16% -> 15%
where the time goes in v2:
time: 240 us; the launch traced here: 238 us
  starting transfers between devices  66.7 us (28%)
  local copies, waits for them, and re-layouts  53.3 us (22%)
  Pallas kernels  46.7 us (19%)
  waiting for transfers between devices  35.7 us (15%)
  blocking collectives  26.5 us (11%)
  other arithmetic  6.12 us (3%)
    ppermute x10, starting transfers between devices, shifted(): return lax.ppermute(value, 'seq', pairs)  36.8 us
    pallas_call x2, Pallas kernels, attend_some(): pl.pallas_call(functools.partial(attend_kernel, first), grid=(count,), in...  36.7 us
    all_to_all x4, starting transfers between devices, exchange(): return lax.all_to_all(value, axis, split_axis=0, concat_axis=0, tiled=True)  29.9 us
    unnamed x74, local copies, waits for them, and re-layouts  29.7 us
    all_to_all x4, waiting for transfers between devices, exchange(): return lax.all_to_all(value, axis, split_axis=0, concat_axis=0, tiled=True)  29.2 us
    all_to_all x1, blocking collectives, exchange(): return lax.all_to_all(value, axis, split_axis=0, concat_axis=0, tiled=True)  26.5 us
    ppermute x10, waiting for transfers between devices, shifted(): return lax.ppermute(value, 'seq', pairs)  6.52 us
  transfers between devices with their start and end apart: 14, of which 5 were waited for; matrix products, arithmetic and copies ran while one was open for 15% of the time, Pallas kernels for 15%

profile of v2, /device:TPU:6, one launch (start us, length us, event | category | flops | bytes accessed | tf_op | source)
XLA Modules:
  0.0 238.1 jit_solution(2652930941893096128)
XLA Ops:
  6.5 10.6 %all-to-all-start = ((bf16[16,3,224,128]{3,2,1,0:T(8,128)(2,1)}), bf16[16,3,224,128]{3,2,1,0:T(8,128)(2,1)S(1)}, u32[]{:S(2)}, u32[]{:S(2)}) async-start(bf16[16,3,224,128]{3,2,1,0:T(8,128)(2,1)} %copy-done.4), calls=%async_computation | async-start | bytes 5505024 | tf_op jit(solution)/shard_map/all_to_all | solution.py:401
  32.4 3.0 %reshape_squeeze.5.rest_9_.qrank_ref = s32[16,224,1]{2,1,0:T(8,128)} reshape(s32[3584]{0:T(1024)S(1)} %reduce.1) | data formatting | bytes 28672 | tf_op jit(solution)/shard_map/reshape;squeeze | solution.py:432
  52.2 28.2 %all-to-all-done.got_ref = bf16[16,3,224,128]{3,2,1,0:T(8,128)(2,1)S(1)} async-done(((bf16[16,3,224,128]{3,2,1,0:T(8,128)(2,1)}), bf16[16,3,224,128]{3,2,1,0:T(8,128)(2,1)S(1)}, u32[]{:S(2)}, u32[]{:S(2)}) %all-to-all-start) | async-done | bytes 2752544 | tf_op jit(solution)/shard_map/all_to_all | solution.py:401
  89.1 3.4 %masked_rows.1 = (bf16[16,16,1536]{2,1,0:T(8,128)(2,1)S(1)}, bf16[256,128]{1,0:T(8,128)(2,1)S(1)}) custom-call(bf16[16,3,224,128]{3,2,1,0:T(8,128)(2,1)S(1)} %all-to-all-done.got_ref, s32[256,1]{1,0:T(8,128)S(1)} %reshape.175.where_ref, s32[256,1]{1,0:T(8,128)S(1)} %reshape.176.qrank_ref, s32[1,3584]{1,0:T(1,128)S(1)} %copy-done.23, ...), custom_call_target="tpu_custom_call" | custom-call | tf_op jit(solution)/shard_map/masked_rows/pallas_call | solution.py:135
  94.0 4.7 %all-to-all-start.1 = ((bf16[16,16,1536]{2,1,0:T(8,128)(2,1)}), bf16[16,16,1536]{2,1,0:T(8,128)(2,1)}, u32[]{:S(2)}, u32[]{:S(2)}) async-start(bf16[16,16,1536]{2,1,0:T(8,128)(2,1)} %copy-done.15), calls=%async_computation.1 | async-start | bytes 1572864 | tf_op jit(solution)/shard_map/all_to_all | solution.py:401
  101.3 18.3 %attention.2.after_ref.rest_1_ = bf16[16,256,128]{2,1,0:T(8,128)(2,1)} custom-call(bf16[16,3,224,128]{3,2,1,0:T(8,128)(2,1)S(1)} %all-to-all-done.got_ref, s32[16,224,1]{2,1,0:T(8,128)S(1)} %copy-done.2, s32[1,3584]{1,0:T(1,128)S(1)} %copy-done.23, bf16[16,16,1536]{2,1,0:T(8,128)(2,1)S(1)} %copy-done.16), custom_call_target="tpu_custom_call" | custom-call | tf_op jit(solution)/shard_map/attention/pallas_call | solution.py:180
  123.7 2.5 %diffusion_head.1.rest_0_ = bf16[16,16,1664]{2,1,0:T(8,128)(2,1)S(1)} custom-call(bf16[16,16,1536]{2,1,0:T(8,128)(2,1)} %all-to-all-done.1.cond_ref, f32[64,1536]{1,0:T(8,128)S(1)} %copy-done.14, f32[1,1536]{1,0:T(1,128)S(1)} %copy-done.29, bf16[1536,128]{1,0:T(8,128)(2,1)S(1)} %copy-done.8, bf16[1536,128]{1,0:T(8,128)(2,1)S(1)} %copy-done.12, ...), custom_call_target="tpu_custom_call" | custom-call | tf_op jit(solution)/shard_map/diffusion_head/pallas_call | solution.py:374
  127.0 7.2 %all-to-all-start.2 = ((bf16[16,16,1664]{2,1,0:T(8,128)(2,1)}), bf16[16,16,1664]{2,1,0:T(8,128)(2,1)}, u32[]{:S(2)}, u32[]{:S(2)}) async-start(bf16[16,16,1664]{2,1,0:T(8,128)(2,1)} %copy-done.5), calls=%async_computation.2 | async-start | bytes 1703936 | tf_op jit(solution)/shard_map/all_to_all | solution.py:401
  136.9 18.3 %attention.3.after_ref.attended_ref = bf16[16,256,128]{2,1,0:T(8,128)(2,1)} custom-call(bf16[16,3,224,128]{3,2,1,0:T(8,128)(2,1)S(1)} %all-to-all-done.got_ref, s32[16,224,1]{2,1,0:T(8,128)S(1)} %copy-done.3, s32[1,3584]{1,0:T(1,128)S(1)} %copy-done.23, bf16[16,16,1664]{2,1,0:T(8,128)(2,1)S(1)} %copy-done.6, ...), custom_call_target="tpu_custom_call", output_to_operand_aliasing={{}: (4, {})} | custom-call | tf_op jit(solution)/shard_map/attention/pallas_call | solution.py:180
  157.7 26.5 %all_to_all.25.got_ref = bf16[32,16,640]{2,1,0:T(8,128)(2,1)S(1)} all-to-all(bf16[32,16,640]{2,1,0:T(8,128)(2,1)S(1)} %cond_weight_grad.1), channel_id=1, replica_groups=mesh['seq'=32,'head'=16] {'seq'}, dimensions={0} | all-to-all | bytes 1310720 | tf_op jit(solution)/shard_map/all_to_all | solution.py:401
  185.0 7.4 %all-to-all-start.4 = ((bf16[16,256,128]{2,1,0:T(8,128)(2,1)}), bf16[16,256,128]{2,1,0:T(8,128)(2,1)S(1)}, u32[]{:S(2)}, u32[]{:S(2)}) async-start(bf16[16,256,128]{2,1,0:T(8,128)(2,1)} %get-tuple-element.17), calls=%async_computation.4 | async-start | bytes 2097152 | tf_op jit(solution)/shard_map/all_to_all | solution.py:401
  192.4 4.4 %collective-permute-start = (bf16[16,384]{1,0:T(8,128)(2,1)S(1)}, bf16[16,384]{1,0:T(8,128)(2,1)S(1)}, u32[]{:S(2)}, u32[]{:S(2)}) collective-permute-start(bf16[16,384]{1,0:T(8,128)(2,1)S(1)} %get-tuple-element.18), channel_id=1, source_target_pairs={{0,128},{16,144},{32,160},{48,176},{64,192},{80,208},{96,224},{112... | collective-permute-start | bytes 36872 | tf_op jit(solution)/shard_map/ppermute | solution.py:390
  196.8 2.3 collective-permute-start.1
  199.1 2.4 %collective-permute-start.2 = (bf16[16,384]{1,0:T(8,128)(2,1)S(1)}, bf16[16,384]{1,0:T(8,128)(2,1)S(1)}, u32[]{:S(2)}, u32[]{:S(2)}) collective-permute-start(bf16[16,384]{1,0:T(8,128)(2,1)S(1)} %get-tuple-element.18), channel_id=1, source_target_pairs={{0,384},{16,400},{32,416},{48,432},{64,448},{80,464},{96,480},{112... | collective-permute-start | bytes 36872 | tf_op jit(solution)/shard_map/ppermute | solution.py:390
  201.6 2.3 collective-permute-done.1
  203.9 2.0 collective-permute-done.2
  205.9 4.9 %collective-permute-start.3 = (bf16[4,16,384]{2,1,0:T(8,128)(2,1)S(1)}, bf16[4,16,384]{2,1,0:T(8,128)(2,1)S(1)}, u32[]{:S(2)}, u32[]{:S(2)}) collective-permute-start(bf16[4,16,384]{2,1,0:T(8,128)(2,1)S(1)} %pad_maximum_fusion.refs_0_), channel_id=1, source_target_pairs={{0,16},{16,32},{32,48},{48,64},{64,80},{80,96},{96,112},{112,0},{1... | collective-permute-start | bytes 147464 | tf_op jit(solution)/shard_map/ppermute | solution.py:390
  210.9 3.0 %collective-permute-start.4 = (bf16[4,16,384]{2,1,0:T(8,128)(2,1)S(1)}, bf16[4,16,384]{2,1,0:T(8,128)(2,1)S(1)}, u32[]{:S(2)}, u32[]{:S(2)}) collective-permute-start(bf16[4,16,384]{2,1,0:T(8,128)(2,1)S(1)} %pad_maximum_fusion.refs_0_), channel_id=1, source_target_pairs={{0,32},{16,48},{32,64},{48,80},{64,96},{80,112},{96,0},{112,16},{1... | collective-permute-start | bytes 147464 | tf_op jit(solution)/shard_map/ppermute | solution.py:390
  213.8 3.6 %collective-permute-start.5 = (bf16[4,16,384]{2,1,0:T(8,128)(2,1)S(1)}, bf16[4,16,384]{2,1,0:T(8,128)(2,1)S(1)}, u32[]{:S(2)}, u32[]{:S(2)}) collective-permute-start(bf16[4,16,384]{2,1,0:T(8,128)(2,1)S(1)} %pad_maximum_fusion.refs_0_), channel_id=1, source_target_pairs={{0,48},{16,64},{32,80},{48,96},{64,112},{80,0},{96,16},{112,32},{1... | collective-permute-start | bytes 147464 | tf_op jit(solution)/shard_map/ppermute | solution.py:390
  217.5 5.7 %collective-permute-start.6 = (bf16[4,16,384]{2,1,0:T(8,128)(2,1)S(1)}, bf16[4,16,384]{2,1,0:T(8,128)(2,1)S(1)}, u32[]{:S(2)}, u32[]{:S(2)}) collective-permute-start(bf16[4,16,384]{2,1,0:T(8,128)(2,1)S(1)} %pad_maximum_fusion.refs_0_), channel_id=1, source_target_pairs={{0,64},{16,80},{32,96},{48,112},{64,0},{80,16},{96,32},{112,48},{1... | collective-permute-start | bytes 147464 | tf_op jit(solution)/shard_map/ppermute | solution.py:390
  223.1 3.8 %collective-permute-start.7 = (bf16[4,16,384]{2,1,0:T(8,128)(2,1)S(1)}, bf16[4,16,384]{2,1,0:T(8,128)(2,1)S(1)}, u32[]{:S(2)}, u32[]{:S(2)}) collective-permute-start(bf16[4,16,384]{2,1,0:T(8,128)(2,1)S(1)} %pad_maximum_fusion.refs_0_), channel_id=1, source_target_pairs={{0,80},{16,96},{32,112},{48,0},{64,16},{80,32},{96,48},{112,64},{1... | collective-permute-start | bytes 147464 | tf_op jit(solution)/shard_map/ppermute | solution.py:390
  227.0 3.9 %collective-permute-start.8 = (bf16[4,16,384]{2,1,0:T(8,128)(2,1)S(1)}, bf16[4,16,384]{2,1,0:T(8,128)(2,1)S(1)}, u32[]{:S(2)}, u32[]{:S(2)}) collective-permute-start(bf16[4,16,384]{2,1,0:T(8,128)(2,1)S(1)} %pad_maximum_fusion.refs_0_), channel_id=1, source_target_pairs={{0,96},{16,112},{32,0},{48,16},{64,32},{80,48},{96,64},{112,80},{1... | collective-permute-start | bytes 147464 | tf_op jit(solution)/shard_map/ppermute | solution.py:390
  230.9 2.7 %collective-permute-start.9 = (bf16[4,16,384]{2,1,0:T(8,128)(2,1)S(1)}, bf16[4,16,384]{2,1,0:T(8,128)(2,1)S(1)}, u32[]{:S(2)}, u32[]{:S(2)}) collective-permute-start(bf16[4,16,384]{2,1,0:T(8,128)(2,1)S(1)} %pad_maximum_fusion.refs_0_), channel_id=1, source_target_pairs={{0,112},{16,0},{32,16},{48,32},{64,48},{80,64},{96,80},{112,96},{1... | collective-permute-start | bytes 147464 | tf_op jit(solution)/shard_map/ppermute | solution.py:390
  234.7 2.2 collective-permute-done.9.refs_7_
  (136 shorter events, 63.6 us)
Async XLA Ops:
  0.6 49.5 %copy-start = (f32[16,1536]{1,0:T(8,128)S(1)}, f32[16,1536]{1,0:T(8,128)}, u32[]{:S(2)}) copy-start(f32[16,1536]{1,0:T(8,128)} %param.24) | copy-start | bytes 294916
  6.5 11.9 %copy-start.32 = (bf16[3584,4]{0,1:T(4,128)(2,1)S(1)}, bf16[3584,4]{0,1:T(4,128)(2,1)}, u32[]{:S(2)}) copy-start(bf16[3584,4]{0,1:T(4,128)(2,1)} %param.22) | copy-start | bytes 86020
  6.5 16.5 %copy-start.31 = (bf16[3584,16]{0,1:T(8,128)(2,1)S(1)}, bf16[3584,16]{0,1:T(8,128)(2,1)}, u32[]{:S(2)}) copy-start(bf16[3584,16]{0,1:T(8,128)(2,1)} %param.20) | copy-start | bytes 344068
  6.5 19.7 %copy-start.30 = (bf16[3584,64]{0,1:T(8,128)(2,1)S(1)}, bf16[3584,64]{0,1:T(8,128)(2,1)}, u32[]{:S(2)}) copy-start(bf16[3584,64]{0,1:T(8,128)(2,1)} %param.21) | copy-start | bytes 1376260
  6.5 73.9 %all-to-all-start = ((bf16[16,3,224,128]{3,2,1,0:T(8,128)(2,1)}), bf16[16,3,224,128]{3,2,1,0:T(8,128)(2,1)S(1)}, u32[]{:S(2)}, u32[]{:S(2)}) async-start(bf16[16,3,224,128]{3,2,1,0:T(8,128)(2,1)} %copy-done.4), calls=%async_computation | async-start | bytes 5505024 | tf_op jit(solution)/shard_map/all_to_all | solution.py:401
  17.1 13.9 %copy-start.34 = (s32[32]{0:T(128)S(1)}, s32[32]{0:T(128)}, u32[]{:S(2)}) copy-start(s32[32]{0:T(128)} %param.19) | copy-start | bytes 388
  17.1 15.3 %copy-start.23 = (s32[1,3584]{1,0:T(1,128)S(1)}, s32[1,3584]{1,0:T(1,128)}, u32[]{:S(2)}) copy-start(s32[1,3584]{1,0:T(1,128)} %rank_ref.5) | copy-start | bytes 43012
  94.0 25.7 %all-to-all-start.1 = ((bf16[16,16,1536]{2,1,0:T(8,128)(2,1)}), bf16[16,16,1536]{2,1,0:T(8,128)(2,1)}, u32[]{:S(2)}, u32[]{:S(2)}) async-start(bf16[16,16,1536]{2,1,0:T(8,128)(2,1)} %copy-done.15), calls=%async_computation.1 | async-start | bytes 1572864 | tf_op jit(solution)/shard_map/all_to_all | solution.py:401
  101.3 18.3 %copy-start.22 = (f32[64,128]{1,0:T(8,128)S(1)}, f32[64,128]{1,0:T(8,128)}, u32[]{:S(2)}) copy-start(f32[64,128]{1,0:T(8,128)} %pad.33.rest_6_.noise_ref) | copy-start | bytes 98308
  101.3 18.3 %copy-start.25 = (bf16[64,64]{1,0:T(8,128)(2,1)S(1)}, bf16[64,64]{1,0:T(8,128)(2,1)}, u32[]{:S(2)}) copy-start(bf16[64,64]{1,0:T(8,128)(2,1)} %pad_maximum_fusion.1.rest_8_.feat_ref) | copy-start | bytes 24580
  101.3 18.4 %copy-start.29 = (f32[1,1536]{1,0:T(1,128)S(1)}, f32[1,1536]{1,0:T(1,128)}, u32[]{:S(2)}) copy-start(f32[1,1536]{1,0:T(1,128)} %reshape.139.rest_1_.gain_ref) | copy-start | bytes 18436
  127.0 29.2 %all-to-all-start.2 = ((bf16[16,16,1664]{2,1,0:T(8,128)(2,1)}), bf16[16,16,1664]{2,1,0:T(8,128)(2,1)}, u32[]{:S(2)}, u32[]{:S(2)}) async-start(bf16[16,16,1664]{2,1,0:T(8,128)(2,1)} %copy-done.5), calls=%async_computation.2 | async-start | bytes 1703936 | tf_op jit(solution)/shard_map/all_to_all | solution.py:401
  136.9 19.3 %copy-start.27 = (bf16[256,128]{1,0:T(8,128)(2,1)S(1)}, bf16[256,128]{1,0:T(8,128)(2,1)}, u32[]{:S(2)}) copy-start(bf16[256,128]{1,0:T(8,128)(2,1)} %copy-done.26) | copy-start | bytes 196612
  185.0 48.6 %all-to-all-start.4 = ((bf16[16,256,128]{2,1,0:T(8,128)(2,1)}), bf16[16,256,128]{2,1,0:T(8,128)(2,1)S(1)}, u32[]{:S(2)}, u32[]{:S(2)}) async-start(bf16[16,256,128]{2,1,0:T(8,128)(2,1)} %get-tuple-element.17), calls=%async_computation.4 | async-start | bytes 2097152 | tf_op jit(solution)/shard_map/all_to_all | solution.py:401
  192.4 9.2 %collective-permute-start = (bf16[16,384]{1,0:T(8,128)(2,1)S(1)}, bf16[16,384]{1,0:T(8,128)(2,1)S(1)}, u32[]{:S(2)}, u32[]{:S(2)}) collective-permute-start(bf16[16,384]{1,0:T(8,128)(2,1)S(1)} %get-tuple-element.18), channel_id=1, source_target_pairs={{0,128},{16,144},{32,160},{48,176},{64,192},{80,208},{96,224},{112... | collective-permute-start | bytes 36872 | tf_op jit(solution)/shard_map/ppermute | solution.py:390
  196.8 7.1 %collective-permute-start.1 = (bf16[16,384]{1,0:T(8,128)(2,1)S(1)}, bf16[16,384]{1,0:T(8,128)(2,1)S(1)}, u32[]{:S(2)}, u32[]{:S(2)}) collective-permute-start(bf16[16,384]{1,0:T(8,128)(2,1)S(1)} %get-tuple-element.18), channel_id=1, source_target_pairs={{0,256},{16,272},{32,288},{48,304},{64,320},{80,336},{96,352},{112... | collective-permute-start | bytes 36872 | tf_op jit(solution)/shard_map/ppermute | solution.py:390
  199.1 6.8 %collective-permute-start.2 = (bf16[16,384]{1,0:T(8,128)(2,1)S(1)}, bf16[16,384]{1,0:T(8,128)(2,1)S(1)}, u32[]{:S(2)}, u32[]{:S(2)}) collective-permute-start(bf16[16,384]{1,0:T(8,128)(2,1)S(1)} %get-tuple-element.18), channel_id=1, source_target_pairs={{0,384},{16,400},{32,416},{48,432},{64,448},{80,464},{96,480},{112... | collective-permute-start | bytes 36872 | tf_op jit(solution)/shard_map/ppermute | solution.py:390
  205.9 21.1 %collective-permute-start.3 = (bf16[4,16,384]{2,1,0:T(8,128)(2,1)S(1)}, bf16[4,16,384]{2,1,0:T(8,128)(2,1)S(1)}, u32[]{:S(2)}, u32[]{:S(2)}) collective-permute-start(bf16[4,16,384]{2,1,0:T(8,128)(2,1)S(1)} %pad_maximum_fusion.refs_0_), channel_id=1, source_target_pairs={{0,16},{16,32},{32,48},{48,64},{64,80},{80,96},{96,112},{112,0},{1... | collective-permute-start | bytes 147464 | tf_op jit(solution)/shard_map/ppermute | solution.py:390
  210.9 20.0 %collective-permute-start.4 = (bf16[4,16,384]{2,1,0:T(8,128)(2,1)S(1)}, bf16[4,16,384]{2,1,0:T(8,128)(2,1)S(1)}, u32[]{:S(2)}, u32[]{:S(2)}) collective-permute-start(bf16[4,16,384]{2,1,0:T(8,128)(2,1)S(1)} %pad_maximum_fusion.refs_0_), channel_id=1, source_target_pairs={{0,32},{16,48},{32,64},{48,80},{64,96},{80,112},{96,0},{112,16},{1... | collective-permute-start | bytes 147464 | tf_op jit(solution)/shard_map/ppermute | solution.py:390
  213.8 20.9 %collective-permute-start.5 = (bf16[4,16,384]{2,1,0:T(8,128)(2,1)S(1)}, bf16[4,16,384]{2,1,0:T(8,128)(2,1)S(1)}, u32[]{:S(2)}, u32[]{:S(2)}) collective-permute-start(bf16[4,16,384]{2,1,0:T(8,128)(2,1)S(1)} %pad_maximum_fusion.refs_0_), channel_id=1, source_target_pairs={{0,48},{16,64},{32,80},{48,96},{64,112},{80,0},{96,16},{112,32},{1... | collective-permute-start | bytes 147464 | tf_op jit(solution)/shard_map/ppermute | solution.py:390
  217.5 17.2 %collective-permute-start.6 = (bf16[4,16,384]{2,1,0:T(8,128)(2,1)S(1)}, bf16[4,16,384]{2,1,0:T(8,128)(2,1)S(1)}, u32[]{:S(2)}, u32[]{:S(2)}) collective-permute-start(bf16[4,16,384]{2,1,0:T(8,128)(2,1)S(1)} %pad_maximum_fusion.refs_0_), channel_id=1, source_target_pairs={{0,64},{16,80},{32,96},{48,112},{64,0},{80,16},{96,32},{112,48},{1... | collective-permute-start | bytes 147464 | tf_op jit(solution)/shard_map/ppermute | solution.py:390
  223.1 11.6 %collective-permute-start.7 = (bf16[4,16,384]{2,1,0:T(8,128)(2,1)S(1)}, bf16[4,16,384]{2,1,0:T(8,128)(2,1)S(1)}, u32[]{:S(2)}, u32[]{:S(2)}) collective-permute-start(bf16[4,16,384]{2,1,0:T(8,128)(2,1)S(1)} %pad_maximum_fusion.refs_0_), channel_id=1, source_target_pairs={{0,80},{16,96},{32,112},{48,0},{64,16},{80,32},{96,48},{112,64},{1... | collective-permute-start | bytes 147464 | tf_op jit(solution)/shard_map/ppermute | solution.py:390
  227.0 7.7 %collective-permute-start.8 = (bf16[4,16,384]{2,1,0:T(8,128)(2,1)S(1)}, bf16[4,16,384]{2,1,0:T(8,128)(2,1)S(1)}, u32[]{:S(2)}, u32[]{:S(2)}) collective-permute-start(bf16[4,16,384]{2,1,0:T(8,128)(2,1)S(1)} %pad_maximum_fusion.refs_0_), channel_id=1, source_target_pairs={{0,96},{16,112},{32,0},{48,16},{64,32},{80,48},{96,64},{112,80},{1... | collective-permute-start | bytes 147464 | tf_op jit(solution)/shard_map/ppermute | solution.py:390
  230.9 6.0 %collective-permute-start.9 = (bf16[4,16,384]{2,1,0:T(8,128)(2,1)S(1)}, bf16[4,16,384]{2,1,0:T(8,128)(2,1)S(1)}, u32[]{:S(2)}, u32[]{:S(2)}) collective-permute-start(bf16[4,16,384]{2,1,0:T(8,128)(2,1)S(1)} %pad_maximum_fusion.refs_0_), channel_id=1, source_target_pairs={{0,112},{16,0},{32,16},{48,32},{64,48},{80,64},{96,80},{112,96},{1... | collective-permute-start | bytes 147464 | tf_op jit(solution)/shard_map/ppermute | solution.py:390
  (25 other events, 36.5 us)

commit v3 on v2

--- a/solution.py
+++ b/solution.py
@@ -18,7 +18,7 @@
 PACK = 256
 TAIL = 32
 GROUP_ROWS = 16
-CHIPS_Y = 8
+STRIDES = (4, 16, 2, 8, 1)
 LOG2E = 1.4426950408889634
 F32 = jnp.float32
 BF16 = jnp.bfloat16
@@ -41,6 +41,14 @@
     return jnp.dot(a, b, preferred_element_type=F32)
 
 
+def dot_rows(a, b):
+    return lax.dot_general(a, b, (((1,), (1,)), ((), ())), preferred_element_type=F32)
+
+
+def dot_over_rows(a, b):
+    return lax.dot_general(a, b, (((0,), (0,)), ((), ())), preferred_element_type=F32)
+
+
 def two_parts(value):
     high = value.astype(BF16)
     return high, (value - high.astype(F32)).astype(BF16)
@@ -48,6 +56,10 @@
 
 def in_vmem(value):
     return pltpu.with_memory_space_constraint(value, pltpu.VMEM)
+
+
+def in_hbm(value):
+    return pltpu.with_memory_space_constraint(value, pltpu.HBM)
 
 
 def stack_kernel(q_ref, k_ref, v_ref, out_ref):
@@ -67,10 +79,10 @@
         grid=(4,),
         in_specs=[spec, spec, spec],
         out_specs=pl.BlockSpec((block, 3, each, HD), lambda i: (i, 0, 0, 0)),
-        out_shape=jax.ShapeDtypeStruct((heads, 3, each, HD), BF16),
+        out_shape=pltpu.HBM((heads, 3, each, HD), BF16),
         compiler_params=params(),
         name="stack_by_head",
-    )(queries, key_rows, value_rows)
+    )(in_hbm(queries), in_hbm(key_rows), in_hbm(value_rows))
 
 
 def load_keys(got_ref, key_scr, val_scr):
@@ -108,7 +120,9 @@
 
 
 def masked_kernel(got_ref, where_ref, qrank_ref, rank_ref, w_ref, *rest):
-    part_ref, picked_ref, key_scr, val_scr, score_scr = rest[-5:]
+    part_ref, picked_ref, key_scr, val_scr, score_scr, w_scr, sem = rest
+    fetch = pltpu.make_async_copy(w_ref, w_scr, sem)
+    fetch.start()
     load_keys(got_ref, key_scr, val_scr)
     slots = where_ref.shape[0]
     total = key_scr.shape[0]
@@ -123,31 +137,34 @@
     out = attend(query.astype(BF16), qrank_ref[...], rank_ref, key_scr, val_scr, score_scr)
     picked = jnp.where(qrank_ref[...] >= 0, out, 0.0).astype(BF16)
     picked_ref[...] = picked
-    part = dot(picked, w_ref[...]).astype(BF16)
+    fetch.wait()
+    part = dot(picked, w_scr[...]).astype(BF16)
     part_ref[...] = part.reshape(part_ref.shape)
 
 
-def attend_masked(arrived, where, where_rank, rank_row, w_cond, after):
+def attend_masked(arrived, where, where_rank, rank_row, w_cond):
     heads, _, each, _ = arrived.shape
     total = heads * each
     slots = where.shape[0]
     width = w_cond.shape[1]
     return pl.pallas_call(
         masked_kernel,
-        in_specs=[vmem()] * 5 + [anywhere()] * len(after),
+        in_specs=[vmem()] * 4 + [anywhere()],
         out_specs=[vmem(), vmem()],
         out_shape=[
-            jax.ShapeDtypeStruct((heads, slots // heads, width), BF16),
+            pltpu.HBM((heads, slots // heads, width), BF16),
             jax.ShapeDtypeStruct((slots, HD), BF16),
         ],
         scratch_shapes=[
             pltpu.VMEM((total, HD), BF16),
             pltpu.VMEM((total, 2 * HD), BF16),
             pltpu.VMEM((slots, total), F32),
+            pltpu.VMEM(w_cond.shape, BF16),
+            pltpu.SemaphoreType.DMA,
         ],
         compiler_params=params(),
         name="masked_rows",
-    )(arrived, where, where_rank, rank_row, w_cond, *after)
+    )(arrived, where, where_rank, rank_row, in_hbm(w_cond))
 
 
 def attend_kernel(first, got_ref, qrank_ref, rank_ref, *rest):
@@ -157,21 +174,24 @@
     def _():
         load_keys(got_ref, key_scr, val_scr)
 
-    query = got_ref[pl.program_id(0) + first, 0]
-    out = attend(query, qrank_ref[0], rank_ref, key_scr, val_scr, score_scr)
+    source = pl.program_id(0) + first
+    columns = qrank_ref[...]
+    lanes = lax.broadcasted_iota(jnp.int32, columns.shape, 1)
+    ranks = jnp.sum(jnp.where(lanes == source, columns, 0), axis=1, keepdims=True)
+    out = attend(got_ref[source, 0], ranks, rank_ref, key_scr, val_scr, score_scr)
     out_ref[0] = out.astype(BF16)
 
 
-def attend_some(arrived, rank_column, rank_row, first, count, after, earlier=None):
+def attend_some(arrived, rank_columns, rank_row, first, count, after, earlier=None):
     heads, _, each, _ = arrived.shape
     total = heads * each
     specs = [
         vmem(),
-        pl.BlockSpec((1, each, 1), lambda i: (i + first, 0, 0)),
+        vmem(),
         vmem(),
         anywhere(),
     ]
-    operands = [arrived, rank_column, rank_row, after]
+    operands = [arrived, rank_columns, rank_row, after]
     aliases = {}
     if earlier is not None:
         specs.append(anywhere())
@@ -195,8 +215,8 @@
 
 
 def head_kernel(
-    cond_ref, base_ref, gain_ref, outhi_ref, outlo_ref, outhi_t_ref, outlo_t_ref, noise_ref,
-    weight_ref, feat_ref, after_ref, send_ref, block_scr,
+    cond_ref, base_ref, gain_ref, out_t_ref, noise_ref, weight_ref, feat_ref, after_ref,
+    send_ref, token_ref, block_scr,
 ):
     heads, rows, width = cond_ref.shape
     count = base_ref.shape[0]
@@ -211,12 +231,13 @@
     gate = 1.0 / (1.0 + jnp.exp(-scaled))
     active = scaled * gate
     act_hi, act_lo = two_parts(active)
-    both = dot(jnp.concatenate([act_hi, act_lo], axis=0), outhi_ref[...])
-    predicted = both[:count] + both[count:] + dot(act_hi, outlo_ref[...])
+    out_hi, out_lo = two_parts(out_t_ref[...])
+    both = dot_rows(jnp.concatenate([act_hi, act_lo], axis=0), out_hi)
+    predicted = both[:count] + both[count:] + dot_rows(act_hi, out_lo)
     pred_grad = (predicted - noise_ref[...]) * weight_ref[...]
     pg_hi, pg_lo = two_parts(pred_grad)
-    both = dot(jnp.concatenate([pg_hi, pg_lo], axis=0), outhi_t_ref[...])
-    act_grad = both[:count] + both[count:] + dot(pg_hi, outlo_t_ref[...])
+    both = dot(jnp.concatenate([pg_hi, pg_lo], axis=0), out_hi)
+    act_grad = both[:count] + both[count:] + dot(pg_hi, out_lo)
     scaled_grad = act_grad * gate * (1.0 + scaled * (1.0 - gate))
     gain_grad = jnp.sum(scaled_grad * unit, axis=0, keepdims=True)
     unit_grad = scaled_grad * gain
@@ -227,10 +248,9 @@
     half = feats.shape[0] // 2
     both = dot(feats, hg_hi)
     feat_grad = both[:half] + both[half:] + dot(feats[:half], hg_lo)
-    turned = jnp.transpose(pred_grad)[:LAT]
-    tg_hi, tg_lo = two_parts(turned)
-    both = dot(jnp.concatenate([tg_hi, tg_lo], axis=0), act_hi)
-    out_grad = both[:LAT] + both[LAT:] + dot(tg_hi, act_lo)
+    out_grad = dot_over_rows(pg_hi, act_hi) + dot_over_rows(pg_lo, act_hi)
+    out_grad = out_grad + dot_over_rows(pg_hi, act_lo)
+    token_ref[...] = inverse[:8] + jnp.zeros(token_ref.shape, F32)
     cond_grad = hidden_grad[:rows]
     for draw in range(1, count // rows):
         cond_grad = cond_grad + hidden_grad[draw * rows : (draw + 1) * rows]
@@ -312,24 +332,20 @@
     )(got, attended)
 
 
-def spread_kernel(seq_ref, *refs):
-    big_refs = refs[:-6]
-    tail_ref, cond_ref, in_ref, time_ref, gain_ref, out_ref = refs[-6:]
-    far, rows, cols = big_refs[0].shape
-    near = len(big_refs)
+def spread_kernel(
+    strides, seq_ref, big_ref, tail_ref, cond_ref, in_ref, time_ref, gain_ref, out_ref
+):
+    groups, rows, cols = big_ref.shape
     heads = tail_ref.shape[0]
     width = cond_ref.shape[1]
     col_groups = width // cols
     seq = seq_ref[0]
-    for back_y in range(near):
-        for back_x in range(far):
-            place_x = lax.rem(seq // near - back_x + far, far)
-            place_y = lax.rem(lax.rem(seq, near) - back_y + near, near)
-            group = place_x * near + place_y
-            top = pl.multiple_of(group // col_groups * GROUP_ROWS, GROUP_ROWS)
-            left = pl.multiple_of(lax.rem(group, col_groups) * cols, 128)
-            piece = big_refs[back_y][back_x].astype(F32)
-            cond_ref[pl.ds(top, GROUP_ROWS), pl.ds(left, cols)] = piece
+    for place in range(groups):
+        apart = sum(stride for bit, stride in enumerate(strides) if place >> bit & 1)
+        group = seq ^ apart
+        top = pl.multiple_of(group // col_groups * GROUP_ROWS, GROUP_ROWS)
+        left = pl.multiple_of(lax.rem(group, col_groups) * cols, 128)
+        cond_ref[pl.ds(top, GROUP_ROWS), pl.ds(left, cols)] = big_ref[place].astype(F32)
     pieces = width // 128
     for head in range(heads):
         packed = tail_ref[head].astype(F32)
@@ -345,14 +361,14 @@
             gain_ref[cut] = packed[row + 1]
 
 
-def write_gradients(seq, big, returned, each, width):
+def write_gradients(seq, big, strides, returned, each, width):
     heads = returned.shape[0]
     return pl.pallas_call(
-        spread_kernel,
+        functools.partial(spread_kernel, strides),
         grid=(1,),
         in_specs=[
             pl.BlockSpec(memory_space=pltpu.SMEM),
-            *[vmem()] * len(big),
+            vmem(),
             pl.BlockSpec((heads, TAIL, HD), lambda i: (0, each // TAIL, 0)),
         ],
         out_specs=[vmem()] * 5,
@@ -365,7 +381,7 @@
         ],
         compiler_params=params(),
         name="write_gradients",
-    )(seq, *big, returned)
+    )(seq, big, returned)
 
 
 def call(kernel, out_shape, scratch, name, *operands, unread=0):
@@ -382,19 +398,15 @@
     )(*operands)
 
 
-def shifted(value, groups, stride, radix, step):
-    pairs = []
-    for source in range(groups):
-        digit = source // stride % radix
-        pairs.append((source, source + ((digit + step) % radix - digit) * stride))
-    return lax.ppermute(value, "seq", pairs)
-
-
 def gather_over_clips(piece, groups):
-    far = groups // CHIPS_Y
-    over_x = [piece] + [shifted(piece, groups, CHIPS_Y, far, k) for k in range(1, far)]
-    column = jnp.stack(over_x)
-    return [column] + [shifted(column, groups, 1, CHIPS_Y, k) for k in range(1, CHIPS_Y)]
+    held = piece[None]
+    strides = []
+    for stride in STRIDES:
+        if stride < groups:
+            pairs = [(source, source ^ stride) for source in range(groups)]
+            held = jnp.concatenate([held, lax.ppermute(held, "seq", pairs)])
+            strides.append(stride)
+    return held, strides
 
 
 def exchange(value, axis):
@@ -429,7 +441,7 @@
     where_rank = in_slots(jnp.where(alive, jnp.take(ranks, chosen), -1), -1)
     where_rank = where_rank.reshape(heads * SLOT, 1)
     rank_row = ranks.reshape(1, total)
-    rank_column = ranks.reshape(heads, each, 1)
+    rank_columns = jnp.pad(ranks.reshape(heads, each).T, ((0, 0), (0, 128 - heads)))
 
     mine = lax.dynamic_index_in_dim(
         in_slots(chosen, 0), lax.axis_index("head"), 0, keepdims=False
@@ -451,31 +463,29 @@
     row_weight = jnp.tile(my_alive * (2.0 * loss_scale), DRAWS).reshape(count, 1)
     feats = jnp.pad(jnp.concatenate([noisy, times], axis=1), ((0, 0), (0, 15))).T
     feats = jnp.concatenate(two_parts(feats), axis=0)
-    out_wide = jnp.pad(w_out, ((0, 0), (0, 128 - LAT)))
-    out_hi, out_lo = two_parts(out_wide)
-    noise = jnp.pad(noise, ((0, 0), (0, 128 - LAT)))
-
-    prepared = (
-        base, norm_gain.reshape(1, width), out_hi, out_lo, out_hi.T, out_lo.T, noise,
-        row_weight, feats,
-    )
-    part, picked = attend_masked(
-        arrived, where, where_rank, rank_row, w_cond, (*prepared, rank_column)
-    )
+
+    where_rank, rank_columns, base, noise, row_weight, feats = lax.optimization_barrier(
+        (where_rank, rank_columns, base, noise, row_weight, feats)
+    )
+    part, picked = attend_masked(arrived, where, where_rank, rank_row, w_cond)
     half = heads // 2
     got_cond = exchange(part, "head")
-    first_half = attend_some(arrived, rank_column, rank_row, 0, half, part)
-
-    send = call(
+    first_half = attend_some(arrived, rank_columns, rank_row, 0, half, picked)
+
+    send, token = call(
         head_kernel,
-        jax.ShapeDtypeStruct((heads, SLOT, width + EXTRA), BF16),
+        [
+            pltpu.HBM((heads, SLOT, width + EXTRA), BF16),
+            jax.ShapeDtypeStruct((8, 128), F32),
+        ],
         [pltpu.VMEM((SLOT, width + EXTRA), F32)],
         "diffusion_head",
-        in_vmem(got_cond), *prepared, first_half,
+        in_vmem(got_cond), base, norm_gain.reshape(1, width), w_out.T, noise, row_weight,
+        feats, first_half,
         unread=1,
     )
     got_grad = exchange(send, "head")
-    attended = attend_some(arrived, rank_column, rank_row, half, half, send, first_half)
+    attended = attend_some(arrived, rank_columns, rank_row, half, half, token, first_half)
 
     col_groups = groups // (HD // GROUP_ROWS)
     cols = width // col_groups
@@ -490,9 +500,9 @@
     got_parts = exchange(parts, "seq")
     big, message = total_over_clips(in_vmem(got_parts), attended, each)
     returned = exchange(message, "head")
-    all_big = gather_over_clips(big, groups)
+    all_big, strides = gather_over_clips(big, groups)
     cond_whole, in_grad, time_grad, gain_grad, out_grad = write_gradients(
-        lax.axis_index("seq").reshape(1), all_big, returned, each, width
+        lax.axis_index("seq").reshape(1), all_big, strides, returned, each, width
     )
     rows = jnp.transpose(returned[:, :each], (1, 0, 2)).reshape(each, heads * HD)
     return (rows, cond_whole, in_grad, time_grad, gain_grad, out_grad.T)

time: 240 us -> 224 us (0.933)
  local copies, waits for them, and re-layouts: 53.3 us -> 24.1 us
  waiting for transfers between devices: 35.7 us -> 64 us
  starting transfers between devices: 66.7 us -> 47.9 us
  Pallas kernels: 46.7 us -> 53.1 us
  other arithmetic: 6.12 us -> 2.88 us
    unnamed x74 -> x32, local copies, waits for them, and re-layouts: 29.7 us -> 8.63 us
    ppermute x10 -> x5, starting transfers between devices: 36.8 us -> 18.6 us  [gather_over_clips(): held = jnp.concatenate([held, lax.ppermute(held, 'seq', pairs)])]
    all_to_all x4, waiting for transfers between devices: 29.2 us -> 44.7 us  [exchange(): return lax.all_to_all(value, axis, split_axis=0, concat_axis=0, tiled=True)]
    ppermute x10 -> x5, waiting for transfers between devices: 6.52 us -> 19.2 us  [gather_over_clips(): held = jnp.concatenate([held, lax.ppermute(held, 'seq', pairs)])]
    convert_element_type x2 -> x0, local copies, waits for them, and re-layouts: 3.85 us -> none  [the longest x1 1.93 us: two_parts(): high = value.astype(BF16)]
    pallas_call x1, Pallas kernels: 0.76 us -> 4.28 us  [stack_by_head(): pl.pallas_call(stack_kernel, grid=(4,), in_specs=[spec, spec, spec], out_...]
    another operation x1 -> x2, local copies, waits for them, and re-layouts: 2.95 us -> 0.17 us  [local(): ranks.reshape(heads, each)]
  transfers between devices with their start and end apart: 14 -> 9, of which waited for: 5 -> 8; matrix products, arithmetic and copies ran while one was open for 15% -> 11% of each run, Pallas kernels for 15% -> 17%
where the time goes in v3:
time: 224 us; the launch traced here: 221 us
  waiting for transfers between devices  64 us (29%)
  Pallas kernels  53.1 us (24%)
  starting transfers between devices  47.9 us (21%)
  blocking collectives  26.5 us (12%)
  local copies, waits for them, and re-layouts  24.1 us (11%)
  other arithmetic  2.88 us (1%)
    all_to_all x4, waiting for transfers between devices, exchange(): return lax.all_to_all(value, axis, split_axis=0, concat_axis=0, tiled=True)  44.7 us
    pallas_call x2, Pallas kernels, attend_some(): pl.pallas_call(functools.partial(attend_kernel, first), grid=(count,), in...  36.7 us
    all_to_all x4, starting transfers between devices, exchange(): return lax.all_to_all(value, axis, split_axis=0, concat_axis=0, tiled=True)  29.3 us
    all_to_all x1, blocking collectives, exchange(): return lax.all_to_all(value, axis, split_axis=0, concat_axis=0, tiled=True)  26.5 us
    ppermute x5, waiting for transfers between devices, gather_over_clips(): held = jnp.concatenate([held, lax.ppermute(held, 'seq', pairs)])  19.2 us
    ppermute x5, starting transfers between devices, gather_over_clips(): held = jnp.concatenate([held, lax.ppermute(held, 'seq', pairs)])  18.6 us
    unnamed x32, local copies, waits for them, and re-layouts  8.63 us
    pallas_call x1, Pallas kernels, attend_masked(): pl.pallas_call(masked_kernel, in_specs=[vmem()] * 4 + [anywhere()], out_s...  5.09 us
  transfers between devices with their start and end apart: 9, of which 8 were waited for; matrix products, arithmetic and copies ran while one was open for 11% of the time, Pallas kernels for 17%

profile of v3, /device:TPU:6, one launch (start us, length us, event | category | flops | bytes accessed | tf_op | source)
XLA Modules:
  0.0 220.6 jit_solution(5546540742688322662)
XLA Ops:
  0.6 4.3 %stack_by_head.1 = bf16[16,3,224,128]{3,2,1,0:T(8,128)(2,1)} custom-call(bf16[224,2048]{1,0:T(8,128)(2,1)} %q_ref.1, bf16[224,2048]{1,0:T(8,128)(2,1)} %k_ref.1, bf16[224,2048]{1,0:T(8,128)(2,1)} %v_ref.1), custom_call_target="tpu_custom_call" | custom-call | tf_op jit(solution)/shard_map/stack_by_head/pallas_call | solution.py:77
  5.0 10.6 %all-to-all-start = ((bf16[16,3,224,128]{3,2,1,0:T(8,128)(2,1)}), bf16[16,3,224,128]{3,2,1,0:T(8,128)(2,1)S(1)}, u32[]{:S(2)}, u32[]{:S(2)}) async-start(bf16[16,3,224,128]{3,2,1,0:T(8,128)(2,1)} %stack_by_head.1), calls=%async_computation | async-start | bytes 5505024 | tf_op jit(solution)/shard_map/all_to_all | solution.py:413
  18.1 1.9 gather_fusion.1
  28.2 2.3 %copy.53 = bf16[3584,64]{1,0:T(8,128)(2,1)} copy(bf16[3584,64]{0,1:T(8,128)(2,1)} %param.21) | data formatting | bytes 917504 | tf_op args[7]
  38.0 40.9 %all-to-all-done.got_ref = bf16[16,3,224,128]{3,2,1,0:T(8,128)(2,1)S(1)} async-done(((bf16[16,3,224,128]{3,2,1,0:T(8,128)(2,1)}), bf16[16,3,224,128]{3,2,1,0:T(8,128)(2,1)S(1)}, u32[]{:S(2)}, u32[]{:S(2)}) %all-to-all-start) | async-done | bytes 2752544 | tf_op jit(solution)/shard_map/all_to_all | solution.py:413
  80.5 5.1 %masked_rows.1 = (bf16[16,16,1536]{2,1,0:T(8,128)(2,1)}, bf16[256,128]{1,0:T(8,128)(2,1)S(1)}) custom-call(bf16[16,3,224,128]{3,2,1,0:T(8,128)(2,1)S(1)} %all-to-all-done.got_ref, s32[256,1]{1,0:T(8,128)S(1)} %reshape.175.where_ref, s32[256,1]{1,0:T(8,128)S(1)} %copy-done.1, s32[1,3584]{1,0:T(1,128)S(1)} %copy-done.3, bf16[128,1536]{1,0:T(8,128)(2,1)} %w_ref.1), custom_call_target="tpu_custom_call" | custom-call | tf_op jit(solution)/shard_map/masked_rows/pallas_call | solution.py:150
  85.6 4.7 %all-to-all-start.1 = ((bf16[16,16,1536]{2,1,0:T(8,128)(2,1)}), bf16[16,16,1536]{2,1,0:T(8,128)(2,1)}, u32[]{:S(2)}, u32[]{:S(2)}) async-start(bf16[16,16,1536]{2,1,0:T(8,128)(2,1)} %get-tuple-element.24), calls=%async_computation.1 | async-start | bytes 1572864 | tf_op jit(solution)/shard_map/all_to_all | solution.py:413
  92.5 18.3 %attention.2.after_ref.rest_1_ = bf16[16,256,128]{2,1,0:T(8,128)(2,1)} custom-call(bf16[16,3,224,128]{3,2,1,0:T(8,128)(2,1)S(1)} %all-to-all-done.got_ref, s32[224,128]{1,0:T(8,128)S(1)} %pad.27.qrank_ref, s32[1,3584]{1,0:T(1,128)S(1)} %copy-done.4, bf16[256,128]{1,0:T(8,128)(2,1)S(1)} %get-tuple-element.30.rest_0_.picked_ref), custom_call_target="tpu_custom_call" | custom-call | tf_op jit(solution)/shard_map/attention/pallas_call | solution.py:200
  112.0 3.6 %diffusion_head.1 = (bf16[16,16,1664]{2,1,0:T(8,128)(2,1)}, f32[8,128]{1,0:T(8,128)S(1)}) custom-call(bf16[16,16,1536]{2,1,0:T(8,128)(2,1)} %all-to-all-done.1.cond_ref, f32[64,1536]{1,0:T(8,128)S(1)} %convolution_add_fusion.base_ref, f32[1,1536]{1,0:T(1,128)S(1)} %reshape.140.gain_ref, f32[16,1536]{1,0:T(8,128)S(1)} %bitcast.53, f32[64,16]{1,0:T(8,128)S(1)} %bitcast.52, ...), custom_call_target="tpu_custom_call" | custom-call | tf_op jit(solution)/shard_map/diffusion_head/pallas_call | solution.py:390
  115.5 7.0 %all-to-all-start.2 = ((bf16[16,16,1664]{2,1,0:T(8,128)(2,1)}), bf16[16,16,1664]{2,1,0:T(8,128)(2,1)}, u32[]{:S(2)}, u32[]{:S(2)}) async-start(bf16[16,16,1664]{2,1,0:T(8,128)(2,1)} %get-tuple-element.31), calls=%async_computation.2 | async-start | bytes 1703936 | tf_op jit(solution)/shard_map/all_to_all | solution.py:413
  122.5 18.4 %attention.3.after_ref.attended_ref = bf16[16,256,128]{2,1,0:T(8,128)(2,1)} custom-call(bf16[16,3,224,128]{3,2,1,0:T(8,128)(2,1)S(1)} %all-to-all-done.got_ref, s32[224,128]{1,0:T(8,128)S(1)} %pad.27.qrank_ref, s32[1,3584]{1,0:T(1,128)S(1)} %copy-done.4, f32[8,128]{1,0:T(8,128)S(1)} %get-tuple-element.32.rest_0_, ...), custom_call_target="tpu_custom_call", output_to_operand_aliasing={{}: (4, {})} | custom-call | tf_op jit(solution)/shard_map/attention/pallas_call | solution.py:200
  140.9 3.6 %all-to-all-done.2.got_ref = bf16[16,16,1664]{2,1,0:T(8,128)(2,1)} async-done(((bf16[16,16,1664]{2,1,0:T(8,128)(2,1)}), bf16[16,16,1664]{2,1,0:T(8,128)(2,1)}, u32[]{:S(2)}, u32[]{:S(2)}) %all-to-all-start.2) | async-done | bytes 852000 | tf_op jit(solution)/shard_map/all_to_all | solution.py:413
  146.0 26.5 %all_to_all.25.got_ref = bf16[32,16,640]{2,1,0:T(8,128)(2,1)S(1)} all-to-all(bf16[32,16,640]{2,1,0:T(8,128)(2,1)S(1)} %cond_weight_grad.1), channel_id=1, replica_groups=mesh['seq'=32,'head'=16] {'seq'}, dimensions={0} | all-to-all | bytes 1310720 | tf_op jit(solution)/shard_map/all_to_all | solution.py:413
  173.3 7.0 %all-to-all-start.4 = ((bf16[16,256,128]{2,1,0:T(8,128)(2,1)}), bf16[16,256,128]{2,1,0:T(8,128)(2,1)S(1)}, u32[]{:S(2)}, u32[]{:S(2)}) async-start(bf16[16,256,128]{2,1,0:T(8,128)(2,1)} %get-tuple-element.33), calls=%async_computation.4 | async-start | bytes 2097152 | tf_op jit(solution)/shard_map/all_to_all | solution.py:413
  180.3 4.1 %collective-permute-start = (bf16[1,16,384]{2,1,0:T(8,128)(2,1)S(1)}, bf16[1,16,384]{2,1,0:T(8,128)(2,1)S(1)}, u32[]{:S(2)}, u32[]{:S(2)}) collective-permute-start(bf16[1,16,384]{2,1,0:T(8,128)(2,1)S(1)} %bitcast.48), channel_id=1, source_target_pairs={{0,64},{16,80},{32,96},{48,112},{64,0},{80,16},{96,32},{112,48},{1... | collective-permute-start | bytes 36872 | tf_op jit(solution)/shard_map/ppermute | solution.py:407
  184.5 5.4 %collective-permute-done = bf16[1,16,384]{2,1,0:T(8,128)(2,1)S(1)} collective-permute-done((bf16[1,16,384]{2,1,0:T(8,128)(2,1)S(1)}, bf16[1,16,384]{2,1,0:T(8,128)(2,1)S(1)}, u32[]{:S(2)}, u32[]{:S(2)}) %collective-permute-start) | collective-permute-done | bytes 12320 | tf_op jit(solution)/shard_map/ppermute | solution.py:407
  189.8 3.4 %collective-permute-start.1 = (bf16[2,16,384]{2,1,0:T(8,128)(2,1)S(1)}, bf16[2,16,384]{2,1,0:T(8,128)(2,1)S(1)}, u32[]{:S(2)}, u32[]{:S(2)}) collective-permute-start(bf16[2,16,384]{2,1,0:T(8,128)(2,1)S(1)} %pad_maximum_fusion.2), channel_id=1, source_target_pairs={{0,256},{16,272},{32,288},{48,304},{64,320},{80,336},{96,352},{112... | collective-permute-start | bytes 73736 | tf_op jit(solution)/shard_map/ppermute | solution.py:407
  193.2 3.8 %collective-permute-done.1 = bf16[2,16,384]{2,1,0:T(8,128)(2,1)S(1)} collective-permute-done((bf16[2,16,384]{2,1,0:T(8,128)(2,1)S(1)}, bf16[2,16,384]{2,1,0:T(8,128)(2,1)S(1)}, u32[]{:S(2)}, u32[]{:S(2)}) %collective-permute-start.1) | collective-permute-done | bytes 24608 | tf_op jit(solution)/shard_map/ppermute | solution.py:407
  197.1 4.3 %collective-permute-start.2 = (bf16[4,16,384]{2,1,0:T(8,128)(2,1)S(1)}, bf16[4,16,384]{2,1,0:T(8,128)(2,1)S(1)}, u32[]{:S(2)}, u32[]{:S(2)}) collective-permute-start(bf16[4,16,384]{2,1,0:T(8,128)(2,1)S(1)} %pad_maximum_fusion.1), channel_id=1, source_target_pairs={{0,32},{16,48},{32,0},{48,16},{64,96},{80,112},{96,64},{112,80},{1... | collective-permute-start | bytes 147464 | tf_op jit(solution)/shard_map/ppermute | solution.py:407
  201.4 2.6 %collective-permute-done.2 = bf16[4,16,384]{2,1,0:T(8,128)(2,1)S(1)} collective-permute-done((bf16[4,16,384]{2,1,0:T(8,128)(2,1)S(1)}, bf16[4,16,384]{2,1,0:T(8,128)(2,1)S(1)}, u32[]{:S(2)}, u32[]{:S(2)}) %collective-permute-start.2) | collective-permute-done | bytes 49184 | tf_op jit(solution)/shard_map/ppermute | solution.py:407
  204.0 2.6 %collective-permute-start.3 = (bf16[8,16,384]{2,1,0:T(8,128)(2,1)S(1)}, bf16[8,16,384]{2,1,0:T(8,128)(2,1)S(1)}, u32[]{:S(2)}, u32[]{:S(2)}) collective-permute-start(bf16[8,16,384]{2,1,0:T(8,128)(2,1)S(1)} %pad_maximum_fusion), channel_id=1, source_target_pairs={{0,128},{16,144},{32,160},{48,176},{64,192},{80,208},{96,224},{112... | collective-permute-start | bytes 294920 | tf_op jit(solution)/shard_map/ppermute | solution.py:407
  206.6 3.8 %collective-permute-done.3 = bf16[8,16,384]{2,1,0:T(8,128)(2,1)S(1)} collective-permute-done((bf16[8,16,384]{2,1,0:T(8,128)(2,1)S(1)}, bf16[8,16,384]{2,1,0:T(8,128)(2,1)S(1)}, u32[]{:S(2)}, u32[]{:S(2)}) %collective-permute-start.3) | collective-permute-done | bytes 98336 | tf_op jit(solution)/shard_map/ppermute | solution.py:407
  210.5 4.2 %collective-permute-start.4 = (bf16[16,16,384]{2,1,0:T(8,128)(2,1)S(1)}, bf16[16,16,384]{2,1,0:T(8,128)(2,1)S(1)}, u32[]{:S(2)}, u32[]{:S(2)}) collective-permute-start(bf16[16,16,384]{2,1,0:T(8,128)(2,1)S(1)} %get-tuple-element.40), channel_id=1, source_target_pairs={{0,16},{16,0},{32,48},{48,32},{64,80},{80,64},{96,112},{112,96},{1... | collective-permute-start | bytes 589832 | tf_op jit(solution)/shard_map/ppermute | solution.py:407
  214.7 3.6 %collective-permute-done.4 = bf16[16,16,384]{2,1,0:T(8,128)(2,1)S(1)} collective-permute-done((bf16[16,16,384]{2,1,0:T(8,128)(2,1)S(1)}, bf16[16,16,384]{2,1,0:T(8,128)(2,1)S(1)}, u32[]{:S(2)}, u32[]{:S(2)}) %collective-permute-start.4) | collective-permute-done | bytes 196640 | tf_op jit(solution)/shard_map/ppermute | solution.py:407
  (86 shorter events, 27.7 us)
Async XLA Ops:
  0.6 34.6 %copy-start = (f32[16,1536]{1,0:T(8,128)S(1)}, f32[16,1536]{1,0:T(8,128)}, u32[]{:S(2)}) copy-start(f32[16,1536]{1,0:T(8,128)} %param.24) | copy-start | bytes 294916
  4.9 11.1 %copy-start.10 = (s32[1,224]{1,0:T(1,128)S(1)}, s32[1,224]{1,0:T(1,128)}, u32[]{:S(2)}) copy-start(s32[1,224]{1,0:T(1,128)} %param.18) | copy-start | bytes 2692
  4.9 11.9 %copy-start.9 = (bf16[3584,4]{0,1:T(4,128)(2,1)S(1)}, bf16[3584,4]{0,1:T(4,128)(2,1)}, u32[]{:S(2)}) copy-start(bf16[3584,4]{0,1:T(4,128)(2,1)} %param.22) | copy-start | bytes 86020
  4.9 15.9 %copy-start.2 = (s32[1,3584]{1,0:T(1,128)S(1)}, s32[1,3584]{1,0:T(1,128)}, u32[]{:S(2)}) copy-start(s32[1,3584]{1,0:T(1,128)} %rank_ref.5) | copy-start | bytes 43012
  4.9 17.8 %copy-start.11 = (s32[32]{0:T(128)S(1)}, s32[32]{0:T(128)}, u32[]{:S(2)}) copy-start(s32[32]{0:T(128)} %param.19) | copy-start | bytes 388
  5.0 73.9 %all-to-all-start = ((bf16[16,3,224,128]{3,2,1,0:T(8,128)(2,1)}), bf16[16,3,224,128]{3,2,1,0:T(8,128)(2,1)S(1)}, u32[]{:S(2)}, u32[]{:S(2)}) async-start(bf16[16,3,224,128]{3,2,1,0:T(8,128)(2,1)} %stack_by_head.1), calls=%async_computation | async-start | bytes 5505024 | tf_op jit(solution)/shard_map/all_to_all | solution.py:413
  15.5 9.4 %copy-start.8 = (bf16[3584,16]{0,1:T(8,128)(2,1)S(1)}, bf16[3584,16]{0,1:T(8,128)(2,1)}, u32[]{:S(2)}) copy-start(bf16[3584,16]{0,1:T(8,128)(2,1)} %param.20) | copy-start | bytes 344068
  78.9 0.9 copy-start.1
  79.8 0.7 copy-start.3
  85.6 25.5 %copy-start.5 = (f32[4,16,16]{2,1,0:T(8,128)S(1)}, f32[4,16,16]{2,1,0:T(8,128)}, u32[]{:S(2)}) copy-start(f32[4,16,16]{2,1,0:T(8,128)} %copy.55) | copy-start | bytes 12292
  85.6 25.5 %copy-start.7 = (bf16[64,64]{1,0:T(8,128)(2,1)S(1)}, bf16[64,64]{1,0:T(8,128)(2,1)}, u32[]{:S(2)}) copy-start(bf16[64,64]{1,0:T(8,128)(2,1)} %pad_maximum_fusion.3.feat_ref) | copy-start | bytes 24580
  85.6 25.5 %all-to-all-start.1 = ((bf16[16,16,1536]{2,1,0:T(8,128)(2,1)}), bf16[16,16,1536]{2,1,0:T(8,128)(2,1)}, u32[]{:S(2)}, u32[]{:S(2)}) async-start(bf16[16,16,1536]{2,1,0:T(8,128)(2,1)} %get-tuple-element.24), calls=%async_computation.1 | async-start | bytes 1572864 | tf_op jit(solution)/shard_map/all_to_all | solution.py:413
  91.8 0.7 copy-start.4
  111.1 0.9 copy-start.6
  115.5 28.9 %all-to-all-start.2 = ((bf16[16,16,1664]{2,1,0:T(8,128)(2,1)}), bf16[16,16,1664]{2,1,0:T(8,128)(2,1)}, u32[]{:S(2)}, u32[]{:S(2)}) async-start(bf16[16,16,1664]{2,1,0:T(8,128)(2,1)} %get-tuple-element.31), calls=%async_computation.2 | async-start | bytes 1703936 | tf_op jit(solution)/shard_map/all_to_all | solution.py:413
  173.3 45.1 %all-to-all-start.4 = ((bf16[16,256,128]{2,1,0:T(8,128)(2,1)}), bf16[16,256,128]{2,1,0:T(8,128)(2,1)S(1)}, u32[]{:S(2)}, u32[]{:S(2)}) async-start(bf16[16,256,128]{2,1,0:T(8,128)(2,1)} %get-tuple-element.33), calls=%async_computation.4 | async-start | bytes 2097152 | tf_op jit(solution)/shard_map/all_to_all | solution.py:413
  180.3 9.5 %collective-permute-start = (bf16[1,16,384]{2,1,0:T(8,128)(2,1)S(1)}, bf16[1,16,384]{2,1,0:T(8,128)(2,1)S(1)}, u32[]{:S(2)}, u32[]{:S(2)}) collective-permute-start(bf16[1,16,384]{2,1,0:T(8,128)(2,1)S(1)} %bitcast.48), channel_id=1, source_target_pairs={{0,64},{16,80},{32,96},{48,112},{64,0},{80,16},{96,32},{112,48},{1... | collective-permute-start | bytes 36872 | tf_op jit(solution)/shard_map/ppermute | solution.py:407
  189.8 7.2 %collective-permute-start.1 = (bf16[2,16,384]{2,1,0:T(8,128)(2,1)S(1)}, bf16[2,16,384]{2,1,0:T(8,128)(2,1)S(1)}, u32[]{:S(2)}, u32[]{:S(2)}) collective-permute-start(bf16[2,16,384]{2,1,0:T(8,128)(2,1)S(1)} %pad_maximum_fusion.2), channel_id=1, source_target_pairs={{0,256},{16,272},{32,288},{48,304},{64,320},{80,336},{96,352},{112... | collective-permute-start | bytes 73736 | tf_op jit(solution)/shard_map/ppermute | solution.py:407
  197.1 6.9 %collective-permute-start.2 = (bf16[4,16,384]{2,1,0:T(8,128)(2,1)S(1)}, bf16[4,16,384]{2,1,0:T(8,128)(2,1)S(1)}, u32[]{:S(2)}, u32[]{:S(2)}) collective-permute-start(bf16[4,16,384]{2,1,0:T(8,128)(2,1)S(1)} %pad_maximum_fusion.1), channel_id=1, source_target_pairs={{0,32},{16,48},{32,0},{48,16},{64,96},{80,112},{96,64},{112,80},{1... | collective-permute-start | bytes 147464 | tf_op jit(solution)/shard_map/ppermute | solution.py:407
  204.0 6.5 %collective-permute-start.3 = (bf16[8,16,384]{2,1,0:T(8,128)(2,1)S(1)}, bf16[8,16,384]{2,1,0:T(8,128)(2,1)S(1)}, u32[]{:S(2)}, u32[]{:S(2)}) collective-permute-start(bf16[8,16,384]{2,1,0:T(8,128)(2,1)S(1)} %pad_maximum_fusion), channel_id=1, source_target_pairs={{0,128},{16,144},{32,160},{48,176},{64,192},{80,208},{96,224},{112... | collective-permute-start | bytes 294920 | tf_op jit(solution)/shard_map/ppermute | solution.py:407
  210.5 7.8 %collective-permute-start.4 = (bf16[16,16,384]{2,1,0:T(8,128)(2,1)S(1)}, bf16[16,16,384]{2,1,0:T(8,128)(2,1)S(1)}, u32[]{:S(2)}, u32[]{:S(2)}) collective-permute-start(bf16[16,16,384]{2,1,0:T(8,128)(2,1)S(1)} %get-tuple-element.40), channel_id=1, source_target_pairs={{0,16},{16,0},{32,48},{48,32},{64,80},{80,64},{96,112},{112,96},{1... | collective-permute-start | bytes 589832 | tf_op jit(solution)/shard_map/ppermute | solution.py:407

commit v4 on v3

--- a/solution.py
+++ b/solution.py
@@ -18,7 +18,6 @@
 PACK = 256
 TAIL = 32
 GROUP_ROWS = 16
-STRIDES = (4, 16, 2, 8, 1)
 LOG2E = 1.4426950408889634
 F32 = jnp.float32
 BF16 = jnp.bfloat16
@@ -72,13 +71,13 @@
 
 def stack_by_head(queries, key_rows, value_rows, heads):
     each = queries.shape[0]
-    block = heads // 4
-    spec = pl.BlockSpec((each, block * HD), lambda i: (0, i))
+    block = each // 2
+    spec = pl.BlockSpec((block, heads * HD), lambda i: (i, 0))
     return pl.pallas_call(
         stack_kernel,
-        grid=(4,),
+        grid=(2,),
         in_specs=[spec, spec, spec],
-        out_specs=pl.BlockSpec((block, 3, each, HD), lambda i: (i, 0, 0, 0)),
+        out_specs=pl.BlockSpec((heads, 3, block, HD), lambda i: (0, 0, i, 0)),
         out_shape=pltpu.HBM((heads, 3, each, HD), BF16),
         compiler_params=params(),
         name="stack_by_head",
@@ -119,37 +118,39 @@
     return total_out[:, :HD] / total_out[:, HD:]
 
 
-def masked_kernel(got_ref, where_ref, qrank_ref, rank_ref, w_ref, *rest):
+def masked_kernel(got_ref, slot_ref, rank_ref, w_ref, *rest):
     part_ref, picked_ref, key_scr, val_scr, score_scr, w_scr, sem = rest
     fetch = pltpu.make_async_copy(w_ref, w_scr, sem)
     fetch.start()
     load_keys(got_ref, key_scr, val_scr)
-    slots = where_ref.shape[0]
+    slots = slot_ref.shape[0]
+    where = slot_ref[:, 0:1]
+    slot_rank = slot_ref[:, 1:2]
     total = key_scr.shape[0]
     sources, _, each, _ = got_ref.shape
     query = jnp.zeros((slots, HD), F32)
     step = math.gcd(each * sources, each * 4)
     for start in range(0, total, step):
         lanes = lax.broadcasted_iota(jnp.int32, (slots, step), 1) + start
-        hit = jnp.where(lanes == where_ref[...], 1.0, 0.0).astype(BF16)
+        hit = jnp.where(lanes == where, 1.0, 0.0).astype(BF16)
         rows = got_ref[start // each : (start + step) // each, 0].reshape(step, HD)
         query = query + dot(hit, rows)
-    out = attend(query.astype(BF16), qrank_ref[...], rank_ref, key_scr, val_scr, score_scr)
-    picked = jnp.where(qrank_ref[...] >= 0, out, 0.0).astype(BF16)
+    out = attend(query.astype(BF16), slot_rank, rank_ref, key_scr, val_scr, score_scr)
+    picked = jnp.where(slot_rank >= 0, out, 0.0).astype(BF16)
     picked_ref[...] = picked
     fetch.wait()
     part = dot(picked, w_scr[...]).astype(BF16)
     part_ref[...] = part.reshape(part_ref.shape)
 
 
-def attend_masked(arrived, where, where_rank, rank_row, w_cond):
+def attend_masked(arrived, slot_columns, rank_row, w_cond):
     heads, _, each, _ = arrived.shape
     total = heads * each
-    slots = where.shape[0]
+    slots = slot_columns.shape[0]
     width = w_cond.shape[1]
     return pl.pallas_call(
         masked_kernel,
-        in_specs=[vmem()] * 4 + [anywhere()],
+        in_specs=[vmem()] * 3 + [anywhere()],
         out_specs=[vmem(), vmem()],
         out_shape=[
             pltpu.HBM((heads, slots // heads, width), BF16),
@@ -164,7 +165,7 @@
         ],
         compiler_params=params(),
         name="masked_rows",
-    )(arrived, where, where_rank, rank_row, in_hbm(w_cond))
+    )(arrived, slot_columns, rank_row, in_hbm(w_cond))
 
 
 def attend_kernel(first, got_ref, qrank_ref, rank_ref, *rest):
@@ -215,14 +216,17 @@
 
 
 def head_kernel(
-    cond_ref, base_ref, gain_ref, out_t_ref, noise_ref, weight_ref, feat_ref, after_ref,
-    send_ref, token_ref, block_scr,
+    cond_ref, gain_ref, out_t_ref, noise_ref, feat_ref, base_hbm, after_ref,
+    send_ref, token_ref, block_scr, base_ref, sem,
 ):
+    fetch = pltpu.make_async_copy(base_hbm, base_ref, sem)
+    fetch.start()
     heads, rows, width = cond_ref.shape
     count = base_ref.shape[0]
     condition = cond_ref[0].astype(F32)
     for source in range(1, heads):
         condition = condition + cond_ref[source].astype(F32)
+    fetch.wait()
     hidden = base_ref[...] + jnp.concatenate([condition] * (count // rows), axis=0)
     inverse = lax.rsqrt(jnp.mean(hidden * hidden, axis=1, keepdims=True) + NORM_EPS)
     unit = hidden * inverse
@@ -234,7 +238,7 @@
     out_hi, out_lo = two_parts(out_t_ref[...])
     both = dot_rows(jnp.concatenate([act_hi, act_lo], axis=0), out_hi)
     predicted = both[:count] + both[count:] + dot_rows(act_hi, out_lo)
-    pred_grad = (predicted - noise_ref[...]) * weight_ref[...]
+    pred_grad = (predicted - noise_ref[:, :LAT]) * noise_ref[:, LAT : LAT + 1]
     pg_hi, pg_lo = two_parts(pred_grad)
     both = dot(jnp.concatenate([pg_hi, pg_lo], axis=0), out_hi)
     act_grad = both[:count] + both[count:] + dot(pg_hi, out_lo)
@@ -332,20 +336,15 @@
     )(got, attended)
 
 
-def spread_kernel(
-    strides, seq_ref, big_ref, tail_ref, cond_ref, in_ref, time_ref, gain_ref, out_ref
-):
+def spread_kernel(big_ref, tail_ref, cond_ref, in_ref, time_ref, gain_ref, out_ref):
     groups, rows, cols = big_ref.shape
     heads = tail_ref.shape[0]
     width = cond_ref.shape[1]
     col_groups = width // cols
-    seq = seq_ref[0]
-    for place in range(groups):
-        apart = sum(stride for bit, stride in enumerate(strides) if place >> bit & 1)
-        group = seq ^ apart
-        top = pl.multiple_of(group // col_groups * GROUP_ROWS, GROUP_ROWS)
-        left = pl.multiple_of(lax.rem(group, col_groups) * cols, 128)
-        cond_ref[pl.ds(top, GROUP_ROWS), pl.ds(left, cols)] = big_ref[place].astype(F32)
+    for group in range(groups):
+        top = group // col_groups * GROUP_ROWS
+        left = group % col_groups * cols
+        cond_ref[top : top + GROUP_ROWS, left : left + cols] = big_ref[group].astype(F32)
     pieces = width // 128
     for head in range(heads):
         packed = tail_ref[head].astype(F32)
@@ -361,13 +360,12 @@
             gain_ref[cut] = packed[row + 1]
 
 
-def write_gradients(seq, big, strides, returned, each, width):
+def write_gradients(big, returned, each, width):
     heads = returned.shape[0]
     return pl.pallas_call(
-        functools.partial(spread_kernel, strides),
+        spread_kernel,
         grid=(1,),
         in_specs=[
-            pl.BlockSpec(memory_space=pltpu.SMEM),
             vmem(),
             pl.BlockSpec((heads, TAIL, HD), lambda i: (0, each // TAIL, 0)),
         ],
@@ -381,11 +379,11 @@
         ],
         compiler_params=params(),
         name="write_gradients",
-    )(seq, big, returned)
-
-
-def call(kernel, out_shape, scratch, name, *operands, unread=0):
-    specs = [vmem()] * (len(operands) - unread) + [anywhere()] * unread
+    )(big, returned)
+
+
+def call(kernel, out_shape, scratch, name, *operands, outside=0):
+    specs = [vmem()] * (len(operands) - outside) + [anywhere()] * outside
     many = isinstance(out_shape, list)
     return pl.pallas_call(
         kernel,
@@ -396,17 +394,6 @@
         compiler_params=params(),
         name=name,
     )(*operands)
-
-
-def gather_over_clips(piece, groups):
-    held = piece[None]
-    strides = []
-    for stride in STRIDES:
-        if stride < groups:
-            pairs = [(source, source ^ stride) for source in range(groups)]
-            held = jnp.concatenate([held, lax.ppermute(held, "seq", pairs)])
-            strides.append(stride)
-    return held, strides
 
 
 def exchange(value, axis):
@@ -437,9 +424,9 @@
         value = value.reshape(heads, share)
         return jnp.pad(value, ((0, 0), (0, SLOT - share)), constant_values=fill)
 
-    where = in_slots(jnp.where(alive, chosen, -1), -1).reshape(heads * SLOT, 1)
+    where = in_slots(jnp.where(alive, chosen, -1), -1).reshape(heads * SLOT)
     where_rank = in_slots(jnp.where(alive, jnp.take(ranks, chosen), -1), -1)
-    where_rank = where_rank.reshape(heads * SLOT, 1)
+    slot_columns = jnp.stack([where, where_rank.reshape(heads * SLOT)], axis=1)
     rank_row = ranks.reshape(1, total)
     rank_columns = jnp.pad(ranks.reshape(heads, each).T, ((0, 0), (0, 128 - heads)))
 
@@ -464,10 +451,12 @@
     feats = jnp.pad(jnp.concatenate([noisy, times], axis=1), ((0, 0), (0, 15))).T
     feats = jnp.concatenate(two_parts(feats), axis=0)
 
-    where_rank, rank_columns, base, noise, row_weight, feats = lax.optimization_barrier(
-        (where_rank, rank_columns, base, noise, row_weight, feats)
-    )
-    part, picked = attend_masked(arrived, where, where_rank, rank_row, w_cond)
+    gain = norm_gain.reshape(1, width)
+    noise = jnp.concatenate([noise, row_weight], axis=1)
+    slot_columns, rank_columns, base, gain, noise, feats = lax.optimization_barrier(
+        (slot_columns, rank_columns, base, gain, noise, feats)
+    )
+    part, picked = attend_masked(arrived, slot_columns, rank_row, w_cond)
     half = heads // 2
     got_cond = exchange(part, "head")
     first_half = attend_some(arrived, rank_columns, rank_row, 0, half, picked)
@@ -478,11 +467,14 @@
             pltpu.HBM((heads, SLOT, width + EXTRA), BF16),
             jax.ShapeDtypeStruct((8, 128), F32),
         ],
-        [pltpu.VMEM((SLOT, width + EXTRA), F32)],
+        [
+            pltpu.VMEM((SLOT, width + EXTRA), F32),
+            pltpu.VMEM(base.shape, F32),
+            pltpu.SemaphoreType.DMA,
+        ],
         "diffusion_head",
-        in_vmem(got_cond), base, norm_gain.reshape(1, width), w_out.T, noise, row_weight,
-        feats, first_half,
-        unread=1,
+        in_vmem(got_cond), gain, w_out.T, noise, feats, in_hbm(base), first_half,
+        outside=2,
     )
     got_grad = exchange(send, "head")
     attended = attend_some(arrived, rank_columns, rank_row, half, half, token, first_half)
@@ -495,14 +487,14 @@
         [pltpu.VMEM((GROUP_ROWS, PACK), F32)],
         "cond_weight_grad",
         in_vmem(got_grad), picked, attended,
-        unread=1,
+        outside=1,
     )
     got_parts = exchange(parts, "seq")
     big, message = total_over_clips(in_vmem(got_parts), attended, each)
     returned = exchange(message, "head")
-    all_big, strides = gather_over_clips(big, groups)
+    all_big = lax.all_gather(big, "seq")
     cond_whole, in_grad, time_grad, gain_grad, out_grad = write_gradients(
-        lax.axis_index("seq").reshape(1), all_big, strides, returned, each, width
+        all_big, returned, each, width
     )
     rows = jnp.transpose(returned[:, :each], (1, 0, 2)).reshape(each, heads * HD)
     return (rows, cond_whole, in_grad, time_grad, gain_grad, out_grad.T)

time: 224 us -> 228 us (1.018)
  blocking collectives: 26.5 us -> 75.2 us
  starting transfers between devices: 47.9 us -> 27.1 us
  waiting for transfers between devices: 64 us -> 44.3 us
  local copies, waits for them, and re-layouts: 24.1 us -> 19.5 us
    all_gather x0 -> x1, blocking collectives: none -> 48.4 us  [local(): all_big = lax.all_gather(big, 'seq')]
    ppermute x5 -> x0, waiting for transfers between devices: 19.2 us -> none  [gather_over_clips(): held = jnp.concatenate([held, lax.ppermute(held, 'seq', pairs)])]
    ppermute x5 -> x0, starting transfers between devices: 18.6 us -> none  [gather_over_clips(): held = jnp.concatenate([held, lax.ppermute(held, 'seq', pairs)])]
    unnamed x32, local copies, waits for them, and re-layouts: 8.63 us -> 5.85 us
  transfers between devices with their start and end apart: 9 -> 4, of which waited for: 8 -> 3; matrix products, arithmetic and copies ran while one was open for 11% -> 11% of each run, Pallas kernels for 17% -> 16%
where the time goes in v4:
time: 228 us; the launch traced here: 226 us
  blocking collectives  75.2 us (33%)
  Pallas kernels  52.7 us (23%)
  waiting for transfers between devices  44.3 us (19%)
  starting transfers between devices  27.1 us (12%)
  local copies, waits for them, and re-layouts  19.5 us (9%)
  other arithmetic  4.65 us (2%)
    all_gather x1, blocking collectives, local(): all_big = lax.all_gather(big, 'seq')  48.4 us
    all_to_all x4, waiting for transfers between devices, exchange(): return lax.all_to_all(value, axis, split_axis=0, concat_axis=0, tiled=True)  44.3 us
    pallas_call x2, Pallas kernels, attend_some(): pl.pallas_call(functools.partial(attend_kernel, first), grid=(count,), in...  36.7 us
    all_to_all x4, starting transfers between devices, exchange(): return lax.all_to_all(value, axis, split_axis=0, concat_axis=0, tiled=True)  27.1 us
    all_to_all x1, blocking collectives, exchange(): return lax.all_to_all(value, axis, split_axis=0, concat_axis=0, tiled=True)  26.8 us
    pallas_call x2, Pallas kernels, call(): pl.pallas_call(kernel, in_specs=specs, out_specs=[vmem()] * len(out_shape...  5.95 us
    unnamed x32, local copies, waits for them, and re-layouts  5.85 us
    pallas_call x1, Pallas kernels, attend_masked(): pl.pallas_call(masked_kernel, in_specs=[vmem()] * 3 + [anywhere()], out_s...  5.14 us
  transfers between devices with their start and end apart: 4, of which 3 were waited for; matrix products, arithmetic and copies ran while one was open for 11% of the time, Pallas kernels for 16%

profile of v4, /device:TPU:6, one launch (start us, length us, event | category | flops | bytes accessed | tf_op | source)
XLA Modules:
  0.0 226.4 jit_solution(5674324120954412522)
XLA Ops:
  0.6 3.1 %stack_by_head.1 = bf16[16,3,224,128]{3,2,1,0:T(8,128)(2,1)} custom-call(bf16[224,2048]{1,0:T(8,128)(2,1)} %q_ref.1, bf16[224,2048]{1,0:T(8,128)(2,1)} %k_ref.1, bf16[224,2048]{1,0:T(8,128)(2,1)} %v_ref.1), custom_call_target="tpu_custom_call" | custom-call | tf_op jit(solution)/shard_map/stack_by_head/pallas_call | solution.py:76
  3.8 10.6 %all-to-all-start = ((bf16[16,3,224,128]{3,2,1,0:T(8,128)(2,1)}), bf16[16,3,224,128]{3,2,1,0:T(8,128)(2,1)S(1)}, u32[]{:S(2)}, u32[]{:S(2)}) async-start(bf16[16,3,224,128]{3,2,1,0:T(8,128)(2,1)} %stack_by_head.1), calls=%async_computation | async-start | bytes 5505024 | tf_op jit(solution)/shard_map/all_to_all | solution.py:400
  15.7 1.3 copy.62
  17.6 1.9 gather_fusion.1
  21.0 1.7 gather_fusion
  25.5 2.1 copy.64
  27.7 2.0 gather_fusion.2
  30.4 1.2 copy.66
  31.6 2.0 gather_fusion.3
  37.4 2.0 convolution_add_fusion.base_hbm
  39.5 38.2 %all-to-all-done.got_ref = bf16[16,3,224,128]{3,2,1,0:T(8,128)(2,1)S(1)} async-done(((bf16[16,3,224,128]{3,2,1,0:T(8,128)(2,1)}), bf16[16,3,224,128]{3,2,1,0:T(8,128)(2,1)S(1)}, u32[]{:S(2)}, u32[]{:S(2)}) %all-to-all-start) | async-done | bytes 2752544 | tf_op jit(solution)/shard_map/all_to_all | solution.py:400
  77.7 5.1 %masked_rows.1 = (bf16[16,16,1536]{2,1,0:T(8,128)(2,1)}, bf16[256,128]{1,0:T(8,128)(2,1)S(1)}) custom-call(bf16[16,3,224,128]{3,2,1,0:T(8,128)(2,1)S(1)} %all-to-all-done.got_ref, s32[256,2]{1,0:T(8,128)S(1)} %copy.68.slot_ref, s32[1,3584]{1,0:T(1,128)S(1)} %copy-done.1, bf16[128,1536]{1,0:T(8,128)(2,1)} %w_ref.1), custom_call_target="tpu_custom_call" | custom-call | tf_op jit(solution)/shard_map/masked_rows/pallas_call | solution.py:151
  82.9 4.9 %all-to-all-start.1 = ((bf16[16,16,1536]{2,1,0:T(8,128)(2,1)}), bf16[16,16,1536]{2,1,0:T(8,128)(2,1)}, u32[]{:S(2)}, u32[]{:S(2)}) async-start(bf16[16,16,1536]{2,1,0:T(8,128)(2,1)} %get-tuple-element.24), calls=%async_computation.1 | async-start | bytes 1572864 | tf_op jit(solution)/shard_map/all_to_all | solution.py:400
  87.8 18.4 %attention.2.after_ref.rest_1_ = bf16[16,256,128]{2,1,0:T(8,128)(2,1)} custom-call(bf16[16,3,224,128]{3,2,1,0:T(8,128)(2,1)S(1)} %all-to-all-done.got_ref, s32[224,128]{1,0:T(8,128)S(1)} %pad.27.qrank_ref, s32[1,3584]{1,0:T(1,128)S(1)} %copy-done.1, bf16[256,128]{1,0:T(8,128)(2,1)S(1)} %get-tuple-element.30.rest_0_.picked_ref), custom_call_target="tpu_custom_call" | custom-call | tf_op jit(solution)/shard_map/attention/pallas_call | solution.py:201
  106.2 2.3 %all-to-all-done.1.cond_ref = bf16[16,16,1536]{2,1,0:T(8,128)(2,1)} async-done(((bf16[16,16,1536]{2,1,0:T(8,128)(2,1)}), bf16[16,16,1536]{2,1,0:T(8,128)(2,1)}, u32[]{:S(2)}, u32[]{:S(2)}) %all-to-all-start.1) | async-done | bytes 786464 | tf_op jit(solution)/shard_map/all_to_all | solution.py:400
  108.5 4.5 %diffusion_head.1 = (bf16[16,16,1664]{2,1,0:T(8,128)(2,1)}, f32[8,128]{1,0:T(8,128)S(1)}) custom-call(bf16[16,16,1536]{2,1,0:T(8,128)(2,1)} %all-to-all-done.1.cond_ref, f32[1,1536]{1,0:T(1,128)S(1)} %reshape.128.gain_ref, f32[16,1536]{1,0:T(8,128)S(1)} %bitcast.47, f32[64,17]{1,0:T(8,128)S(1)} %copy.69.noise_ref, ...), custom_call_target="tpu_custom_call" | custom-call | tf_op jit(solution)/shard_map/diffusion_head/pallas_call | solution.py:388
  113.0 5.2 %all-to-all-start.2 = ((bf16[16,16,1664]{2,1,0:T(8,128)(2,1)}), bf16[16,16,1664]{2,1,0:T(8,128)(2,1)}, u32[]{:S(2)}, u32[]{:S(2)}) async-start(bf16[16,16,1664]{2,1,0:T(8,128)(2,1)} %get-tuple-element.31), calls=%async_computation.2 | async-start | bytes 1703936 | tf_op jit(solution)/shard_map/all_to_all | solution.py:400
  118.2 18.4 %attention.3.after_ref.attended_ref = bf16[16,256,128]{2,1,0:T(8,128)(2,1)} custom-call(bf16[16,3,224,128]{3,2,1,0:T(8,128)(2,1)S(1)} %all-to-all-done.got_ref, s32[224,128]{1,0:T(8,128)S(1)} %pad.27.qrank_ref, s32[1,3584]{1,0:T(1,128)S(1)} %copy-done.1, f32[8,128]{1,0:T(8,128)S(1)} %get-tuple-element.32.rest_0_, ...), custom_call_target="tpu_custom_call", output_to_operand_aliasing={{}: (4, {})} | custom-call | tf_op jit(solution)/shard_map/attention/pallas_call | solution.py:201
  136.6 3.9 %all-to-all-done.2.got_ref = bf16[16,16,1664]{2,1,0:T(8,128)(2,1)} async-done(((bf16[16,16,1664]{2,1,0:T(8,128)(2,1)}), bf16[16,16,1664]{2,1,0:T(8,128)(2,1)}, u32[]{:S(2)}, u32[]{:S(2)}) %all-to-all-start.2) | async-done | bytes 852000 | tf_op jit(solution)/shard_map/all_to_all | solution.py:400
  140.4 1.5 cond_weight_grad.1
  141.9 26.8 %all_to_all.25.got_ref = bf16[32,16,640]{2,1,0:T(8,128)(2,1)S(1)} all-to-all(bf16[32,16,640]{2,1,0:T(8,128)(2,1)S(1)} %cond_weight_grad.1), channel_id=1, replica_groups=mesh['seq'=32,'head'=16] {'seq'}, dimensions={0} | all-to-all | bytes 1310720 | tf_op jit(solution)/shard_map/all_to_all | solution.py:400
  169.5 6.4 %all-to-all-start.4 = ((bf16[16,256,128]{2,1,0:T(8,128)(2,1)}), bf16[16,256,128]{2,1,0:T(8,128)(2,1)S(1)}, u32[]{:S(2)}, u32[]{:S(2)}) async-start(bf16[16,256,128]{2,1,0:T(8,128)(2,1)} %get-tuple-element.33), calls=%async_computation.4 | async-start | bytes 2097152 | tf_op jit(solution)/shard_map/all_to_all | solution.py:400
  175.9 48.4 %all-gather = bf16[512,384]{1,0:T(8,128)(2,1)S(1)} all-gather(bf16[16,384]{1,0:T(8,128)(2,1)S(1)} %get-tuple-element.34), channel_id=2, replica_groups=mesh['seq'=32,'head'=16] {'seq'}, dimensions={0}, use_global_device_ids=true | all-gather | bytes 405504 | tf_op jit(solution)/shard_map/all_gather | solution.py:495
  224.4 1.1 copy_bitcast_fusion
  (75 shorter events, 12.6 us)
Async XLA Ops:
  0.6 36.8 %copy-start = (f32[16,1536]{1,0:T(8,128)S(1)}, f32[16,1536]{1,0:T(8,128)}, u32[]{:S(2)}) copy-start(f32[16,1536]{1,0:T(8,128)} %param.24) | copy-start | bytes 294916
  3.8 11.1 %copy-start.9 = (s32[1,224]{1,0:T(1,128)S(1)}, s32[1,224]{1,0:T(1,128)}, u32[]{:S(2)}) copy-start(s32[1,224]{1,0:T(1,128)} %param.18) | copy-start | bytes 2692
  3.8 11.9 %copy-start.4 = (bf16[3584,4]{0,1:T(4,128)(2,1)S(1)}, bf16[3584,4]{0,1:T(4,128)(2,1)}, u32[]{:S(2)}) copy-start(bf16[3584,4]{0,1:T(4,128)(2,1)} %param.22) | copy-start | bytes 86020
  3.8 17.1 %copy-start.1 = (s32[1,3584]{1,0:T(1,128)S(1)}, s32[1,3584]{1,0:T(1,128)}, u32[]{:S(2)}) copy-start(s32[1,3584]{1,0:T(1,128)} %rank_ref.5) | copy-start | bytes 43012
  3.8 19.0 %copy-start.13 = (s32[32]{0:T(128)S(1)}, s32[32]{0:T(128)}, u32[]{:S(2)}) copy-start(s32[32]{0:T(128)} %param.19) | copy-start | bytes 388
  3.8 73.9 %all-to-all-start = ((bf16[16,3,224,128]{3,2,1,0:T(8,128)(2,1)}), bf16[16,3,224,128]{3,2,1,0:T(8,128)(2,1)S(1)}, u32[]{:S(2)}, u32[]{:S(2)}) async-start(bf16[16,3,224,128]{3,2,1,0:T(8,128)(2,1)} %stack_by_head.1), calls=%async_computation | async-start | bytes 5505024 | tf_op jit(solution)/shard_map/all_to_all | solution.py:400
  14.4 16.0 %copy-start.3 = (bf16[3584,64]{0,1:T(8,128)(2,1)S(1)}, bf16[3584,64]{0,1:T(8,128)(2,1)}, u32[]{:S(2)}) copy-start(bf16[3584,64]{0,1:T(8,128)(2,1)} %param.21) | copy-start | bytes 1376260
  17.0 0.6 copy-start.7
  19.5 1.3 copy-start.6
  19.6 1.3 copy-start.5
  25.5 11.8 %copy-start.10 = (s32[256,1]{0,1:T(1,128)S(1)}, s32[256,1]{0,1:T(1,128)}, u32[]{:S(2)}) copy-start(s32[256,1]{0,1:T(1,128)} %stack_reshape.7) | copy-start | bytes 3076
  25.5 11.8 %copy-start.11 = (s32[256,1]{0,1:T(1,128)S(1)}, s32[256,1]{0,1:T(1,128)}, u32[]{:S(2)}) copy-start(s32[256,1]{0,1:T(1,128)} %stack_reshape.6) | copy-start | bytes 3076
  25.5 11.8 %copy-start.8 = (f32[64,1]{0,1:T(1,128)S(1)}, f32[64,1]{0,1:T(1,128)}, u32[]{:S(2)}) copy-start(f32[64,1]{0,1:T(1,128)} %reshape_broadcast_in_dim.3) | copy-start | bytes 772
  25.5 11.9 %copy-start.12 = (f32[64]{0:T(128)S(1)}, f32[64]{0:T(128)}, u32[]{:S(2)}) copy-start(f32[64]{0:T(128)} %mul.54) | copy-start | bytes 772
  82.9 25.6 %copy-start.2 = (f32[1536,16]{0,1:T(8,128)S(1)}, f32[1536,16]{0,1:T(8,128)}, u32[]{:S(2)}) copy-start(f32[1536,16]{0,1:T(8,128)} %param.27) | copy-start | bytes 294916
  82.9 25.6 %all-to-all-start.1 = ((bf16[16,16,1536]{2,1,0:T(8,128)(2,1)}), bf16[16,16,1536]{2,1,0:T(8,128)(2,1)}, u32[]{:S(2)}, u32[]{:S(2)}) async-start(bf16[16,16,1536]{2,1,0:T(8,128)(2,1)} %get-tuple-element.24), calls=%async_computation.1 | async-start | bytes 1572864 | tf_op jit(solution)/shard_map/all_to_all | solution.py:400
  113.0 27.5 %all-to-all-start.2 = ((bf16[16,16,1664]{2,1,0:T(8,128)(2,1)}), bf16[16,16,1664]{2,1,0:T(8,128)(2,1)}, u32[]{:S(2)}, u32[]{:S(2)}) async-start(bf16[16,16,1664]{2,1,0:T(8,128)(2,1)} %get-tuple-element.31), calls=%async_computation.2 | async-start | bytes 1703936 | tf_op jit(solution)/shard_map/all_to_all | solution.py:400
  169.5 54.9 %all-to-all-start.4 = ((bf16[16,256,128]{2,1,0:T(8,128)(2,1)}), bf16[16,256,128]{2,1,0:T(8,128)(2,1)S(1)}, u32[]{:S(2)}, u32[]{:S(2)}) async-start(bf16[16,256,128]{2,1,0:T(8,128)(2,1)} %get-tuple-element.33), calls=%async_computation.4 | async-start | bytes 2097152 | tf_op jit(solution)/shard_map/all_to_all | solution.py:400

commit v5 on v4

--- a/solution.py
+++ b/solution.py
@@ -18,6 +18,7 @@
 PACK = 256
 TAIL = 32
 GROUP_ROWS = 16
+STAGES = ((8, 16, 24), (4, 2, 6), (1,))
 LOG2E = 1.4426950408889634
 F32 = jnp.float32
 BF16 = jnp.bfloat16
@@ -336,15 +337,19 @@
     )(got, attended)
 
 
-def spread_kernel(big_ref, tail_ref, cond_ref, in_ref, time_ref, gain_ref, out_ref):
-    groups, rows, cols = big_ref.shape
+def spread_kernel(order, seq_ref, *refs):
+    tail_ref, cond_ref, in_ref, time_ref, gain_ref, out_ref = refs[-6:]
+    cols = refs[0].shape[2]
     heads = tail_ref.shape[0]
     width = cond_ref.shape[1]
     col_groups = width // cols
-    for group in range(groups):
-        top = group // col_groups * GROUP_ROWS
-        left = group % col_groups * cols
-        cond_ref[top : top + GROUP_ROWS, left : left + cols] = big_ref[group].astype(F32)
+    seq = seq_ref[0]
+    for big_ref, masks in zip(refs, order):
+        for place, mask in enumerate(masks):
+            group = seq ^ mask
+            top = pl.multiple_of(group // col_groups * GROUP_ROWS, GROUP_ROWS)
+            left = pl.multiple_of(lax.rem(group, col_groups) * cols, 128)
+            cond_ref[pl.ds(top, GROUP_ROWS), pl.ds(left, cols)] = big_ref[place].astype(F32)
     pieces = width // 128
     for head in range(heads):
         packed = tail_ref[head].astype(F32)
@@ -360,13 +365,14 @@
             gain_ref[cut] = packed[row + 1]
 
 
-def write_gradients(big, returned, each, width):
+def write_gradients(seq, big, order, returned, each, width):
     heads = returned.shape[0]
     return pl.pallas_call(
-        spread_kernel,
+        functools.partial(spread_kernel, order),
         grid=(1,),
         in_specs=[
-            vmem(),
+            pl.BlockSpec(memory_space=pltpu.SMEM),
+            *[vmem()] * len(big),
             pl.BlockSpec((heads, TAIL, HD), lambda i: (0, each // TAIL, 0)),
         ],
         out_specs=[vmem()] * 5,
@@ -379,7 +385,7 @@
         ],
         compiler_params=params(),
         name="write_gradients",
-    )(big, returned)
+    )(seq, *big, returned)
 
 
 def call(kernel, out_shape, scratch, name, *operands, outside=0):
@@ -394,6 +400,20 @@
         compiler_params=params(),
         name=name,
     )(*operands)
+
+
+def gather_over_clips(piece, groups):
+    parts, order = [piece[None]], [[0]]
+    for stage in STAGES:
+        held = parts[0] if len(parts) == 1 else jnp.concatenate(parts)
+        masks = [mask for part in order for mask in part]
+        parts, order = [held], [masks]
+        for partner in stage:
+            if partner < groups:
+                pairs = [(source, source ^ partner) for source in range(groups)]
+                parts.append(lax.ppermute(held, "seq", pairs))
+                order.append([mask ^ partner for mask in masks])
+    return parts, order
 
 
 def exchange(value, axis):
@@ -492,9 +512,9 @@
     got_parts = exchange(parts, "seq")
     big, message = total_over_clips(in_vmem(got_parts), attended, each)
     returned = exchange(message, "head")
-    all_big = lax.all_gather(big, "seq")
+    all_big, order = gather_over_clips(big, groups)
     cond_whole, in_grad, time_grad, gain_grad, out_grad = write_gradients(
-        all_big, returned, each, width
+        lax.axis_index("seq").reshape(1), all_big, order, returned, each, width
     )
     rows = jnp.transpose(returned[:, :each], (1, 0, 2)).reshape(each, heads * HD)
     return (rows, cond_whole, in_grad, time_grad, gain_grad, out_grad.T)

time: 228 us -> 218 us (0.956)
  blocking collectives: 75.2 us -> 26.8 us
  starting transfers between devices: 27.1 us -> 52 us
  waiting for transfers between devices: 44.3 us -> 56.9 us
    all_gather x1 -> x0, blocking collectives: 48.4 us -> none  [local(): all_big = lax.all_gather(big, 'seq')]
    ppermute x0 -> x7, starting transfers between devices: none -> 25 us  [gather_over_clips(): parts.append(lax.ppermute(held, 'seq', pairs))]
    ppermute x0 -> x7, waiting for transfers between devices: none -> 12.1 us  [gather_over_clips(): parts.append(lax.ppermute(held, 'seq', pairs))]
    unnamed x32 -> x38, local copies, waits for them, and re-layouts: 5.85 us -> 5.33 us
  transfers between devices with their start and end apart: 4 -> 11, of which waited for: 3 -> 6; matrix products, arithmetic and copies ran while one was open for 11% -> 12% of each run, Pallas kernels for 16% -> 17%
where the time goes in v5:
time: 218 us; the launch traced here: 215 us
  waiting for transfers between devices  56.9 us (26%)
  Pallas kernels  52.9 us (24%)
  starting transfers between devices  52 us (24%)
  blocking collectives  26.8 us (12%)
  local copies, waits for them, and re-layouts  18.9 us (9%)
  other arithmetic  4.76 us (2%)
    all_to_all x4, waiting for transfers between devices, exchange(): return lax.all_to_all(value, axis, split_axis=0, concat_axis=0, tiled=True)  44.9 us
    pallas_call x2, Pallas kernels, attend_some(): pl.pallas_call(functools.partial(attend_kernel, first), grid=(count,), in...  36.7 us
    all_to_all x4, starting transfers between devices, exchange(): return lax.all_to_all(value, axis, split_axis=0, concat_axis=0, tiled=True)  27.1 us
    all_to_all x1, blocking collectives, exchange(): return lax.all_to_all(value, axis, split_axis=0, concat_axis=0, tiled=True)  26.8 us
    ppermute x7, starting transfers between devices, gather_over_clips(): parts.append(lax.ppermute(held, 'seq', pairs))  25 us
    ppermute x7, waiting for transfers between devices, gather_over_clips(): parts.append(lax.ppermute(held, 'seq', pairs))  12.1 us
    pallas_call x2, Pallas kernels, call(): pl.pallas_call(kernel, in_specs=specs, out_specs=[vmem()] * len(out_shape...  5.95 us
    unnamed x38, local copies, waits for them, and re-layouts  5.33 us
  transfers between devices with their start and end apart: 11, of which 6 were waited for; matrix products, arithmetic and copies ran while one was open for 12% of the time, Pallas kernels for 17%

profile of v5, /device:TPU:6, one launch (start us, length us, event | category | flops | bytes accessed | tf_op | source)
XLA Modules:
  0.0 215.5 jit_solution(13557809027698256446)
XLA Ops:
  0.6 3.2 %stack_by_head.1 = bf16[16,3,224,128]{3,2,1,0:T(8,128)(2,1)} custom-call(bf16[224,2048]{1,0:T(8,128)(2,1)} %q_ref.1, bf16[224,2048]{1,0:T(8,128)(2,1)} %k_ref.1, bf16[224,2048]{1,0:T(8,128)(2,1)} %v_ref.1), custom_call_target="tpu_custom_call" | custom-call | tf_op jit(solution)/shard_map/stack_by_head/pallas_call | solution.py:77
  3.8 10.6 %all-to-all-start = ((bf16[16,3,224,128]{3,2,1,0:T(8,128)(2,1)}), bf16[16,3,224,128]{3,2,1,0:T(8,128)(2,1)S(1)}, u32[]{:S(2)}, u32[]{:S(2)}) async-start(bf16[16,3,224,128]{3,2,1,0:T(8,128)(2,1)} %stack_by_head.1), calls=%async_computation | async-start | bytes 5505024 | tf_op jit(solution)/shard_map/all_to_all | solution.py:420
  24.9 2.1 copy.64
  39.0 38.7 %all-to-all-done.got_ref = bf16[16,3,224,128]{3,2,1,0:T(8,128)(2,1)S(1)} async-done(((bf16[16,3,224,128]{3,2,1,0:T(8,128)(2,1)}), bf16[16,3,224,128]{3,2,1,0:T(8,128)(2,1)S(1)}, u32[]{:S(2)}, u32[]{:S(2)}) %all-to-all-start) | async-done | bytes 2752544 | tf_op jit(solution)/shard_map/all_to_all | solution.py:420
  77.7 5.1 %masked_rows.1 = (bf16[16,16,1536]{2,1,0:T(8,128)(2,1)}, bf16[256,128]{1,0:T(8,128)(2,1)S(1)}) custom-call(bf16[16,3,224,128]{3,2,1,0:T(8,128)(2,1)S(1)} %all-to-all-done.got_ref, s32[256,2]{1,0:T(8,128)S(1)} %copy.68.slot_ref, s32[1,3584]{1,0:T(1,128)S(1)} %copy-done.1, bf16[128,1536]{1,0:T(8,128)(2,1)} %w_ref.1), custom_call_target="tpu_custom_call" | custom-call | tf_op jit(solution)/shard_map/masked_rows/pallas_call | solution.py:152
  82.9 4.9 %all-to-all-start.1 = ((bf16[16,16,1536]{2,1,0:T(8,128)(2,1)}), bf16[16,16,1536]{2,1,0:T(8,128)(2,1)}, u32[]{:S(2)}, u32[]{:S(2)}) async-start(bf16[16,16,1536]{2,1,0:T(8,128)(2,1)} %get-tuple-element.24), calls=%async_computation.1 | async-start | bytes 1572864 | tf_op jit(solution)/shard_map/all_to_all | solution.py:420
  87.8 18.4 %attention.2.after_ref.rest_1_ = bf16[16,256,128]{2,1,0:T(8,128)(2,1)} custom-call(bf16[16,3,224,128]{3,2,1,0:T(8,128)(2,1)S(1)} %all-to-all-done.got_ref, s32[224,128]{1,0:T(8,128)S(1)} %pad.27.qrank_ref, s32[1,3584]{1,0:T(1,128)S(1)} %copy-done.1, bf16[256,128]{1,0:T(8,128)(2,1)S(1)} %get-tuple-element.30.rest_0_.picked_ref), custom_call_target="tpu_custom_call" | custom-call | tf_op jit(solution)/shard_map/attention/pallas_call | solution.py:202
  106.2 2.3 %all-to-all-done.1.cond_ref = bf16[16,16,1536]{2,1,0:T(8,128)(2,1)} async-done(((bf16[16,16,1536]{2,1,0:T(8,128)(2,1)}), bf16[16,16,1536]{2,1,0:T(8,128)(2,1)}, u32[]{:S(2)}, u32[]{:S(2)}) %all-to-all-start.1) | async-done | bytes 786464 | tf_op jit(solution)/shard_map/all_to_all | solution.py:420
  108.5 4.5 %diffusion_head.1 = (bf16[16,16,1664]{2,1,0:T(8,128)(2,1)}, f32[8,128]{1,0:T(8,128)S(1)}) custom-call(bf16[16,16,1536]{2,1,0:T(8,128)(2,1)} %all-to-all-done.1.cond_ref, f32[1,1536]{1,0:T(1,128)S(1)} %reshape.131.gain_ref, f32[16,1536]{1,0:T(8,128)S(1)} %bitcast.48, f32[64,17]{1,0:T(8,128)S(1)} %copy.69.noise_ref, ...), custom_call_target="tpu_custom_call" | custom-call | tf_op jit(solution)/shard_map/diffusion_head/pallas_call | solution.py:394
  113.0 5.2 %all-to-all-start.2 = ((bf16[16,16,1664]{2,1,0:T(8,128)(2,1)}), bf16[16,16,1664]{2,1,0:T(8,128)(2,1)}, u32[]{:S(2)}, u32[]{:S(2)}) async-start(bf16[16,16,1664]{2,1,0:T(8,128)(2,1)} %get-tuple-element.31), calls=%async_computation.2 | async-start | bytes 1703936 | tf_op jit(solution)/shard_map/all_to_all | solution.py:420
  118.2 18.4 %attention.3.after_ref.attended_ref = bf16[16,256,128]{2,1,0:T(8,128)(2,1)} custom-call(bf16[16,3,224,128]{3,2,1,0:T(8,128)(2,1)S(1)} %all-to-all-done.got_ref, s32[224,128]{1,0:T(8,128)S(1)} %pad.27.qrank_ref, s32[1,3584]{1,0:T(1,128)S(1)} %copy-done.1, f32[8,128]{1,0:T(8,128)S(1)} %get-tuple-element.32.rest_0_, ...), custom_call_target="tpu_custom_call", output_to_operand_aliasing={{}: (4, {})} | custom-call | tf_op jit(solution)/shard_map/attention/pallas_call | solution.py:202
  136.6 3.9 %all-to-all-done.2.got_ref = bf16[16,16,1664]{2,1,0:T(8,128)(2,1)} async-done(((bf16[16,16,1664]{2,1,0:T(8,128)(2,1)}), bf16[16,16,1664]{2,1,0:T(8,128)(2,1)}, u32[]{:S(2)}, u32[]{:S(2)}) %all-to-all-start.2) | async-done | bytes 852000 | tf_op jit(solution)/shard_map/all_to_all | solution.py:420
  141.9 26.8 %all_to_all.25.got_ref = bf16[32,16,640]{2,1,0:T(8,128)(2,1)S(1)} all-to-all(bf16[32,16,640]{2,1,0:T(8,128)(2,1)S(1)} %cond_weight_grad.1), channel_id=1, replica_groups=mesh['seq'=32,'head'=16] {'seq'}, dimensions={0} | all-to-all | bytes 1310720 | tf_op jit(solution)/shard_map/all_to_all | solution.py:420
  169.5 6.4 %all-to-all-start.4 = ((bf16[16,256,128]{2,1,0:T(8,128)(2,1)}), bf16[16,256,128]{2,1,0:T(8,128)(2,1)S(1)}, u32[]{:S(2)}, u32[]{:S(2)}) async-start(bf16[16,256,128]{2,1,0:T(8,128)(2,1)} %get-tuple-element.33), calls=%async_computation.4 | async-start | bytes 2097152 | tf_op jit(solution)/shard_map/all_to_all | solution.py:420
  176.0 2.5 %collective-permute-start = (bf16[1,16,384]{2,1,0:T(8,128)(2,1)S(1)}, bf16[1,16,384]{2,1,0:T(8,128)(2,1)S(1)}, u32[]{:S(2)}, u32[]{:S(2)}) collective-permute-start(bf16[1,16,384]{2,1,0:T(8,128)(2,1)S(1)} %bitcast.49), channel_id=1, source_target_pairs={{0,128},{16,144},{32,160},{48,176},{64,192},{80,208},{96,224},{112... | collective-permute-start | bytes 36872 | tf_op jit(solution)/shard_map/ppermute | solution.py:414
  178.4 5.3 %collective-permute-start.1 = (bf16[1,16,384]{2,1,0:T(8,128)(2,1)S(1)}, bf16[1,16,384]{2,1,0:T(8,128)(2,1)S(1)}, u32[]{:S(2)}, u32[]{:S(2)}) collective-permute-start(bf16[1,16,384]{2,1,0:T(8,128)(2,1)S(1)} %bitcast.50), channel_id=1, source_target_pairs={{0,256},{16,272},{32,288},{48,304},{64,320},{80,336},{96,352},{112... | collective-permute-start | bytes 36872 | tf_op jit(solution)/shard_map/ppermute | solution.py:414
  183.7 2.7 %collective-permute-start.2 = (bf16[1,16,384]{2,1,0:T(8,128)(2,1)S(1)}, bf16[1,16,384]{2,1,0:T(8,128)(2,1)S(1)}, u32[]{:S(2)}, u32[]{:S(2)}) collective-permute-start(bf16[1,16,384]{2,1,0:T(8,128)(2,1)S(1)} %bitcast.51), channel_id=1, source_target_pairs={{0,384},{16,400},{32,416},{48,432},{64,448},{80,464},{96,480},{112... | collective-permute-start | bytes 36872 | tf_op jit(solution)/shard_map/ppermute | solution.py:414
  186.5 4.0 %collective-permute-done.2 = bf16[1,16,384]{2,1,0:T(8,128)(2,1)S(1)} collective-permute-done((bf16[1,16,384]{2,1,0:T(8,128)(2,1)S(1)}, bf16[1,16,384]{2,1,0:T(8,128)(2,1)S(1)}, u32[]{:S(2)}, u32[]{:S(2)}) %collective-permute-start.2) | collective-permute-done | bytes 12320 | tf_op jit(solution)/shard_map/ppermute | solution.py:414
  190.5 3.7 %collective-permute-start.3 = (bf16[4,16,384]{2,1,0:T(8,128)(2,1)S(1)}, bf16[4,16,384]{2,1,0:T(8,128)(2,1)S(1)}, u32[]{:S(2)}, u32[]{:S(2)}) collective-permute-start(bf16[4,16,384]{2,1,0:T(8,128)(2,1)S(1)} %pad_maximum_fusion), channel_id=1, source_target_pairs={{0,64},{16,80},{32,96},{48,112},{64,0},{80,16},{96,32},{112,48},{1... | collective-permute-start | bytes 147464 | tf_op jit(solution)/shard_map/ppermute | solution.py:414
  194.2 4.4 %collective-permute-start.4 = (bf16[4,16,384]{2,1,0:T(8,128)(2,1)S(1)}, bf16[4,16,384]{2,1,0:T(8,128)(2,1)S(1)}, u32[]{:S(2)}, u32[]{:S(2)}) collective-permute-start(bf16[4,16,384]{2,1,0:T(8,128)(2,1)S(1)} %pad_maximum_fusion), channel_id=1, source_target_pairs={{0,32},{16,48},{32,0},{48,16},{64,96},{80,112},{96,64},{112,80},{1... | collective-permute-start | bytes 147464 | tf_op jit(solution)/shard_map/ppermute | solution.py:414
  198.6 4.1 %collective-permute-start.5 = (bf16[4,16,384]{2,1,0:T(8,128)(2,1)S(1)}, bf16[4,16,384]{2,1,0:T(8,128)(2,1)S(1)}, u32[]{:S(2)}, u32[]{:S(2)}) collective-permute-start(bf16[4,16,384]{2,1,0:T(8,128)(2,1)S(1)} %pad_maximum_fusion), channel_id=1, source_target_pairs={{0,96},{16,112},{32,64},{48,80},{64,32},{80,48},{96,0},{112,16},{1... | collective-permute-start | bytes 147464 | tf_op jit(solution)/shard_map/ppermute | solution.py:414
  202.9 3.9 %collective-permute-done.5 = bf16[4,16,384]{2,1,0:T(8,128)(2,1)S(1)} collective-permute-done((bf16[4,16,384]{2,1,0:T(8,128)(2,1)S(1)}, bf16[4,16,384]{2,1,0:T(8,128)(2,1)S(1)}, u32[]{:S(2)}, u32[]{:S(2)}) %collective-permute-start.5) | collective-permute-done | bytes 49184 | tf_op jit(solution)/shard_map/ppermute | solution.py:414
  206.7 2.3 %collective-permute-start.6 = (bf16[16,16,384]{2,1,0:T(8,128)(2,1)S(1)}, bf16[16,16,384]{2,1,0:T(8,128)(2,1)S(1)}, u32[]{:S(2)}, u32[]{:S(2)}) collective-permute-start(bf16[16,16,384]{2,1,0:T(8,128)(2,1)S(1)} %constant_dynamic-update-slice_fusion.refs_0_), channel_id=1, source_target_pairs={{0,16},{16,0},{32,48},{48,32},{64,80},{80,64},{96,112},{112,96},{1... | collective-permute-start | bytes 589832 | tf_op jit(solution)/shard_map/ppermute | solution.py:414
  210.1 4.2 %collective-permute-done.6.refs_1_ = bf16[16,16,384]{2,1,0:T(8,128)(2,1)S(1)} collective-permute-done((bf16[16,16,384]{2,1,0:T(8,128)(2,1)S(1)}, bf16[16,16,384]{2,1,0:T(8,128)(2,1)S(1)}, u32[]{:S(2)}, u32[]{:S(2)}) %collective-permute-start.6) | collective-permute-done | bytes 196640 | tf_op jit(solution)/shard_map/ppermute | solution.py:414
  (95 shorter events, 26.9 us)
Async XLA Ops:
  0.6 36.3 %copy-start = (f32[16,1536]{1,0:T(8,128)S(1)}, f32[16,1536]{1,0:T(8,128)}, u32[]{:S(2)}) copy-start(f32[16,1536]{1,0:T(8,128)} %param.24) | copy-start | bytes 294916
  3.8 11.1 %copy-start.9 = (s32[1,224]{1,0:T(1,128)S(1)}, s32[1,224]{1,0:T(1,128)}, u32[]{:S(2)}) copy-start(s32[1,224]{1,0:T(1,128)} %param.18) | copy-start | bytes 2692
  3.8 11.9 %copy-start.4 = (bf16[3584,4]{0,1:T(4,128)(2,1)S(1)}, bf16[3584,4]{0,1:T(4,128)(2,1)}, u32[]{:S(2)}) copy-start(bf16[3584,4]{0,1:T(4,128)(2,1)} %param.22) | copy-start | bytes 86020
  3.8 16.4 %copy-start.1 = (s32[1,3584]{1,0:T(1,128)S(1)}, s32[1,3584]{1,0:T(1,128)}, u32[]{:S(2)}) copy-start(s32[1,3584]{1,0:T(1,128)} %rank_ref.5) | copy-start | bytes 43012
  3.8 18.4 %copy-start.13 = (s32[32]{0:T(128)S(1)}, s32[32]{0:T(128)}, u32[]{:S(2)}) copy-start(s32[32]{0:T(128)} %param.19) | copy-start | bytes 388
  3.8 73.9 %all-to-all-start = ((bf16[16,3,224,128]{3,2,1,0:T(8,128)(2,1)}), bf16[16,3,224,128]{3,2,1,0:T(8,128)(2,1)S(1)}, u32[]{:S(2)}, u32[]{:S(2)}) async-start(bf16[16,3,224,128]{3,2,1,0:T(8,128)(2,1)} %stack_by_head.1), calls=%async_computation | async-start | bytes 5505024 | tf_op jit(solution)/shard_map/all_to_all | solution.py:420
  14.4 15.4 %copy-start.3 = (bf16[3584,64]{0,1:T(8,128)(2,1)S(1)}, bf16[3584,64]{0,1:T(8,128)(2,1)}, u32[]{:S(2)}) copy-start(bf16[3584,64]{0,1:T(8,128)(2,1)} %param.21) | copy-start | bytes 1376260
  17.0 2.0 copy-start.7
  19.0 1.3 copy-start.6
  24.9 12.0 %copy-start.10 = (s32[256,1]{0,1:T(1,128)S(1)}, s32[256,1]{0,1:T(1,128)}, u32[]{:S(2)}) copy-start(s32[256,1]{0,1:T(1,128)} %stack_reshape.7) | copy-start | bytes 3076
  24.9 11.9 %copy-start.11 = (s32[256,1]{0,1:T(1,128)S(1)}, s32[256,1]{0,1:T(1,128)}, u32[]{:S(2)}) copy-start(s32[256,1]{0,1:T(1,128)} %stack_reshape.6) | copy-start | bytes 3076
  24.9 11.9 %copy-start.8 = (f32[64,1]{0,1:T(1,128)S(1)}, f32[64,1]{0,1:T(1,128)}, u32[]{:S(2)}) copy-start(f32[64,1]{0,1:T(1,128)} %reshape_broadcast_in_dim.3) | copy-start | bytes 772
  24.9 12.0 %copy-start.12 = (f32[64]{0:T(128)S(1)}, f32[64]{0:T(128)}, u32[]{:S(2)}) copy-start(f32[64]{0:T(128)} %mul.54) | copy-start | bytes 772
  82.9 25.6 %copy-start.2 = (f32[1536,16]{0,1:T(8,128)S(1)}, f32[1536,16]{0,1:T(8,128)}, u32[]{:S(2)}) copy-start(f32[1536,16]{0,1:T(8,128)} %param.27) | copy-start | bytes 294916
  82.9 25.6 %all-to-all-start.1 = ((bf16[16,16,1536]{2,1,0:T(8,128)(2,1)}), bf16[16,16,1536]{2,1,0:T(8,128)(2,1)}, u32[]{:S(2)}, u32[]{:S(2)}) async-start(bf16[16,16,1536]{2,1,0:T(8,128)(2,1)} %get-tuple-element.24), calls=%async_computation.1 | async-start | bytes 1572864 | tf_op jit(solution)/shard_map/all_to_all | solution.py:420
  113.0 27.5 %all-to-all-start.2 = ((bf16[16,16,1664]{2,1,0:T(8,128)(2,1)}), bf16[16,16,1664]{2,1,0:T(8,128)(2,1)}, u32[]{:S(2)}, u32[]{:S(2)}) async-start(bf16[16,16,1664]{2,1,0:T(8,128)(2,1)} %get-tuple-element.31), calls=%async_computation.2 | async-start | bytes 1703936 | tf_op jit(solution)/shard_map/all_to_all | solution.py:420
  169.5 39.5 %all-to-all-start.4 = ((bf16[16,256,128]{2,1,0:T(8,128)(2,1)}), bf16[16,256,128]{2,1,0:T(8,128)(2,1)S(1)}, u32[]{:S(2)}, u32[]{:S(2)}) async-start(bf16[16,256,128]{2,1,0:T(8,128)(2,1)} %get-tuple-element.33), calls=%async_computation.4 | async-start | bytes 2097152 | tf_op jit(solution)/shard_map/all_to_all | solution.py:420
  176.0 10.5 %collective-permute-start = (bf16[1,16,384]{2,1,0:T(8,128)(2,1)S(1)}, bf16[1,16,384]{2,1,0:T(8,128)(2,1)S(1)}, u32[]{:S(2)}, u32[]{:S(2)}) collective-permute-start(bf16[1,16,384]{2,1,0:T(8,128)(2,1)S(1)} %bitcast.49), channel_id=1, source_target_pairs={{0,128},{16,144},{32,160},{48,176},{64,192},{80,208},{96,224},{112... | collective-permute-start | bytes 36872 | tf_op jit(solution)/shard_map/ppermute | solution.py:414
  178.4 8.0 %collective-permute-start.1 = (bf16[1,16,384]{2,1,0:T(8,128)(2,1)S(1)}, bf16[1,16,384]{2,1,0:T(8,128)(2,1)S(1)}, u32[]{:S(2)}, u32[]{:S(2)}) collective-permute-start(bf16[1,16,384]{2,1,0:T(8,128)(2,1)S(1)} %bitcast.50), channel_id=1, source_target_pairs={{0,256},{16,272},{32,288},{48,304},{64,320},{80,336},{96,352},{112... | collective-permute-start | bytes 36872 | tf_op jit(solution)/shard_map/ppermute | solution.py:414
  183.7 6.8 %collective-permute-start.2 = (bf16[1,16,384]{2,1,0:T(8,128)(2,1)S(1)}, bf16[1,16,384]{2,1,0:T(8,128)(2,1)S(1)}, u32[]{:S(2)}, u32[]{:S(2)}) collective-permute-start(bf16[1,16,384]{2,1,0:T(8,128)(2,1)S(1)} %bitcast.51), channel_id=1, source_target_pairs={{0,384},{16,400},{32,416},{48,432},{64,448},{80,464},{96,480},{112... | collective-permute-start | bytes 36872 | tf_op jit(solution)/shard_map/ppermute | solution.py:414
  190.5 12.3 %collective-permute-start.3 = (bf16[4,16,384]{2,1,0:T(8,128)(2,1)S(1)}, bf16[4,16,384]{2,1,0:T(8,128)(2,1)S(1)}, u32[]{:S(2)}, u32[]{:S(2)}) collective-permute-start(bf16[4,16,384]{2,1,0:T(8,128)(2,1)S(1)} %pad_maximum_fusion), channel_id=1, source_target_pairs={{0,64},{16,80},{32,96},{48,112},{64,0},{80,16},{96,32},{112,48},{1... | collective-permute-start | bytes 147464 | tf_op jit(solution)/shard_map/ppermute | solution.py:414
  194.2 8.6 %collective-permute-start.4 = (bf16[4,16,384]{2,1,0:T(8,128)(2,1)S(1)}, bf16[4,16,384]{2,1,0:T(8,128)(2,1)S(1)}, u32[]{:S(2)}, u32[]{:S(2)}) collective-permute-start(bf16[4,16,384]{2,1,0:T(8,128)(2,1)S(1)} %pad_maximum_fusion), channel_id=1, source_target_pairs={{0,32},{16,48},{32,0},{48,16},{64,96},{80,112},{96,64},{112,80},{1... | collective-permute-start | bytes 147464 | tf_op jit(solution)/shard_map/ppermute | solution.py:414
  198.6 8.1 %collective-permute-start.5 = (bf16[4,16,384]{2,1,0:T(8,128)(2,1)S(1)}, bf16[4,16,384]{2,1,0:T(8,128)(2,1)S(1)}, u32[]{:S(2)}, u32[]{:S(2)}) collective-permute-start(bf16[4,16,384]{2,1,0:T(8,128)(2,1)S(1)} %pad_maximum_fusion), channel_id=1, source_target_pairs={{0,96},{16,112},{32,64},{48,80},{64,32},{80,48},{96,0},{112,16},{1... | collective-permute-start | bytes 147464 | tf_op jit(solution)/shard_map/ppermute | solution.py:414
  206.7 7.6 %collective-permute-start.6 = (bf16[16,16,384]{2,1,0:T(8,128)(2,1)S(1)}, bf16[16,16,384]{2,1,0:T(8,128)(2,1)S(1)}, u32[]{:S(2)}, u32[]{:S(2)}) collective-permute-start(bf16[16,16,384]{2,1,0:T(8,128)(2,1)S(1)} %constant_dynamic-update-slice_fusion.refs_0_), channel_id=1, source_target_pairs={{0,16},{16,0},{32,48},{48,32},{64,80},{80,64},{96,112},{112,96},{1... | collective-permute-start | bytes 589832 | tf_op jit(solution)/shard_map/ppermute | solution.py:414
  (1 other events, 1.2 us)

commit v6 on v4

--- a/solution.py
+++ b/solution.py
@@ -14,6 +14,7 @@
 NORM_EPS = 1e-06
 HIDDEN_SCORE = -1e30
 SLOT = 16
+EARLY = 6
 EXTRA = 128
 PACK = 256
 TAIL = 32
@@ -203,7 +204,7 @@
         grid=(count,),
         in_specs=specs,
         out_specs=pl.BlockSpec((1, each, HD), lambda i: (i + first, 0, 0)),
-        out_shape=jax.ShapeDtypeStruct((heads, each + TAIL, HD), BF16),
+        out_shape=jax.ShapeDtypeStruct((heads, each, HD), BF16),
         scratch_shapes=[
             pltpu.VMEM((total, HD), BF16),
             pltpu.VMEM((total, 2 * HD), BF16),
@@ -274,7 +275,7 @@
         send_ref[target] = block_scr[...].astype(BF16)
 
 
-def grad_kernel(got_ref, picked_ref, after_ref, send_ref, pack_scr):
+def grad_kernel(got_ref, picked_ref, after_ref, send_ref, token_ref, pack_scr):
     heads, rows, wide = got_ref.shape
     width = wide - EXTRA
     groups = send_ref.shape[0]
@@ -295,6 +296,7 @@
     row, lane = 2 * (pieces % 8), 128 * (pieces // 8)
     pack_scr[row : row + 2, lane : lane + 128] = summed[0:2, width:]
     packed = pack_scr[...].astype(BF16)
+    token_ref[...] = summed[:8, :HD]
     row_groups = HD // GROUP_ROWS
     col_groups = groups // row_groups
     cols = width // col_groups
@@ -305,35 +307,71 @@
         send_ref[group, :, cols:] = packed
 
 
-def total_kernel(got_ref, attended_ref, big_ref, tail_ref):
+def total_kernel(got_ref, big_ref, tail_ref, token_ref):
     groups, rows, wide = got_ref.shape
     cols = wide - PACK
     total = got_ref[0].astype(F32)
     for source in range(1, groups):
         total = total + got_ref[source].astype(F32)
+    token_ref[...] = total[:8, :HD]
     rounded = total.astype(BF16)
-    big_ref[...] = rounded[:, :cols]
+    for group in range(groups):
+        big_ref[group] = rounded[:, :cols]
     for head in range(tail_ref.shape[0]):
         tail_ref[head, :rows] = rounded[:, cols : cols + HD]
         tail_ref[head, rows:] = rounded[:, cols + HD :]
 
 
-def total_over_clips(got, attended, each):
-    groups, rows, wide = got.shape
-    heads = attended.shape[0]
+def route_kernel(steps, place_ref, own_ref, other_ref, *rest):
+    chips = other_ref.shape[0]
+    for step, out_ref in zip(steps, rest[-len(steps) :]):
+        target = lax.rem(place_ref[0] + step, chips)
+        out_ref[0] = own_ref[2 * target + place_ref[1]]
+        out_ref[1] = other_ref[target]
+
+
+def collect_kernel(place_ref, *refs):
+    out_ref = refs[-1]
+    chips = len(refs) - 1
+    for step in range(chips):
+        source = lax.rem(place_ref[0] - step + chips, chips)
+        for part in range(2):
+            core = place_ref[1] if part == 0 else 1 - place_ref[1]
+            left = pl.multiple_of((2 * source + core) * HD, HD)
+            out_ref[:, pl.ds(left, HD)] = refs[step][part]
+
+
+def smem():
+    return pl.BlockSpec(memory_space=pltpu.SMEM)
+
+
+def route(steps, place, own, other, after):
+    _, each, _ = own.shape
     return pl.pallas_call(
-        total_kernel,
-        grid=(1,),
-        in_specs=[vmem(), anywhere()],
-        out_specs=[vmem(), pl.BlockSpec((heads, TAIL, HD), lambda i: (0, each // TAIL, 0))],
-        out_shape=[
-            jax.ShapeDtypeStruct((rows, wide - PACK), BF16),
-            jax.ShapeDtypeStruct(attended.shape, BF16),
-        ],
-        input_output_aliases={1: 1},
+        functools.partial(route_kernel, steps),
+        in_specs=[smem(), vmem(), vmem(), anywhere()],
+        out_specs=[vmem()] * len(steps),
+        out_shape=[jax.ShapeDtypeStruct((2, each, HD), BF16)] * len(steps),
         compiler_params=params(),
-        name="sum_over_clips",
-    )(got, attended)
+        name="route",
+    )(place, own, other, after)
+
+
+def round_chips(value, step, heads):
+    pairs = [(source, (source + 2 * step) % heads) for source in range(heads)]
+    return lax.ppermute(value, "head", pairs)
+
+
+def collect(place, pieces):
+    _, each, _ = pieces[0].shape
+    return pl.pallas_call(
+        collect_kernel,
+        in_specs=[smem()] + [vmem()] * len(pieces),
+        out_specs=vmem(),
+        out_shape=jax.ShapeDtypeStruct((each, 2 * len(pieces) * HD), BF16),
+        compiler_params=params(),
+        name="collect",
+    )(place, *pieces)
 
 
 def spread_kernel(big_ref, tail_ref, cond_ref, in_ref, time_ref, gain_ref, out_ref):
@@ -360,28 +398,6 @@
             gain_ref[cut] = packed[row + 1]
 
 
-def write_gradients(big, returned, each, width):
-    heads = returned.shape[0]
-    return pl.pallas_call(
-        spread_kernel,
-        grid=(1,),
-        in_specs=[
-            vmem(),
-            pl.BlockSpec((heads, TAIL, HD), lambda i: (0, each // TAIL, 0)),
-        ],
-        out_specs=[vmem()] * 5,
-        out_shape=[
-            jax.ShapeDtypeStruct((HD, width), F32),
-            jax.ShapeDtypeStruct((LAT, width), F32),
-            jax.ShapeDtypeStruct((width,), F32),
-            jax.ShapeDtypeStruct((width,), F32),
-            jax.ShapeDtypeStruct((LAT, width), F32),
-        ],
-        compiler_params=params(),
-        name="write_gradients",
-    )(big, returned)
-
-
 def call(kernel, out_shape, scratch, name, *operands, outside=0):
     specs = [vmem()] * (len(operands) - outside) + [anywhere()] * outside
     many = isinstance(out_shape, list)
@@ -481,22 +497,57 @@
 
     col_groups = groups // (HD // GROUP_ROWS)
     cols = width // col_groups
-    parts = call(
+    place = lax.axis_index("head")
+    core = lax.rem(place, 2)
+    place = jnp.stack([place // 2, core])
+    to_other = lax.dynamic_index_in_dim(
+        attended.reshape(half, 2, each, HD), 1 - core, 1, keepdims=False
+    )
+    other = lax.ppermute(to_other, "head", [(i, i ^ 1) for i in range(heads)])
+    parts, token = call(
         grad_kernel,
-        jax.ShapeDtypeStruct((groups, GROUP_ROWS, cols + PACK), BF16),
+        [
+            jax.ShapeDtypeStruct((groups, GROUP_ROWS, cols + PACK), BF16),
+            jax.ShapeDtypeStruct((8, HD), F32),
+        ],
         [pltpu.VMEM((GROUP_ROWS, PACK), F32)],
         "cond_weight_grad",
         in_vmem(got_grad), picked, attended,
         outside=1,
     )
     got_parts = exchange(parts, "seq")
-    big, message = total_over_clips(in_vmem(got_parts), attended, each)
-    returned = exchange(message, "head")
-    all_big = lax.all_gather(big, "seq")
-    cond_whole, in_grad, time_grad, gain_grad, out_grad = write_gradients(
-        all_big, returned, each, width
-    )
-    rows = jnp.transpose(returned[:, :each], (1, 0, 2)).reshape(each, heads * HD)
+    early, late = tuple(range(EARLY)), tuple(range(EARLY, half))
+    messages = route(early, place, attended, other, token)
+    pieces = [messages[0]] + [round_chips(messages[k], k, heads) for k in early[1:]]
+    big, small, token = call(
+        total_kernel,
+        [
+            jax.ShapeDtypeStruct((groups, GROUP_ROWS, cols), BF16),
+            jax.ShapeDtypeStruct((heads, TAIL, HD), BF16),
+            jax.ShapeDtypeStruct((8, HD), F32),
+        ],
+        [],
+        "sum_over_clips",
+        in_vmem(got_parts),
+    )
+    all_big = exchange(big, "seq")
+    messages = route(late, place, attended, other, token)
+    pieces += [round_chips(message, k, heads) for k, message in zip(late, messages)]
+    all_small = exchange(small, "head")
+    cond_whole, in_grad, time_grad, gain_grad, out_grad = call(
+        spread_kernel,
+        [
+            jax.ShapeDtypeStruct((HD, width), F32),
+            jax.ShapeDtypeStruct((LAT, width), F32),
+            jax.ShapeDtypeStruct((width,), F32),
+            jax.ShapeDtypeStruct((width,), F32),
+            jax.ShapeDtypeStruct((LAT, width), F32),
+        ],
+        [],
+        "write_gradients",
+        in_vmem(all_big), in_vmem(all_small),
+    )
+    rows = collect(place, pieces)
     return (rows, cond_whole, in_grad, time_grad, gain_grad, out_grad.T)
 
 

time: 228 us -> 241 us (1.057)
  blocking collectives: 75.2 us -> 26.8 us
  starting transfers between devices: 27.1 us -> 62.8 us
  waiting for transfers between devices: 44.3 us -> 62.4 us
  local copies, waits for them, and re-layouts: 19.5 us -> 23.8 us
    all_gather x1 -> x0, blocking collectives: 48.4 us -> none  [local(): all_big = lax.all_gather(big, 'seq')]
    ppermute x0 -> x8, starting transfers between devices: none -> 28.4 us  [the longest x7 26.2 us: round_chips(): return lax.ppermute(value, 'head', pairs)]
    ppermute x0 -> x8, waiting for transfers between devices: none -> 11.4 us  [the longest x7 9.94 us: round_chips(): return lax.ppermute(value, 'head', pairs)]
    all_to_all x4 -> x5, starting transfers between devices: 27.1 us -> 34.5 us  [exchange(): return lax.all_to_all(value, axis, split_axis=0, concat_axis=0, tiled=True)]
    all_to_all x4 -> x5, waiting for transfers between devices: 44.3 us -> 51.1 us  [exchange(): return lax.all_to_all(value, axis, split_axis=0, concat_axis=0, tiled=True)]
    unnamed x32 -> x44, local copies, waits for them, and re-layouts: 5.85 us -> 11.2 us
    pallas_call x2 -> x4, Pallas kernels: 5.95 us -> 7.9 us  [call(): pl.pallas_call(kernel, in_specs=specs, out_specs=[vmem()] * len(out_shape...]
  transfers between devices with their start and end apart: 4 -> 13, of which waited for: 3 -> 8; matrix products, arithmetic and copies ran while one was open for 11% -> 10% of each run, Pallas kernels for 16% -> 16%
where the time goes in v6:
time: 241 us; the launch traced here: 239 us
  starting transfers between devices  62.8 us (26%)
  waiting for transfers between devices  62.4 us (26%)
  Pallas kernels  54.4 us (23%)
  blocking collectives  26.8 us (11%)
  local copies, waits for them, and re-layouts  23.8 us (10%)
  other arithmetic  5.03 us (2%)
    all_to_all x5, waiting for transfers between devices, exchange(): return lax.all_to_all(value, axis, split_axis=0, concat_axis=0, tiled=True)  51.1 us
    pallas_call x2, Pallas kernels, attend_some(): pl.pallas_call(functools.partial(attend_kernel, first), grid=(count,), in...  35.4 us
    all_to_all x5, starting transfers between devices, exchange(): return lax.all_to_all(value, axis, split_axis=0, concat_axis=0, tiled=True)  34.5 us
    all_to_all x1, blocking collectives, exchange(): return lax.all_to_all(value, axis, split_axis=0, concat_axis=0, tiled=True)  26.8 us
    ppermute x7, starting transfers between devices, round_chips(): return lax.ppermute(value, 'head', pairs)  26.2 us
    unnamed x44, local copies, waits for them, and re-layouts  11.2 us
    ppermute x7, waiting for transfers between devices, round_chips(): return lax.ppermute(value, 'head', pairs)  9.94 us
    pallas_call x4, Pallas kernels, call(): pl.pallas_call(kernel, in_specs=specs, out_specs=[vmem()] * len(out_shape...  7.9 us
  transfers between devices with their start and end apart: 13, of which 8 were waited for; matrix products, arithmetic and copies ran while one was open for 10% of the time, Pallas kernels for 16%

profile of v6, /device:TPU:6, one launch (start us, length us, event | category | flops | bytes accessed | tf_op | source)
XLA Modules:
  0.0 238.5 jit_solution(10552399295460359796)
XLA Ops:
  0.6 3.1 %stack_by_head.1 = bf16[16,3,224,128]{3,2,1,0:T(8,128)(2,1)} custom-call(bf16[224,2048]{1,0:T(8,128)(2,1)} %q_ref.1, bf16[224,2048]{1,0:T(8,128)(2,1)} %k_ref.1, bf16[224,2048]{1,0:T(8,128)(2,1)} %v_ref.1), custom_call_target="tpu_custom_call" | custom-call | tf_op jit(solution)/shard_map/stack_by_head/pallas_call | solution.py:77
  3.8 10.6 %all-to-all-start = ((bf16[16,3,224,128]{3,2,1,0:T(8,128)(2,1)}), bf16[16,3,224,128]{3,2,1,0:T(8,128)(2,1)S(1)}, u32[]{:S(2)}, u32[]{:S(2)}) async-start(bf16[16,3,224,128]{3,2,1,0:T(8,128)(2,1)} %stack_by_head.1), calls=%async_computation | async-start | bytes 5505024 | tf_op jit(solution)/shard_map/all_to_all | solution.py:416
  39.8 37.9 %all-to-all-done.got_ref = bf16[16,3,224,128]{3,2,1,0:T(8,128)(2,1)S(1)} async-done(((bf16[16,3,224,128]{3,2,1,0:T(8,128)(2,1)}), bf16[16,3,224,128]{3,2,1,0:T(8,128)(2,1)S(1)}, u32[]{:S(2)}, u32[]{:S(2)}) %all-to-all-start) | async-done | bytes 2752544 | tf_op jit(solution)/shard_map/all_to_all | solution.py:416
  77.7 5.1 %masked_rows.1 = (bf16[16,16,1536]{2,1,0:T(8,128)(2,1)}, bf16[256,128]{1,0:T(8,128)(2,1)S(1)}) custom-call(bf16[16,3,224,128]{3,2,1,0:T(8,128)(2,1)S(1)} %all-to-all-done.got_ref, s32[256,2]{1,0:T(8,128)S(1)} %copy.68.slot_ref, s32[1,3584]{1,0:T(1,128)S(1)} %copy-done.7, bf16[128,1536]{1,0:T(8,128)(2,1)} %w_ref.1), custom_call_target="tpu_custom_call" | custom-call | tf_op jit(solution)/shard_map/masked_rows/pallas_call | solution.py:152
  82.9 4.9 %all-to-all-start.1 = ((bf16[16,16,1536]{2,1,0:T(8,128)(2,1)}), bf16[16,16,1536]{2,1,0:T(8,128)(2,1)}, u32[]{:S(2)}, u32[]{:S(2)}) async-start(bf16[16,16,1536]{2,1,0:T(8,128)(2,1)} %get-tuple-element.36), calls=%async_computation.1 | async-start | bytes 1572864 | tf_op jit(solution)/shard_map/all_to_all | solution.py:416
  87.8 17.7 %attention.2.after_ref.rest_1_ = bf16[16,224,128]{2,1,0:T(8,128)(2,1)S(1)} custom-call(bf16[16,3,224,128]{3,2,1,0:T(8,128)(2,1)S(1)} %all-to-all-done.got_ref, s32[224,128]{1,0:T(8,128)S(1)} %pad.27.qrank_ref, s32[1,3584]{1,0:T(1,128)S(1)} %copy-done.7, bf16[256,128]{1,0:T(8,128)(2,1)S(1)} %get-tuple-element.41.rest_0_.picked_ref), custom_call_target="tpu_custom_call" | custom-call | tf_op jit(solution)/shard_map/attention/pallas_call | solution.py:202
  109.7 4.5 %diffusion_head.1 = (bf16[16,16,1664]{2,1,0:T(8,128)(2,1)}, f32[8,128]{1,0:T(8,128)S(1)}) custom-call(bf16[16,16,1536]{2,1,0:T(8,128)(2,1)} %all-to-all-done.1.cond_ref, f32[1,1536]{1,0:T(1,128)S(1)} %reshape.128.gain_ref, f32[16,1536]{1,0:T(8,128)S(1)} %bitcast.47, f32[64,17]{1,0:T(8,128)S(1)} %copy.69.noise_ref, ...), custom_call_target="tpu_custom_call" | custom-call | tf_op jit(solution)/shard_map/diffusion_head/pallas_call | solution.py:404
  114.2 5.2 %all-to-all-start.2 = ((bf16[16,16,1664]{2,1,0:T(8,128)(2,1)}), bf16[16,16,1664]{2,1,0:T(8,128)(2,1)}, u32[]{:S(2)}, u32[]{:S(2)}) async-start(bf16[16,16,1664]{2,1,0:T(8,128)(2,1)} %get-tuple-element.43), calls=%async_computation.2 | async-start | bytes 1703936 | tf_op jit(solution)/shard_map/all_to_all | solution.py:416
  120.6 17.7 %attention.3.after_ref.own_ref = bf16[16,224,128]{2,1,0:T(8,128)(2,1)S(1)} custom-call(bf16[16,3,224,128]{3,2,1,0:T(8,128)(2,1)S(1)} %all-to-all-done.got_ref, s32[224,128]{1,0:T(8,128)S(1)} %pad.27.qrank_ref, s32[1,3584]{1,0:T(1,128)S(1)} %copy-done.7, f32[8,128]{1,0:T(8,128)S(1)} %get-tuple-element.42.rest_0_, ...), custom_call_target="tpu_custom_call", output_to_operand_aliasing={{}: (4, {})} | custom-call | tf_op jit(solution)/shard_map/attention/pallas_call | solution.py:202
  139.2 2.4 %all-to-all-done.2.got_ref = bf16[16,16,1664]{2,1,0:T(8,128)(2,1)} async-done(((bf16[16,16,1664]{2,1,0:T(8,128)(2,1)}), bf16[16,16,1664]{2,1,0:T(8,128)(2,1)}, u32[]{:S(2)}, u32[]{:S(2)}) %all-to-all-start.2) | async-done | bytes 852000 | tf_op jit(solution)/shard_map/all_to_all | solution.py:416
  144.4 26.8 %all_to_all.30.got_ref = bf16[32,16,640]{2,1,0:T(8,128)(2,1)S(1)} all-to-all(bf16[32,16,640]{2,1,0:T(8,128)(2,1)S(1)} %get-tuple-element.51), channel_id=1, replica_groups=mesh['seq'=32,'head'=16] {'seq'}, dimensions={0} | all-to-all | bytes 1310720 | tf_op jit(solution)/shard_map/all_to_all | solution.py:416
  172.1 6.5 %all-to-all-start.5 = ((bf16[16,32,128]{2,1,0:T(8,128)(2,1)}), bf16[16,32,128]{2,1,0:T(8,128)(2,1)S(1)}, u32[]{:S(2)}, u32[]{:S(2)}) async-start(bf16[16,32,128]{2,1,0:T(8,128)(2,1)} %get-tuple-element.56), calls=%async_computation.5 | async-start | bytes 262144 | tf_op jit(solution)/shard_map/all_to_all | solution.py:416
  178.5 8.7 %all-to-all-done.5.tail_ref = bf16[16,32,128]{2,1,0:T(8,128)(2,1)S(1)} async-done(((bf16[16,32,128]{2,1,0:T(8,128)(2,1)}), bf16[16,32,128]{2,1,0:T(8,128)(2,1)S(1)}, u32[]{:S(2)}, u32[]{:S(2)}) %all-to-all-start.5) | async-done | bytes 131104 | tf_op jit(solution)/shard_map/all_to_all | solution.py:416
  187.3 7.4 %all-to-all-start.4 = ((bf16[32,16,384]{2,1,0:T(8,128)(2,1)}), bf16[32,16,384]{2,1,0:T(8,128)(2,1)S(1)}, u32[]{:S(2)}, u32[]{:S(2)}) async-start(bf16[32,16,384]{2,1,0:T(8,128)(2,1)} %get-tuple-element.55), calls=%async_computation.4 | async-start | bytes 786432 | tf_op jit(solution)/shard_map/all_to_all | solution.py:416
  194.7 2.2 collective-permute-start
  199.0 2.5 %collective-permute-start.1 = (bf16[2,224,128]{2,1,0:T(8,128)(2,1)S(1)}, bf16[2,224,128]{2,1,0:T(8,128)(2,1)S(1)}, u32[]{:S(2)}, u32[]{:S(2)}) collective-permute-start(bf16[2,224,128]{2,1,0:T(8,128)(2,1)S(1)} %get-tuple-element.46), channel_id=1, source_target_pairs={{0,2},{1,3},{2,4},{3,5},{4,6},{5,7},{6,8},{7,9},{8,10},{9,11},{10,... | collective-permute-start | bytes 344072 | tf_op jit(solution)/shard_map/ppermute | solution.py:362
  201.5 3.3 %collective-permute-start.2 = (bf16[2,224,128]{2,1,0:T(8,128)(2,1)S(1)}, bf16[2,224,128]{2,1,0:T(8,128)(2,1)S(1)}, u32[]{:S(2)}, u32[]{:S(2)}) collective-permute-start(bf16[2,224,128]{2,1,0:T(8,128)(2,1)S(1)} %get-tuple-element.47), channel_id=1, source_target_pairs={{0,4},{1,5},{2,6},{3,7},{4,8},{5,9},{6,10},{7,11},{8,12},{9,13},{1... | collective-permute-start | bytes 344072 | tf_op jit(solution)/shard_map/ppermute | solution.py:362
  204.8 4.1 %collective-permute-start.3 = (bf16[2,224,128]{2,1,0:T(8,128)(2,1)S(1)}, bf16[2,224,128]{2,1,0:T(8,128)(2,1)S(1)}, u32[]{:S(2)}, u32[]{:S(2)}) collective-permute-start(bf16[2,224,128]{2,1,0:T(8,128)(2,1)S(1)} %get-tuple-element.48), channel_id=1, source_target_pairs={{0,6},{1,7},{2,8},{3,9},{4,10},{5,11},{6,12},{7,13},{8,14},{9,15},... | collective-permute-start | bytes 344072 | tf_op jit(solution)/shard_map/ppermute | solution.py:362
  208.9 5.1 %collective-permute-start.4 = (bf16[2,224,128]{2,1,0:T(8,128)(2,1)S(1)}, bf16[2,224,128]{2,1,0:T(8,128)(2,1)S(1)}, u32[]{:S(2)}, u32[]{:S(2)}) collective-permute-start(bf16[2,224,128]{2,1,0:T(8,128)(2,1)S(1)} %get-tuple-element.49), channel_id=1, source_target_pairs={{0,8},{1,9},{2,10},{3,11},{4,12},{5,13},{6,14},{7,15},{8,0},{9,1},... | collective-permute-start | bytes 344072 | tf_op jit(solution)/shard_map/ppermute | solution.py:362
  214.0 3.6 %collective-permute-start.5 = (bf16[2,224,128]{2,1,0:T(8,128)(2,1)S(1)}, bf16[2,224,128]{2,1,0:T(8,128)(2,1)S(1)}, u32[]{:S(2)}, u32[]{:S(2)}) collective-permute-start(bf16[2,224,128]{2,1,0:T(8,128)(2,1)S(1)} %get-tuple-element.50), channel_id=1, source_target_pairs={{0,10},{1,11},{2,12},{3,13},{4,14},{5,15},{6,0},{7,1},{8,2},{9,3},... | collective-permute-start | bytes 344072 | tf_op jit(solution)/shard_map/ppermute | solution.py:362
  218.2 5.2 %collective-permute-start.6 = (bf16[2,224,128]{2,1,0:T(8,128)(2,1)S(1)}, bf16[2,224,128]{2,1,0:T(8,128)(2,1)S(1)}, u32[]{:S(2)}, u32[]{:S(2)}) collective-permute-start(bf16[2,224,128]{2,1,0:T(8,128)(2,1)S(1)} %get-tuple-element.53), channel_id=1, source_target_pairs={{0,12},{1,13},{2,14},{3,15},{4,0},{5,1},{6,2},{7,3},{8,4},{9,5},{1... | collective-permute-start | bytes 344072 | tf_op jit(solution)/shard_map/ppermute | solution.py:362
  223.4 2.4 %collective-permute-start.7 = (bf16[2,224,128]{2,1,0:T(8,128)(2,1)S(1)}, bf16[2,224,128]{2,1,0:T(8,128)(2,1)S(1)}, u32[]{:S(2)}, u32[]{:S(2)}) collective-permute-start(bf16[2,224,128]{2,1,0:T(8,128)(2,1)S(1)} %get-tuple-element.54), channel_id=1, source_target_pairs={{0,14},{1,15},{2,0},{3,1},{4,2},{5,3},{6,4},{7,5},{8,6},{9,7},{10,... | collective-permute-start | bytes 344072 | tf_op jit(solution)/shard_map/ppermute | solution.py:362
  225.9 3.0 %collective-permute-done.5.refs_5_ = bf16[2,224,128]{2,1,0:T(8,128)(2,1)S(1)} collective-permute-done((bf16[2,224,128]{2,1,0:T(8,128)(2,1)S(1)}, bf16[2,224,128]{2,1,0:T(8,128)(2,1)S(1)}, u32[]{:S(2)}, u32[]{:S(2)}) %collective-permute-start.5) | collective-permute-done | bytes 114720 | tf_op jit(solution)/shard_map/ppermute | solution.py:362
  228.8 5.2 %collective-permute-done.6.refs_6_ = bf16[2,224,128]{2,1,0:T(8,128)(2,1)S(1)} collective-permute-done((bf16[2,224,128]{2,1,0:T(8,128)(2,1)S(1)}, bf16[2,224,128]{2,1,0:T(8,128)(2,1)S(1)}, u32[]{:S(2)}, u32[]{:S(2)}) %collective-permute-start.6) | collective-permute-done | bytes 114720 | tf_op jit(solution)/shard_map/ppermute | solution.py:362
  (108 shorter events, 42.4 us)
Async XLA Ops:
  0.6 37.1 %copy-start = (f32[16,1536]{1,0:T(8,128)S(1)}, f32[16,1536]{1,0:T(8,128)}, u32[]{:S(2)}) copy-start(f32[16,1536]{1,0:T(8,128)} %param.24) | copy-start | bytes 294916
  3.8 11.9 %copy-start.10 = (bf16[3584,4]{0,1:T(4,128)(2,1)S(1)}, bf16[3584,4]{0,1:T(4,128)(2,1)}, u32[]{:S(2)}) copy-start(bf16[3584,4]{0,1:T(4,128)(2,1)} %param.22) | copy-start | bytes 86020
  3.8 17.1 %copy-start.7 = (s32[1,3584]{1,0:T(1,128)S(1)}, s32[1,3584]{1,0:T(1,128)}, u32[]{:S(2)}) copy-start(s32[1,3584]{1,0:T(1,128)} %rank_ref.5) | copy-start | bytes 43012
  3.8 19.0 %copy-start.19 = (s32[32]{0:T(128)S(1)}, s32[32]{0:T(128)}, u32[]{:S(2)}) copy-start(s32[32]{0:T(128)} %param.19) | copy-start | bytes 388
  3.8 73.9 %all-to-all-start = ((bf16[16,3,224,128]{3,2,1,0:T(8,128)(2,1)}), bf16[16,3,224,128]{3,2,1,0:T(8,128)(2,1)S(1)}, u32[]{:S(2)}, u32[]{:S(2)}) async-start(bf16[16,3,224,128]{3,2,1,0:T(8,128)(2,1)} %stack_by_head.1), calls=%async_computation | async-start | bytes 5505024 | tf_op jit(solution)/shard_map/all_to_all | solution.py:416
  14.4 16.1 %copy-start.9 = (bf16[3584,64]{0,1:T(8,128)(2,1)S(1)}, bf16[3584,64]{0,1:T(8,128)(2,1)}, u32[]{:S(2)}) copy-start(bf16[3584,64]{0,1:T(8,128)(2,1)} %param.21) | copy-start | bytes 1376260
  25.5 12.1 %copy-start.16 = (s32[256,1]{0,1:T(1,128)S(1)}, s32[256,1]{0,1:T(1,128)}, u32[]{:S(2)}) copy-start(s32[256,1]{0,1:T(1,128)} %stack_reshape.7) | copy-start | bytes 3076
  25.5 12.1 %copy-start.17 = (s32[256,1]{0,1:T(1,128)S(1)}, s32[256,1]{0,1:T(1,128)}, u32[]{:S(2)}) copy-start(s32[256,1]{0,1:T(1,128)} %stack_reshape.6) | copy-start | bytes 3076
  25.5 12.1 %copy-start.14 = (f32[64,1]{0,1:T(1,128)S(1)}, f32[64,1]{0,1:T(1,128)}, u32[]{:S(2)}) copy-start(f32[64,1]{0,1:T(1,128)} %reshape_broadcast_in_dim.3) | copy-start | bytes 772
  25.5 12.2 %copy-start.18 = (f32[64]{0:T(128)S(1)}, f32[64]{0:T(128)}, u32[]{:S(2)}) copy-start(f32[64]{0:T(128)} %mul.54) | copy-start | bytes 772
  82.8 25.6 %copy-start.8 = (f32[1536,16]{0,1:T(8,128)S(1)}, f32[1536,16]{0,1:T(8,128)}, u32[]{:S(2)}) copy-start(f32[1536,16]{0,1:T(8,128)} %param.27) | copy-start | bytes 294916
  82.9 25.6 %all-to-all-start.1 = ((bf16[16,16,1536]{2,1,0:T(8,128)(2,1)}), bf16[16,16,1536]{2,1,0:T(8,128)(2,1)}, u32[]{:S(2)}, u32[]{:S(2)}) async-start(bf16[16,16,1536]{2,1,0:T(8,128)(2,1)} %get-tuple-element.36), calls=%async_computation.1 | async-start | bytes 1572864 | tf_op jit(solution)/shard_map/all_to_all | solution.py:416
  114.2 27.5 %all-to-all-start.2 = ((bf16[16,16,1664]{2,1,0:T(8,128)(2,1)}), bf16[16,16,1664]{2,1,0:T(8,128)(2,1)}, u32[]{:S(2)}, u32[]{:S(2)}) async-start(bf16[16,16,1664]{2,1,0:T(8,128)(2,1)} %get-tuple-element.43), calls=%async_computation.2 | async-start | bytes 1703936 | tf_op jit(solution)/shard_map/all_to_all | solution.py:416
  142.8 51.9 %copy-start.6 = (bf16[16,224,128]{2,1,0:T(8,128)(2,1)S(1)}, bf16[16,224,128]{2,1,0:T(8,128)(2,1)}, u32[]{:S(2)}) copy-start(bf16[16,224,128]{2,1,0:T(8,128)(2,1)} %copy-done.4) | copy-start | bytes 2752516
  172.1 15.2 %all-to-all-start.5 = ((bf16[16,32,128]{2,1,0:T(8,128)(2,1)}), bf16[16,32,128]{2,1,0:T(8,128)(2,1)S(1)}, u32[]{:S(2)}, u32[]{:S(2)}) async-start(bf16[16,32,128]{2,1,0:T(8,128)(2,1)} %get-tuple-element.56), calls=%async_computation.5 | async-start | bytes 262144 | tf_op jit(solution)/shard_map/all_to_all | solution.py:416
  187.3 50.3 %all-to-all-start.4 = ((bf16[32,16,384]{2,1,0:T(8,128)(2,1)}), bf16[32,16,384]{2,1,0:T(8,128)(2,1)S(1)}, u32[]{:S(2)}, u32[]{:S(2)}) async-start(bf16[32,16,384]{2,1,0:T(8,128)(2,1)} %get-tuple-element.55), calls=%async_computation.4 | async-start | bytes 786432 | tf_op jit(solution)/shard_map/all_to_all | solution.py:416
  194.7 3.7 %collective-permute-start = (bf16[8,224,128]{2,1,0:T(8,128)(2,1)S(1)}, bf16[8,224,128]{2,1,0:T(8,128)(2,1)S(1)}, u32[]{:S(2)}, u32[]{:S(2)}) collective-permute-start(bf16[8,224,128]{2,1,0:T(8,128)(2,1)S(1)} %dynamic-slice_bitcast_fusion), channel_id=1, source_target_pairs={{0,1},{1,0},{2,3},{3,2},{4,5},{5,4},{6,7},{7,6},{8,9},{9,8},{10,11... | collective-permute-start | bytes 1376264 | tf_op jit(solution)/shard_map/ppermute | solution.py:506
  199.0 19.2 %collective-permute-start.1 = (bf16[2,224,128]{2,1,0:T(8,128)(2,1)S(1)}, bf16[2,224,128]{2,1,0:T(8,128)(2,1)S(1)}, u32[]{:S(2)}, u32[]{:S(2)}) collective-permute-start(bf16[2,224,128]{2,1,0:T(8,128)(2,1)S(1)} %get-tuple-element.46), channel_id=1, source_target_pairs={{0,2},{1,3},{2,4},{3,5},{4,6},{5,7},{6,8},{7,9},{8,10},{9,11},{10,... | collective-permute-start | bytes 344072 | tf_op jit(solution)/shard_map/ppermute | solution.py:362
  201.5 21.9 %collective-permute-start.2 = (bf16[2,224,128]{2,1,0:T(8,128)(2,1)S(1)}, bf16[2,224,128]{2,1,0:T(8,128)(2,1)S(1)}, u32[]{:S(2)}, u32[]{:S(2)}) collective-permute-start(bf16[2,224,128]{2,1,0:T(8,128)(2,1)S(1)} %get-tuple-element.47), channel_id=1, source_target_pairs={{0,4},{1,5},{2,6},{3,7},{4,8},{5,9},{6,10},{7,11},{8,12},{9,13},{1... | collective-permute-start | bytes 344072 | tf_op jit(solution)/shard_map/ppermute | solution.py:362
  204.8 21.1 %collective-permute-start.3 = (bf16[2,224,128]{2,1,0:T(8,128)(2,1)S(1)}, bf16[2,224,128]{2,1,0:T(8,128)(2,1)S(1)}, u32[]{:S(2)}, u32[]{:S(2)}) collective-permute-start(bf16[2,224,128]{2,1,0:T(8,128)(2,1)S(1)} %get-tuple-element.48), channel_id=1, source_target_pairs={{0,6},{1,7},{2,8},{3,9},{4,10},{5,11},{6,12},{7,13},{8,14},{9,15},... | collective-permute-start | bytes 344072 | tf_op jit(solution)/shard_map/ppermute | solution.py:362
  208.9 17.0 %collective-permute-start.4 = (bf16[2,224,128]{2,1,0:T(8,128)(2,1)S(1)}, bf16[2,224,128]{2,1,0:T(8,128)(2,1)S(1)}, u32[]{:S(2)}, u32[]{:S(2)}) collective-permute-start(bf16[2,224,128]{2,1,0:T(8,128)(2,1)S(1)} %get-tuple-element.49), channel_id=1, source_target_pairs={{0,8},{1,9},{2,10},{3,11},{4,12},{5,13},{6,14},{7,15},{8,0},{9,1},... | collective-permute-start | bytes 344072 | tf_op jit(solution)/shard_map/ppermute | solution.py:362
  214.0 14.9 %collective-permute-start.5 = (bf16[2,224,128]{2,1,0:T(8,128)(2,1)S(1)}, bf16[2,224,128]{2,1,0:T(8,128)(2,1)S(1)}, u32[]{:S(2)}, u32[]{:S(2)}) collective-permute-start(bf16[2,224,128]{2,1,0:T(8,128)(2,1)S(1)} %get-tuple-element.50), channel_id=1, source_target_pairs={{0,10},{1,11},{2,12},{3,13},{4,14},{5,15},{6,0},{7,1},{8,2},{9,3},... | collective-permute-start | bytes 344072 | tf_op jit(solution)/shard_map/ppermute | solution.py:362
  218.2 15.8 %collective-permute-start.6 = (bf16[2,224,128]{2,1,0:T(8,128)(2,1)S(1)}, bf16[2,224,128]{2,1,0:T(8,128)(2,1)S(1)}, u32[]{:S(2)}, u32[]{:S(2)}) collective-permute-start(bf16[2,224,128]{2,1,0:T(8,128)(2,1)S(1)} %get-tuple-element.53), channel_id=1, source_target_pairs={{0,12},{1,13},{2,14},{3,15},{4,0},{5,1},{6,2},{7,3},{8,4},{9,5},{1... | collective-permute-start | bytes 344072 | tf_op jit(solution)/shard_map/ppermute | solution.py:362
  223.4 12.4 %collective-permute-start.7 = (bf16[2,224,128]{2,1,0:T(8,128)(2,1)S(1)}, bf16[2,224,128]{2,1,0:T(8,128)(2,1)S(1)}, u32[]{:S(2)}, u32[]{:S(2)}) collective-permute-start(bf16[2,224,128]{2,1,0:T(8,128)(2,1)S(1)} %get-tuple-element.54), channel_id=1, source_target_pairs={{0,14},{1,15},{2,0},{3,1},{4,2},{5,3},{6,4},{7,5},{8,6},{9,7},{10,... | collective-permute-start | bytes 344072 | tf_op jit(solution)/shard_map/ppermute | solution.py:362
  (9 other events, 19.7 us)

commit v7 on v6

--- a/solution.py
+++ b/solution.py
@@ -14,7 +14,7 @@
 NORM_EPS = 1e-06
 HIDDEN_SCORE = -1e30
 SLOT = 16
-EARLY = 6
+EARLY = 5
 EXTRA = 128
 PACK = 256
 TAIL = 32
@@ -197,14 +197,14 @@
     aliases = {}
     if earlier is not None:
         specs.append(anywhere())
-        operands.append(earlier)
+        operands.append(in_hbm(earlier))
         aliases = {len(operands) - 1: 0}
     return pl.pallas_call(
         functools.partial(attend_kernel, first),
         grid=(count,),
         in_specs=specs,
         out_specs=pl.BlockSpec((1, each, HD), lambda i: (i + first, 0, 0)),
-        out_shape=jax.ShapeDtypeStruct((heads, each, HD), BF16),
+        out_shape=pltpu.HBM((heads, each, HD), BF16),
         scratch_shapes=[
             pltpu.VMEM((total, HD), BF16),
             pltpu.VMEM((total, 2 * HD), BF16),
@@ -354,7 +354,7 @@
         out_shape=[jax.ShapeDtypeStruct((2, each, HD), BF16)] * len(steps),
         compiler_params=params(),
         name="route",
-    )(place, own, other, after)
+    )(place, in_hbm(own), other, after)
 
 
 def round_chips(value, step, heads):
@@ -489,7 +489,7 @@
             pltpu.SemaphoreType.DMA,
         ],
         "diffusion_head",
-        in_vmem(got_cond), gain, w_out.T, noise, feats, in_hbm(base), first_half,
+        in_vmem(got_cond), gain, w_out.T, noise, feats, in_hbm(base), in_hbm(first_half),
         outside=2,
     )
     got_grad = exchange(send, "head")
@@ -504,6 +504,7 @@
         attended.reshape(half, 2, each, HD), 1 - core, 1, keepdims=False
     )
     other = lax.ppermute(to_other, "head", [(i, i ^ 1) for i in range(heads)])
+    got_grad, other = lax.optimization_barrier((got_grad, other))
     parts, token = call(
         grad_kernel,
         [
@@ -512,13 +513,14 @@
         ],
         [pltpu.VMEM((GROUP_ROWS, PACK), F32)],
         "cond_weight_grad",
-        in_vmem(got_grad), picked, attended,
+        in_vmem(got_grad), picked, token,
         outside=1,
     )
     got_parts = exchange(parts, "seq")
     early, late = tuple(range(EARLY)), tuple(range(EARLY, half))
     messages = route(early, place, attended, other, token)
     pieces = [messages[0]] + [round_chips(messages[k], k, heads) for k in early[1:]]
+    got_parts, *pieces = lax.optimization_barrier((got_parts, *pieces))
     big, small, token = call(
         total_kernel,
         [
@@ -532,7 +534,9 @@
     )
     all_big = exchange(big, "seq")
     messages = route(late, place, attended, other, token)
-    pieces += [round_chips(message, k, heads) for k, message in zip(late, messages)]
+    later = [round_chips(message, k, heads) for k, message in zip(late, messages)]
+    all_big, small, *later = lax.optimization_barrier((all_big, small, *later))
+    pieces = [*pieces, *later]
     all_small = exchange(small, "head")
     cond_whole, in_grad, time_grad, gain_grad, out_grad = call(
         spread_kernel,

time: 241 us -> 233 us (0.967)
  blocking collectives: 26.8 us -> 0 us
  starting transfers between devices: 62.8 us -> 78.2 us
  local copies, waits for them, and re-layouts: 23.8 us -> 19.4 us
  Pallas kernels: 54.4 us -> 57.8 us
  waiting for transfers between devices: 62.4 us -> 65.7 us
    all_to_all x1 -> x0, blocking collectives: 26.8 us -> none  [exchange(): return lax.all_to_all(value, axis, split_axis=0, concat_axis=0, tiled=True)]
    all_to_all x5 -> x6, starting transfers between devices: 34.5 us -> 45 us  [exchange(): return lax.all_to_all(value, axis, split_axis=0, concat_axis=0, tiled=True)]
    ppermute x7, waiting for transfers between devices: 9.94 us -> 17 us  [round_chips(): return lax.ppermute(value, 'head', pairs)]
    unnamed x44 -> x32, local copies, waits for them, and re-layouts: 11.2 us -> 5.85 us
    all_to_all x5 -> x6, waiting for transfers between devices: 51.1 us -> 47.3 us  [exchange(): return lax.all_to_all(value, axis, split_axis=0, concat_axis=0, tiled=True)]
    ppermute x7, starting transfers between devices: 26.2 us -> 29.7 us  [round_chips(): return lax.ppermute(value, 'head', pairs)]
  transfers between devices with their start and end apart: 13 -> 14, of which waited for: 8 -> 8; matrix products, arithmetic and copies ran while one was open for 10% -> 11% of each run, Pallas kernels for 16% -> 18%
where the time goes in v7:
time: 233 us; the launch traced here: 229 us
  starting transfers between devices  78.2 us (34%)
  waiting for transfers between devices  65.7 us (28%)
  Pallas kernels  57.8 us (25%)
  local copies, waits for them, and re-layouts  19.4 us (8%)
  other arithmetic  4.99 us (2%)
    all_to_all x6, waiting for transfers between devices, exchange(): return lax.all_to_all(value, axis, split_axis=0, concat_axis=0, tiled=True)  47.3 us
    all_to_all x6, starting transfers between devices, exchange(): return lax.all_to_all(value, axis, split_axis=0, concat_axis=0, tiled=True)  45 us
    pallas_call x2, Pallas kernels, attend_some(): pl.pallas_call(functools.partial(attend_kernel, first), grid=(count,), in...  36.7 us
    ppermute x7, starting transfers between devices, round_chips(): return lax.ppermute(value, 'head', pairs)  29.7 us
    ppermute x7, waiting for transfers between devices, round_chips(): return lax.ppermute(value, 'head', pairs)  17 us
    pallas_call x4, Pallas kernels, call(): pl.pallas_call(kernel, in_specs=specs, out_specs=[vmem()] * len(out_shape...  8.64 us
    unnamed x32, local copies, waits for them, and re-layouts  5.85 us
    pallas_call x1, Pallas kernels, attend_masked(): pl.pallas_call(masked_kernel, in_specs=[vmem()] * 3 + [anywhere()], out_s...  5.13 us
  transfers between devices with their start and end apart: 14, of which 8 were waited for; matrix products, arithmetic and copies ran while one was open for 11% of the time, Pallas kernels for 18%

profile of v7, /device:TPU:6, one launch (start us, length us, event | category | flops | bytes accessed | tf_op | source)
XLA Modules:
  0.0 229.2 jit_solution(10598976832710593571)
XLA Ops:
  0.6 3.1 %stack_by_head.1 = bf16[16,3,224,128]{3,2,1,0:T(8,128)(2,1)} custom-call(bf16[224,2048]{1,0:T(8,128)(2,1)} %q_ref.1, bf16[224,2048]{1,0:T(8,128)(2,1)} %k_ref.1, bf16[224,2048]{1,0:T(8,128)(2,1)} %v_ref.1), custom_call_target="tpu_custom_call" | custom-call | tf_op jit(solution)/shard_map/stack_by_head/pallas_call | solution.py:77
  3.8 10.6 %all-to-all-start = ((bf16[16,3,224,128]{3,2,1,0:T(8,128)(2,1)}), bf16[16,3,224,128]{3,2,1,0:T(8,128)(2,1)S(1)}, u32[]{:S(2)}, u32[]{:S(2)}) async-start(bf16[16,3,224,128]{3,2,1,0:T(8,128)(2,1)} %stack_by_head.1), calls=%async_computation | async-start | bytes 5505024 | tf_op jit(solution)/shard_map/all_to_all | solution.py:416
  39.7 38.0 %all-to-all-done.got_ref = bf16[16,3,224,128]{3,2,1,0:T(8,128)(2,1)S(1)} async-done(((bf16[16,3,224,128]{3,2,1,0:T(8,128)(2,1)}), bf16[16,3,224,128]{3,2,1,0:T(8,128)(2,1)S(1)}, u32[]{:S(2)}, u32[]{:S(2)}) %all-to-all-start) | async-done | bytes 2752544 | tf_op jit(solution)/shard_map/all_to_all | solution.py:416
  77.7 5.1 %masked_rows.1 = (bf16[16,16,1536]{2,1,0:T(8,128)(2,1)}, bf16[256,128]{1,0:T(8,128)(2,1)S(1)}) custom-call(bf16[16,3,224,128]{3,2,1,0:T(8,128)(2,1)S(1)} %all-to-all-done.got_ref, s32[256,2]{1,0:T(8,128)S(1)} %copy.68.slot_ref, s32[1,3584]{1,0:T(1,128)S(1)} %copy-done.1, bf16[128,1536]{1,0:T(8,128)(2,1)} %w_ref.1), custom_call_target="tpu_custom_call" | custom-call | tf_op jit(solution)/shard_map/masked_rows/pallas_call | solution.py:152
  82.8 4.9 %all-to-all-start.1 = ((bf16[16,16,1536]{2,1,0:T(8,128)(2,1)}), bf16[16,16,1536]{2,1,0:T(8,128)(2,1)}, u32[]{:S(2)}, u32[]{:S(2)}) async-start(bf16[16,16,1536]{2,1,0:T(8,128)(2,1)} %get-tuple-element.48), calls=%async_computation.1 | async-start | bytes 1572864 | tf_op jit(solution)/shard_map/all_to_all | solution.py:416
  87.8 18.4 %attention.2.after_ref.rest_1_ = bf16[16,224,128]{2,1,0:T(8,128)(2,1)} custom-call(bf16[16,3,224,128]{3,2,1,0:T(8,128)(2,1)S(1)} %all-to-all-done.got_ref, s32[224,128]{1,0:T(8,128)S(1)} %pad.27.qrank_ref, s32[1,3584]{1,0:T(1,128)S(1)} %copy-done.1, bf16[256,128]{1,0:T(8,128)(2,1)S(1)} %get-tuple-element.54.rest_0_.picked_ref), custom_call_target="tpu_custom_call" | custom-call | tf_op jit(solution)/shard_map/attention/pallas_call | solution.py:202
  108.5 4.5 %diffusion_head.1 = (bf16[16,16,1664]{2,1,0:T(8,128)(2,1)}, f32[8,128]{1,0:T(8,128)S(1)}) custom-call(bf16[16,16,1536]{2,1,0:T(8,128)(2,1)} %all-to-all-done.1.cond_ref, f32[1,1536]{1,0:T(1,128)S(1)} %reshape.128.gain_ref, f32[16,1536]{1,0:T(8,128)S(1)} %bitcast.46, f32[64,17]{1,0:T(8,128)S(1)} %copy.69.noise_ref, ...), custom_call_target="tpu_custom_call" | custom-call | tf_op jit(solution)/shard_map/diffusion_head/pallas_call | solution.py:404
  113.0 5.2 %all-to-all-start.2 = ((bf16[16,16,1664]{2,1,0:T(8,128)(2,1)}), bf16[16,16,1664]{2,1,0:T(8,128)(2,1)}, u32[]{:S(2)}, u32[]{:S(2)}) async-start(bf16[16,16,1664]{2,1,0:T(8,128)(2,1)} %get-tuple-element.55), calls=%async_computation.2 | async-start | bytes 1703936 | tf_op jit(solution)/shard_map/all_to_all | solution.py:416
  118.2 18.4 %attention.3.own_ref = bf16[16,224,128]{2,1,0:T(8,128)(2,1)} custom-call(bf16[16,3,224,128]{3,2,1,0:T(8,128)(2,1)S(1)} %all-to-all-done.got_ref, s32[224,128]{1,0:T(8,128)S(1)} %pad.27.qrank_ref, s32[1,3584]{1,0:T(1,128)S(1)} %copy-done.1, f32[8,128]{1,0:T(8,128)S(1)} %get-tuple-element.56.rest_0_.after_ref, ...), custom_call_target="tpu_custom_call", output_to_operand_aliasing={{}: (4, {})} | custom-call | tf_op jit(solution)/shard_map/attention/pallas_call | solution.py:202
  137.6 3.5 %collective-permute-start = (bf16[8,224,128]{2,1,0:T(8,128)(2,1)S(1)}, bf16[8,224,128]{2,1,0:T(8,128)(2,1)S(1)}, u32[]{:S(2)}, u32[]{:S(2)}) collective-permute-start(bf16[8,224,128]{2,1,0:T(8,128)(2,1)S(1)} %dynamic-slice_bitcast_fusion), channel_id=1, source_target_pairs={{0,1},{1,0},{2,3},{3,2},{4,5},{5,4},{6,7},{7,6},{8,9},{9,8},{10,11... | collective-permute-start | bytes 1376264 | tf_op jit(solution)/shard_map/ppermute | solution.py:506
  144.8 10.3 %all-to-all-start.3 = ((bf16[32,16,640]{2,1,0:T(8,128)(2,1)}), bf16[32,16,640]{2,1,0:T(8,128)(2,1)S(1)}, u32[]{:S(2)}, u32[]{:S(2)}) async-start(bf16[32,16,640]{2,1,0:T(8,128)(2,1)} %get-tuple-element.58), calls=%async_computation.3 | async-start | bytes 1310720 | tf_op jit(solution)/shard_map/all_to_all | solution.py:416
  159.0 4.3 %collective-permute-start.2 = (bf16[2,224,128]{2,1,0:T(8,128)(2,1)S(1)}, bf16[2,224,128]{2,1,0:T(8,128)(2,1)S(1)}, u32[]{:S(2)}, u32[]{:S(2)}) collective-permute-start(bf16[2,224,128]{2,1,0:T(8,128)(2,1)S(1)} %get-tuple-element.63), channel_id=1, source_target_pairs={{0,4},{1,5},{2,6},{3,7},{4,8},{5,9},{6,10},{7,11},{8,12},{9,13},{1... | collective-permute-start | bytes 344072 | tf_op jit(solution)/shard_map/ppermute | solution.py:362
  163.3 4.6 %collective-permute-start.3 = (bf16[2,224,128]{2,1,0:T(8,128)(2,1)S(1)}, bf16[2,224,128]{2,1,0:T(8,128)(2,1)S(1)}, u32[]{:S(2)}, u32[]{:S(2)}) collective-permute-start(bf16[2,224,128]{2,1,0:T(8,128)(2,1)S(1)} %get-tuple-element.64), channel_id=1, source_target_pairs={{0,6},{1,7},{2,8},{3,9},{4,10},{5,11},{6,12},{7,13},{8,14},{9,15},... | collective-permute-start | bytes 344072 | tf_op jit(solution)/shard_map/ppermute | solution.py:362
  167.9 4.3 %collective-permute-start.4 = (bf16[2,224,128]{2,1,0:T(8,128)(2,1)S(1)}, bf16[2,224,128]{2,1,0:T(8,128)(2,1)S(1)}, u32[]{:S(2)}, u32[]{:S(2)}) collective-permute-start(bf16[2,224,128]{2,1,0:T(8,128)(2,1)S(1)} %get-tuple-element.65), channel_id=1, source_target_pairs={{0,8},{1,9},{2,10},{3,11},{4,12},{5,13},{6,14},{7,15},{8,0},{9,1},... | collective-permute-start | bytes 344072 | tf_op jit(solution)/shard_map/ppermute | solution.py:362
  172.1 5.8 %collective-permute-done.3.refs_3_ = bf16[2,224,128]{2,1,0:T(8,128)(2,1)S(1)} collective-permute-done((bf16[2,224,128]{2,1,0:T(8,128)(2,1)S(1)}, bf16[2,224,128]{2,1,0:T(8,128)(2,1)S(1)}, u32[]{:S(2)}, u32[]{:S(2)}) %collective-permute-start.3) | collective-permute-done | bytes 114720 | tf_op jit(solution)/shard_map/ppermute | solution.py:362
  177.9 3.4 %collective-permute-done.4.refs_4_ = bf16[2,224,128]{2,1,0:T(8,128)(2,1)S(1)} collective-permute-done((bf16[2,224,128]{2,1,0:T(8,128)(2,1)S(1)}, bf16[2,224,128]{2,1,0:T(8,128)(2,1)S(1)}, u32[]{:S(2)}, u32[]{:S(2)}) %collective-permute-start.4) | collective-permute-done | bytes 114720 | tf_op jit(solution)/shard_map/ppermute | solution.py:362
  182.2 9.8 %all-to-all-start.4 = ((bf16[32,16,384]{2,1,0:T(8,128)(2,1)}), bf16[32,16,384]{2,1,0:T(8,128)(2,1)S(1)}, u32[]{:S(2)}, u32[]{:S(2)}) async-start(bf16[32,16,384]{2,1,0:T(8,128)(2,1)} %get-tuple-element.72), calls=%async_computation.4 | async-start | bytes 786432 | tf_op jit(solution)/shard_map/all_to_all | solution.py:416
  193.2 4.0 %collective-permute-start.5 = (bf16[2,224,128]{2,1,0:T(8,128)(2,1)S(1)}, bf16[2,224,128]{2,1,0:T(8,128)(2,1)S(1)}, u32[]{:S(2)}, u32[]{:S(2)}) collective-permute-start(bf16[2,224,128]{2,1,0:T(8,128)(2,1)S(1)} %get-tuple-element.75), channel_id=1, source_target_pairs={{0,10},{1,11},{2,12},{3,13},{4,14},{5,15},{6,0},{7,1},{8,2},{9,3},... | collective-permute-start | bytes 344072 | tf_op jit(solution)/shard_map/ppermute | solution.py:362
  197.2 5.1 %collective-permute-start.6 = (bf16[2,224,128]{2,1,0:T(8,128)(2,1)S(1)}, bf16[2,224,128]{2,1,0:T(8,128)(2,1)S(1)}, u32[]{:S(2)}, u32[]{:S(2)}) collective-permute-start(bf16[2,224,128]{2,1,0:T(8,128)(2,1)S(1)} %get-tuple-element.76), channel_id=1, source_target_pairs={{0,12},{1,13},{2,14},{3,15},{4,0},{5,1},{6,2},{7,3},{8,4},{9,5},{1... | collective-permute-start | bytes 344072 | tf_op jit(solution)/shard_map/ppermute | solution.py:362
  202.3 4.9 %collective-permute-start.7 = (bf16[2,224,128]{2,1,0:T(8,128)(2,1)S(1)}, bf16[2,224,128]{2,1,0:T(8,128)(2,1)S(1)}, u32[]{:S(2)}, u32[]{:S(2)}) collective-permute-start(bf16[2,224,128]{2,1,0:T(8,128)(2,1)S(1)} %get-tuple-element.77), channel_id=1, source_target_pairs={{0,14},{1,15},{2,0},{3,1},{4,2},{5,3},{6,4},{7,5},{8,6},{9,7},{10,... | collective-permute-start | bytes 344072 | tf_op jit(solution)/shard_map/ppermute | solution.py:362
  207.2 3.7 %collective-permute-done.6.refs_6_ = bf16[2,224,128]{2,1,0:T(8,128)(2,1)S(1)} collective-permute-done((bf16[2,224,128]{2,1,0:T(8,128)(2,1)S(1)}, bf16[2,224,128]{2,1,0:T(8,128)(2,1)S(1)}, u32[]{:S(2)}, u32[]{:S(2)}) %collective-permute-start.6) | collective-permute-done | bytes 114720 | tf_op jit(solution)/shard_map/ppermute | solution.py:362
  210.9 4.2 %collective-permute-done.7.refs_7_ = bf16[2,224,128]{2,1,0:T(8,128)(2,1)S(1)} collective-permute-done((bf16[2,224,128]{2,1,0:T(8,128)(2,1)S(1)}, bf16[2,224,128]{2,1,0:T(8,128)(2,1)S(1)}, u32[]{:S(2)}, u32[]{:S(2)}) %collective-permute-start.7) | collective-permute-done | bytes 114720 | tf_op jit(solution)/shard_map/ppermute | solution.py:362
  215.1 4.4 %all-to-all-start.5 = ((bf16[16,32,128]{2,1,0:T(8,128)(2,1)}), bf16[16,32,128]{2,1,0:T(8,128)(2,1)S(1)}, u32[]{:S(2)}, u32[]{:S(2)}) async-start(bf16[16,32,128]{2,1,0:T(8,128)(2,1)} %get-tuple-element.82), calls=%async_computation.5 | async-start | bytes 262144 | tf_op jit(solution)/shard_map/all_to_all | solution.py:416
  221.2 7.0 %all-to-all-done.5.tail_ref = bf16[16,32,128]{2,1,0:T(8,128)(2,1)S(1)} async-done(((bf16[16,32,128]{2,1,0:T(8,128)(2,1)}), bf16[16,32,128]{2,1,0:T(8,128)(2,1)S(1)}, u32[]{:S(2)}, u32[]{:S(2)}) %all-to-all-start.5) | async-done | bytes 131104 | tf_op jit(solution)/shard_map/all_to_all | solution.py:416
  (97 shorter events, 41.0 us)
Async XLA Ops:
  0.6 37.0 %copy-start = (f32[16,1536]{1,0:T(8,128)S(1)}, f32[16,1536]{1,0:T(8,128)}, u32[]{:S(2)}) copy-start(f32[16,1536]{1,0:T(8,128)} %param.24) | copy-start | bytes 294916
  3.8 11.9 %copy-start.4 = (bf16[3584,4]{0,1:T(4,128)(2,1)S(1)}, bf16[3584,4]{0,1:T(4,128)(2,1)}, u32[]{:S(2)}) copy-start(bf16[3584,4]{0,1:T(4,128)(2,1)} %param.22) | copy-start | bytes 86020
  3.8 17.0 %copy-start.1 = (s32[1,3584]{1,0:T(1,128)S(1)}, s32[1,3584]{1,0:T(1,128)}, u32[]{:S(2)}) copy-start(s32[1,3584]{1,0:T(1,128)} %rank_ref.5) | copy-start | bytes 43012
  3.8 19.0 %copy-start.13 = (s32[32]{0:T(128)S(1)}, s32[32]{0:T(128)}, u32[]{:S(2)}) copy-start(s32[32]{0:T(128)} %param.19) | copy-start | bytes 388
  3.8 73.9 %all-to-all-start = ((bf16[16,3,224,128]{3,2,1,0:T(8,128)(2,1)}), bf16[16,3,224,128]{3,2,1,0:T(8,128)(2,1)S(1)}, u32[]{:S(2)}, u32[]{:S(2)}) async-start(bf16[16,3,224,128]{3,2,1,0:T(8,128)(2,1)} %stack_by_head.1), calls=%async_computation | async-start | bytes 5505024 | tf_op jit(solution)/shard_map/all_to_all | solution.py:416
  14.4 16.0 %copy-start.3 = (bf16[3584,64]{0,1:T(8,128)(2,1)S(1)}, bf16[3584,64]{0,1:T(8,128)(2,1)}, u32[]{:S(2)}) copy-start(bf16[3584,64]{0,1:T(8,128)(2,1)} %param.21) | copy-start | bytes 1376260
  25.4 12.1 %copy-start.10 = (s32[256,1]{0,1:T(1,128)S(1)}, s32[256,1]{0,1:T(1,128)}, u32[]{:S(2)}) copy-start(s32[256,1]{0,1:T(1,128)} %stack_reshape.7) | copy-start | bytes 3076
  25.4 12.1 %copy-start.11 = (s32[256,1]{0,1:T(1,128)S(1)}, s32[256,1]{0,1:T(1,128)}, u32[]{:S(2)}) copy-start(s32[256,1]{0,1:T(1,128)} %stack_reshape.6) | copy-start | bytes 3076
  25.4 12.1 %copy-start.8 = (f32[64,1]{0,1:T(1,128)S(1)}, f32[64,1]{0,1:T(1,128)}, u32[]{:S(2)}) copy-start(f32[64,1]{0,1:T(1,128)} %reshape_broadcast_in_dim.3) | copy-start | bytes 772
  25.4 12.2 %copy-start.12 = (f32[64]{0:T(128)S(1)}, f32[64]{0:T(128)}, u32[]{:S(2)}) copy-start(f32[64]{0:T(128)} %mul.54) | copy-start | bytes 772
  82.8 25.6 %copy-start.2 = (f32[1536,16]{0,1:T(8,128)S(1)}, f32[1536,16]{0,1:T(8,128)}, u32[]{:S(2)}) copy-start(f32[1536,16]{0,1:T(8,128)} %param.27) | copy-start | bytes 294916
  82.8 25.6 %all-to-all-start.1 = ((bf16[16,16,1536]{2,1,0:T(8,128)(2,1)}), bf16[16,16,1536]{2,1,0:T(8,128)(2,1)}, u32[]{:S(2)}, u32[]{:S(2)}) async-start(bf16[16,16,1536]{2,1,0:T(8,128)(2,1)} %get-tuple-element.48), calls=%async_computation.1 | async-start | bytes 1572864 | tf_op jit(solution)/shard_map/all_to_all | solution.py:416
  113.0 29.5 %all-to-all-start.2 = ((bf16[16,16,1664]{2,1,0:T(8,128)(2,1)}), bf16[16,16,1664]{2,1,0:T(8,128)(2,1)}, u32[]{:S(2)}, u32[]{:S(2)}) async-start(bf16[16,16,1664]{2,1,0:T(8,128)(2,1)} %get-tuple-element.55), calls=%async_computation.2 | async-start | bytes 1703936 | tf_op jit(solution)/shard_map/all_to_all | solution.py:416
  137.6 4.9 %collective-permute-start = (bf16[8,224,128]{2,1,0:T(8,128)(2,1)S(1)}, bf16[8,224,128]{2,1,0:T(8,128)(2,1)S(1)}, u32[]{:S(2)}, u32[]{:S(2)}) collective-permute-start(bf16[8,224,128]{2,1,0:T(8,128)(2,1)S(1)} %dynamic-slice_bitcast_fusion), channel_id=1, source_target_pairs={{0,1},{1,0},{2,3},{3,2},{4,5},{5,4},{6,7},{7,6},{8,9},{9,8},{10,11... | collective-permute-start | bytes 1376264 | tf_op jit(solution)/shard_map/ppermute | solution.py:506
  144.8 36.5 %all-to-all-start.3 = ((bf16[32,16,640]{2,1,0:T(8,128)(2,1)}), bf16[32,16,640]{2,1,0:T(8,128)(2,1)S(1)}, u32[]{:S(2)}, u32[]{:S(2)}) async-start(bf16[32,16,640]{2,1,0:T(8,128)(2,1)} %get-tuple-element.58), calls=%async_computation.3 | async-start | bytes 1310720 | tf_op jit(solution)/shard_map/all_to_all | solution.py:416
  156.4 15.7 %collective-permute-start.1 = (bf16[2,224,128]{2,1,0:T(8,128)(2,1)S(1)}, bf16[2,224,128]{2,1,0:T(8,128)(2,1)S(1)}, u32[]{:S(2)}, u32[]{:S(2)}) collective-permute-start(bf16[2,224,128]{2,1,0:T(8,128)(2,1)S(1)} %get-tuple-element.62), channel_id=1, source_target_pairs={{0,2},{1,3},{2,4},{3,5},{4,6},{5,7},{6,8},{7,9},{8,10},{9,11},{10,... | collective-permute-start | bytes 344072 | tf_op jit(solution)/shard_map/ppermute | solution.py:362
  159.0 13.2 %collective-permute-start.2 = (bf16[2,224,128]{2,1,0:T(8,128)(2,1)S(1)}, bf16[2,224,128]{2,1,0:T(8,128)(2,1)S(1)}, u32[]{:S(2)}, u32[]{:S(2)}) collective-permute-start(bf16[2,224,128]{2,1,0:T(8,128)(2,1)S(1)} %get-tuple-element.63), channel_id=1, source_target_pairs={{0,4},{1,5},{2,6},{3,7},{4,8},{5,9},{6,10},{7,11},{8,12},{9,13},{1... | collective-permute-start | bytes 344072 | tf_op jit(solution)/shard_map/ppermute | solution.py:362
  163.3 14.7 %collective-permute-start.3 = (bf16[2,224,128]{2,1,0:T(8,128)(2,1)S(1)}, bf16[2,224,128]{2,1,0:T(8,128)(2,1)S(1)}, u32[]{:S(2)}, u32[]{:S(2)}) collective-permute-start(bf16[2,224,128]{2,1,0:T(8,128)(2,1)S(1)} %get-tuple-element.64), channel_id=1, source_target_pairs={{0,6},{1,7},{2,8},{3,9},{4,10},{5,11},{6,12},{7,13},{8,14},{9,15},... | collective-permute-start | bytes 344072 | tf_op jit(solution)/shard_map/ppermute | solution.py:362
  167.9 13.4 %collective-permute-start.4 = (bf16[2,224,128]{2,1,0:T(8,128)(2,1)S(1)}, bf16[2,224,128]{2,1,0:T(8,128)(2,1)S(1)}, u32[]{:S(2)}, u32[]{:S(2)}) collective-permute-start(bf16[2,224,128]{2,1,0:T(8,128)(2,1)S(1)} %get-tuple-element.65), channel_id=1, source_target_pairs={{0,8},{1,9},{2,10},{3,11},{4,12},{5,13},{6,14},{7,15},{8,0},{9,1},... | collective-permute-start | bytes 344072 | tf_op jit(solution)/shard_map/ppermute | solution.py:362
  182.2 32.9 %all-to-all-start.4 = ((bf16[32,16,384]{2,1,0:T(8,128)(2,1)}), bf16[32,16,384]{2,1,0:T(8,128)(2,1)S(1)}, u32[]{:S(2)}, u32[]{:S(2)}) async-start(bf16[32,16,384]{2,1,0:T(8,128)(2,1)} %get-tuple-element.72), calls=%async_computation.4 | async-start | bytes 786432 | tf_op jit(solution)/shard_map/all_to_all | solution.py:416
  193.2 14.0 %collective-permute-start.5 = (bf16[2,224,128]{2,1,0:T(8,128)(2,1)S(1)}, bf16[2,224,128]{2,1,0:T(8,128)(2,1)S(1)}, u32[]{:S(2)}, u32[]{:S(2)}) collective-permute-start(bf16[2,224,128]{2,1,0:T(8,128)(2,1)S(1)} %get-tuple-element.75), channel_id=1, source_target_pairs={{0,10},{1,11},{2,12},{3,13},{4,14},{5,15},{6,0},{7,1},{8,2},{9,3},... | collective-permute-start | bytes 344072 | tf_op jit(solution)/shard_map/ppermute | solution.py:362
  197.2 13.7 %collective-permute-start.6 = (bf16[2,224,128]{2,1,0:T(8,128)(2,1)S(1)}, bf16[2,224,128]{2,1,0:T(8,128)(2,1)S(1)}, u32[]{:S(2)}, u32[]{:S(2)}) collective-permute-start(bf16[2,224,128]{2,1,0:T(8,128)(2,1)S(1)} %get-tuple-element.76), channel_id=1, source_target_pairs={{0,12},{1,13},{2,14},{3,15},{4,0},{5,1},{6,2},{7,3},{8,4},{9,5},{1... | collective-permute-start | bytes 344072 | tf_op jit(solution)/shard_map/ppermute | solution.py:362
  202.3 12.7 %collective-permute-start.7 = (bf16[2,224,128]{2,1,0:T(8,128)(2,1)S(1)}, bf16[2,224,128]{2,1,0:T(8,128)(2,1)S(1)}, u32[]{:S(2)}, u32[]{:S(2)}) collective-permute-start(bf16[2,224,128]{2,1,0:T(8,128)(2,1)S(1)} %get-tuple-element.77), channel_id=1, source_target_pairs={{0,14},{1,15},{2,0},{3,1},{4,2},{5,3},{6,4},{7,5},{8,6},{9,7},{10,... | collective-permute-start | bytes 344072 | tf_op jit(solution)/shard_map/ppermute | solution.py:362
  215.1 13.1 %all-to-all-start.5 = ((bf16[16,32,128]{2,1,0:T(8,128)(2,1)}), bf16[16,32,128]{2,1,0:T(8,128)(2,1)S(1)}, u32[]{:S(2)}, u32[]{:S(2)}) async-start(bf16[16,32,128]{2,1,0:T(8,128)(2,1)} %get-tuple-element.82), calls=%async_computation.5 | async-start | bytes 262144 | tf_op jit(solution)/shard_map/all_to_all | solution.py:416
  (4 other events, 14.2 us)
